TPU v7x, 128 devices: a whole 4x4x4 slice. The times are simulated.
128 devices in a mesh: row: 16 (over y_hi, z, core), col: 8 (over y_lo, x).
Axes of the slice: x: 4, y: 4 (y_hi: 2, y_lo: 2; y = y_hi * 2 + y_lo), z: 4, core: 2. Of those that a mesh axis runs over, the one named last changes fastest.
Arguments:
- pair_rep: bfloat16 [1024, 1024, 128], P('row', 'col'), may hold values from -260 to 260
- labels: int32 [1024, 1024], P('row', 'col'), may hold values from 0 to 63
- residue_mask: int32 [1024], replicated, may hold values 0 or 1
- dist_weight: bfloat16 [128, 64], replicated, may hold values from -0.5 to 0.5
- dist_bias: float32 [64], replicated, may hold values from -4 to 4
- bias_weight: bfloat16 [128, 12], replicated, may hold values from -0.5 to 0.5
- query_scalar: bfloat16 [1024, 192], P('row'), may hold values from -6 to 6
- query_points: bfloat16 [1024, 144], P('row'), may hold values from -6 to 6
- key_scalar: bfloat16 [1024, 192], P('row'), may hold values from -6 to 6
- key_points: bfloat16 [1024, 144], P('row'), may hold values from -6 to 6
- value_scalar: bfloat16 [1024, 192], P('row'), may hold values from -6 to 6
- value_points: bfloat16 [1024, 288], P('row'), may hold values from -6 to 6
- point_weight: float32 [12], replicated, may hold values from -1 to 2
- cot_scalar: bfloat16 [1024, 192], P('row'), may hold values from -768 to 768
- cot_points: bfloat16 [1024, 288], P('row'), may hold values from -768 to 768
- cot_pair: bfloat16 [1024, 1536], P('row'), may hold values from -768 to 768
Outputs:
- pair_grad: bfloat16 [1024, 1024, 128], P('row', 'col')
- weight_grad: float32 [128, 64], replicated
All inputs are finite; a program needn't handle non-finite values.
Results may differ from a plain program's by a relative error of at most 0.0052.
Values may be sent and summed in bfloat16 or wider, within the bound.
No kernel may reach another device: no remote copies, remote signals or barrier semaphores. Data moves between devices by JAX's collectives and lax.ppermute only.
A program may use at most 64 MiB of HBM per device.

v0:
```python
import math

import jax
import jax.numpy as jnp
from jax import lax
from jax.sharding import PartitionSpec as P

logit_weight = math.sqrt(1.0 / 3.0)


def mirror_blocks(values, groups):
    row_count = values.shape[0]
    shaped = values.reshape((row_count, groups, row_count) + values.shape[2:])
    axis_order = (1, 2, 0) + tuple(range(3, shaped.ndim))
    return jnp.transpose(shaped, axis_order)


def attention_logits(
    queries, query_pts, keys_cols, keypts_cols, pair_tile, bias_weight, point_weight, key_bias
):
    head_size = queries.shape[2]
    per_head = (((2,), (2,)), ((1,), (1,)))
    scalar_term = lax.dot_general(queries, keys_cols, per_head, preferred_element_type=jnp.float32)
    cross_term = lax.dot_general(
        query_pts, keypts_cols, per_head, preferred_element_type=jnp.float32
    )
    query_sq = jnp.transpose(jnp.sum(jnp.square(query_pts.astype(jnp.float32)), axis=2))[:, :, None]
    key_sq = jnp.transpose(jnp.sum(jnp.square(keypts_cols.astype(jnp.float32)), axis=2))[:, None, :]
    squared_gap = query_sq + key_sq - 2.0 * cross_term
    pair_bias = jnp.transpose(
        jnp.dot(pair_tile, bias_weight, preferred_element_type=jnp.float32), (2, 0, 1)
    )
    point_count = query_pts.shape[2] // 3
    point_scale = jax.nn.softplus(point_weight) * (math.sqrt(2.0 / (9.0 * point_count)) / 2.0)
    return (
        logit_weight
        * (
            scalar_term * (1.0 / math.sqrt(head_size))
            + pair_bias
            - point_scale[:, None, None] * squared_gap
        )
        + key_bias[None, None, :]
    )


def value_gradient(cot_values, value_rows, pair_cot, pair_tile):
    per_head = (((2,), (2,)), ((1,), (1,)))
    pair_part = lax.dot_general(
        pair_cot, pair_tile, (((2,), (2,)), ((0,), (0,))), preferred_element_type=jnp.float32
    )
    return lax.dot_general(
        cot_values, value_rows, per_head, preferred_element_type=jnp.float32
    ) + jnp.transpose(pair_part, (1, 0, 2))


def pair_from_attention(attention_half, logit_grad, pair_cot, bias_weight):
    return lax.dot_general(
        attention_half, pair_cot, (((0,), (1,)), ((1,), (0,))), preferred_element_type=jnp.float32
    ) + logit_weight * lax.dot_general(
        logit_grad, bias_weight, (((0,), (1,)), ((), ())), preferred_element_type=jnp.float32
    )


def body(
    pair_rep,
    labels,
    residue_mask,
    dist_weight,
    dist_bias,
    bias_weight,
    query_scalar,
    query_points,
    key_scalar,
    key_points,
    value_scalar,
    value_points,
    point_weight,
    cot_scalar,
    cot_points,
    cot_pair,
):
    stripe_pairs = lax.all_to_all(pair_rep, "col", split_axis=0, concat_axis=1, tiled=True)
    stripe_labels = lax.all_to_all(labels, "col", split_axis=0, concat_axis=1, tiled=True)
    row_count, length, channels = stripe_pairs.shape
    groups = lax.axis_size(("row", "col"))
    bin_count = dist_weight.shape[1]
    head_count = bias_weight.shape[1]
    head_size = query_scalar.shape[1] // head_count
    arrived = lax.all_to_all(
        mirror_blocks(stripe_pairs, groups), ("row", "col"), split_axis=0, concat_axis=2, tiled=True
    )
    pair_flip = arrived.reshape(row_count, length, channels)
    mask_float = residue_mask.astype(jnp.float32)
    bin_iota = lax.broadcasted_iota(jnp.int32, (1, 1, bin_count), 2)
    weight_flip = jnp.transpose(dist_weight)
    first_dims = (((0,), (0,)), ((), ()))
    key_bias_all = jnp.where(mask_float > 0, 0.0, -1000000000.0)
    key_all, keypt_all, value_all, valuept_all = (
        lax.all_gather(key_scalar, "row", axis=0, tiled=True),
        lax.all_gather(key_points, "row", axis=0, tiled=True),
        lax.all_gather(value_scalar, "row", axis=0, tiled=True),
        lax.all_gather(value_points, "row", axis=0, tiled=True),
    )
    start_row = lax.axis_index(("row", "col")) * row_count
    local_start = lax.axis_index("col") * row_count
    own_mask = lax.dynamic_slice_in_dim(mask_float, start_row, row_count, 0)
    valid_pairs = (own_mask[:, None] * mask_float[None, :])[:, :, None]
    logits = (
        jnp.dot(stripe_pairs, dist_weight, preferred_element_type=jnp.float32)
        + jnp.dot(pair_flip, dist_weight, preferred_element_type=jnp.float32)
        + dist_bias
    )
    probabilities = jax.nn.softmax(logits, axis=-1)
    grad_bins = (
        valid_pairs * (probabilities - (stripe_labels[:, :, None] == bin_iota).astype(jnp.float32))
    ).astype(jnp.bfloat16)
    own_term = jnp.dot(grad_bins, weight_flip, preferred_element_type=jnp.float32)
    arrived_grad = lax.all_to_all(
        mirror_blocks(own_term, groups).astype(jnp.bfloat16),
        ("row", "col"),
        split_axis=0,
        concat_axis=2,
        tiled=True,
    ).astype(jnp.float32)
    dist_grad = own_term + arrived_grad.reshape(row_count, length, channels)
    flat_bins = grad_bins.reshape(-1, bin_count)
    weight_term = lax.dot_general(
        stripe_pairs.reshape(-1, channels),
        flat_bins,
        first_dims,
        preferred_element_type=jnp.float32,
    ) + lax.dot_general(
        pair_flip.reshape(-1, channels), flat_bins, first_dims, preferred_element_type=jnp.float32
    )
    queries = lax.dynamic_slice_in_dim(query_scalar, local_start, row_count, 0).reshape(
        row_count, head_count, head_size
    )
    query_pts = lax.dynamic_slice_in_dim(query_points, local_start, row_count, 0).reshape(
        row_count, head_count, -1
    )
    attn_logits = attention_logits(
        queries,
        query_pts,
        key_all.reshape(length, head_count, head_size),
        keypt_all.reshape(length, head_count, -1),
        stripe_pairs,
        bias_weight,
        point_weight,
        key_bias_all,
    )
    attention = jax.nn.softmax(attn_logits, axis=-1)
    attention_half = attention.astype(jnp.bfloat16)
    cot_values = jnp.concatenate(
        [
            lax.dynamic_slice_in_dim(cot_scalar, local_start, row_count, 0).reshape(
                row_count, head_count, head_size
            ),
            lax.dynamic_slice_in_dim(cot_points, local_start, row_count, 0).reshape(
                row_count, head_count, -1
            ),
        ],
        axis=2,
    )
    value_rows = jnp.concatenate(
        [
            value_all.reshape(length, head_count, head_size),
            valuept_all.reshape(length, head_count, -1),
        ],
        axis=2,
    )
    pair_cot = lax.dynamic_slice_in_dim(cot_pair, local_start, row_count, 0).reshape(
        row_count, head_count, channels
    )
    value_grad = value_gradient(cot_values, value_rows, pair_cot, stripe_pairs)
    row_total = jnp.sum(attention * value_grad, axis=-1, keepdims=True)
    logit_grad = (attention * (value_grad - row_total)).astype(jnp.bfloat16)
    ipa_grad = pair_from_attention(attention_half, logit_grad, pair_cot, bias_weight)
    stripe_grad = (dist_grad + ipa_grad).astype(jnp.bfloat16)
    pair_grad = lax.all_to_all(stripe_grad, "col", split_axis=1, concat_axis=0, tiled=True)
    weight_grad = lax.psum(weight_term, ("row", "col"))
    return (pair_grad, weight_grad)


def solution(mesh):
    placed = (
        P("row", "col", None),
        P("row", "col"),
        P(),
        P(),
        P(),
        P(),
        P("row", None),
        P("row", None),
        P("row", None),
        P("row", None),
        P("row", None),
        P("row", None),
        P(),
        P("row", None),
        P("row", None),
        P("row", None),
    )
    return jax.shard_map(
        body, mesh=mesh, in_specs=placed, out_specs=(P("row", "col", None), P()), check_vma=False
    )
```

profile of v0, /device:TPU:2, one launch (start us, length us, event | category | flops | bytes accessed | tf_op | source)
XLA Modules:
  0.0 307.7 jit_solution(3419801581025930627)
XLA Ops:
  0.7 6.0 %all-to-all-start = ((bf16[64,128,128]{2,1,0:T(8,128)(2,1)}), bf16[64,128,128]{2,1,0:T(8,128)(2,1)S(1)}, u32[]{:S(2)}, u32[]{:S(2)}) async-start(bf16[64,128,128]{2,1,0:T(8,128)(2,1)} %param.16), calls=%async_computation | async-start | bytes 4194304 | tf_op jit(solution)/shard_map/all_to_all | solution.py:82
  7.5 41.4 %all_gather.13 = bf16[1024,144]{1,0:T(8,128)(2,1)S(1)} all-gather(bf16[64,144]{1,0:T(8,128)(2,1)S(1)} %copy-done.6), channel_id=1, replica_groups=mesh['row'=16,'col'=8] {'row'}, dimensions={0}, use_global_device_ids=true | all-gather | bytes 313344 | tf_op jit(solution)/shard_map/all_gather | solution.py:100
  48.9 4.8 %all-to-all-start.2 = ((s32[8,8,128]{2,1,0:T(8,128)}), s32[8,8,128]{2,1,0:T(8,128)S(1)}, u32[]{:S(2)}, u32[]{:S(2)}) async-start(s32[8,8,128]{2,1,0:T(8,128)} %bitcast.10), calls=%async_computation.2 | async-start | bytes 65536 | tf_op jit(solution)/shard_map/all_to_all | solution.py:83
  54.4 2.8 copy.73
  57.1 1.4 all-to-all-done.2
  58.6 6.8 %all-to-all-start.1 = ((bf16[128,8,8,128]{3,2,1,0:T(8,128)(2,1)}), bf16[128,8,8,128]{3,2,1,0:T(8,128)(2,1)}, u32[]{:S(2)}, u32[]{:S(2)}) async-start(bf16[128,8,8,128]{3,2,1,0:T(8,128)(2,1)} %bitcast.109), calls=%async_computation.1 | async-start | bytes 4194304 | tf_op jit(solution)/shard_map/all_to_all | solution.py:89
  65.4 0.7 constant_dynamic-slice_fusion.3
  66.7 40.9 %all_gather.12 = bf16[1024,192]{1,0:T(8,128)(2,1)} all-gather(bf16[64,192]{1,0:T(8,128)(2,1)S(1)} %copy-done.7), channel_id=1, replica_groups=mesh['row'=16,'col'=8] {'row'}, dimensions={0}, use_global_device_ids=true | all-gather | bytes 417792 | tf_op jit(solution)/shard_map/all_gather | solution.py:99
  107.6 24.3 %all_gather.14 = bf16[1024,192]{1,0:T(8,128)(2,1)} all-gather(bf16[64,192]{1,0:T(8,128)(2,1)S(1)} %copy-done.8), channel_id=1, replica_groups=mesh['row'=16,'col'=8] {'row'}, dimensions={0}, use_global_device_ids=true | all-gather | bytes 417792 | tf_op jit(solution)/shard_map/all_gather | solution.py:101
  132.6 0.9 fusion.18
  133.6 21.4 %all_gather.15 = bf16[1024,288]{1,0:T(8,128)(2,1)S(1)} all-gather(bf16[64,288]{1,0:T(8,128)(2,1)S(1)} %copy-done.5), channel_id=1, replica_groups=mesh['row'=16,'col'=8] {'row'}, dimensions={0}, use_global_device_ids=true | all-gather | bytes 626688 | tf_op jit(solution)/shard_map/all_gather | solution.py:102
  155.0 1.7 copy.72
  156.7 2.2 fusion.40
  158.9 6.0 %fusion.37 = f32[8,1024,128]{2,1,0:T(8,128)} fusion(s32[8,1024]{1,0:T(8,128)S(1)} %bitcast.117, f32[8,1024]{1,0:T(8,128)S(1)} %broadcast_multiply_fusion, bf16[128,64]{0,1:T(8,128)(2,1)S(1)} %copy-done.11, f32[8,1024,64]{1,2,0:T(8,128)} %fusion.40, f32[64]{0:T(128)S(1)} %copy-done.16, bf16[128,8,8,128]{3,2,1,0:T(8,128)(2,1)} %all-to-all-done.1), kind=kOutput, calls=%fused_computation.52 | convolution fusion | flops 273170560 | bytes 8470784 | tf_op jit(solution)/shard_map/dot_general | solution.py:117
  164.9 2.5 convert_bitcast_fusion.1
  167.4 3.8 %copy.129 = bf16[8,128,8,128]{3,0,2,1:T(8,128)(2,1)} copy(bf16[8,128,8,128]{3,2,1,0:T(8,128)(2,1)S(1)} %convert_bitcast_fusion.1) | data formatting | bytes 4194304 | tf_op jit(solution)/shard_map/convert_element_type | solution.py:119
  171.2 6.5 %all-to-all-start.3 = ((bf16[128,8,8,128]{3,2,1,0:T(8,128)(2,1)}), bf16[128,8,8,128]{3,2,1,0:T(8,128)(2,1)}, u32[]{:S(2)}, u32[]{:S(2)}) async-start(bf16[128,8,8,128]{3,2,1,0:T(8,128)(2,1)} %bitcast.110), calls=%async_computation.3 | async-start | bytes 4194304 | tf_op jit(solution)/shard_map/all_to_all | solution.py:118
  177.7 0.7 constant_dynamic-slice_fusion.1
  178.7 2.0 copy.77
  180.7 2.0 copy.87
  182.7 1.1 copy.88
  184.5 2.4 fusion.51
  186.8 1.1 fusion.49
  189.4 2.8 fusion.27
  192.2 13.7 %all-to-all-done.3 = bf16[128,8,8,128]{3,2,1,0:T(8,128)(2,1)} async-done(((bf16[128,8,8,128]{3,2,1,0:T(8,128)(2,1)}), bf16[128,8,8,128]{3,2,1,0:T(8,128)(2,1)}, u32[]{:S(2)}, u32[]{:S(2)}) %all-to-all-start.3) | async-done | bytes 2097184 | tf_op jit(solution)/shard_map/all_to_all | solution.py:118
  205.9 5.4 %fusion.5 = bf16[8,1024,128]{2,1,0:T(8,128)(2,1)S(1)} fusion(f32[8,1024,128]{2,1,0:T(8,128)} %fusion.37, f32[8,1024,128]{2,1,0:T(8,128)} %fusion.27, bf16[12,8,1024]{2,1,0:T(8,128)(2,1)S(1)} %fusion.20, bf16[128,12]{0,1:T(8,128)(2,1)S(1)} %copy-done.13, bf16[128,8,8,128]{3,2,1,0:T(8,128)(2,1)} %all-to-all-done.3), kind=kOutput, calls=%fused_computation.7 | convolution fusion | flops 31457280 | bytes 12782592 | tf_op jit(solution)/shard_map/dot_general | solution.py:59
  211.3 2.6 copy.92
  213.9 6.7 %all-to-all-start.4 = ((bf16[8,1024,128]{2,0,1:T(8,128)(2,1)}), bf16[8,1024,128]{2,0,1:T(8,128)(2,1)}, u32[]{:S(2)}, u32[]{:S(2)}) async-start(bf16[8,1024,128]{2,0,1:T(8,128)(2,1)} %copy.92), calls=%async_computation.4 | async-start | bytes 4194304 | tf_op jit(solution)/shard_map/all_to_all | solution.py:179
  220.6 3.7 %fusion.47 = bf16[8,8,8,1024]{3,2,1,0:T(8,128)(2,1)S(1)} fusion(s32[8,1024]{1,0:T(8,128)S(1)} %bitcast.118, f32[8,1024]{1,0:T(8,128)S(1)} %broadcast_multiply_fusion, f32[8,1024,64]{1,2,0:T(8,128)} %fusion.40, f32[64]{0:T(128)S(1)} %copy-done.17, bf16[128,64]{0,1:T(8,128)(2,1)} %param.19, bf16[128,8,8,128]{3,2,1,0:T(8,128)(2,1)} %all-to-all-done.1), kind=kOutput, calls=%fused_computation.69 | convolution fusion | flops 138952832 | bytes 5325056 | tf_op jit(solution)/shard_map/div | solution.py:113
  224.4 2.0 copy.74
  227.4 76.8 %psum.7 = f32[128,64]{0,1:T(8,128)} all-reduce(f32[128,64]{0,1:T(8,128)S(1)} %fusion.21), channel_id=1, replica_groups=mesh['row'=16,'col'=8] {'row','col'}, use_global_device_ids=true, to_apply=%region_7.8 | all-reduce | flops 8192 | bytes 65536 | tf_op jit(solution)/shard_map/psum | solution.py:180
  304.2 3.5 %copy.93 = bf16[8,8,128,128]{3,2,1,0:T(8,128)(2,1)} copy(bf16[8,8,128,128]{3,1,2,0:T(8,128)(2,1)} %bitcast.28) | data formatting | bytes 4194304 | tf_op jit(solution)/shard_map/all_to_all | solution.py:179
  (65 shorter events, 6.3 us)
Async XLA Ops:
  0.6 183.2 %copy-start = (bf16[64,1536]{1,0:T(8,128)(2,1)S(1)}, bf16[64,1536]{1,0:T(8,128)(2,1)}, u32[]{:S(2)}) copy-start(bf16[64,1536]{1,0:T(8,128)(2,1)} %param.31) | copy-start | bytes 589828
  0.6 6.9 %copy-start.6 = (bf16[64,144]{1,0:T(8,128)(2,1)S(1)}, bf16[64,144]{1,0:T(8,128)(2,1)}, u32[]{:S(2)}) copy-start(bf16[64,144]{1,0:T(8,128)(2,1)} %param.25) | copy-start | bytes 55300
  0.7 48.3 %all-to-all-start = ((bf16[64,128,128]{2,1,0:T(8,128)(2,1)}), bf16[64,128,128]{2,1,0:T(8,128)(2,1)S(1)}, u32[]{:S(2)}, u32[]{:S(2)}) async-start(bf16[64,128,128]{2,1,0:T(8,128)(2,1)} %param.16), calls=%async_computation | async-start | bytes 4194304 | tf_op jit(solution)/shard_map/all_to_all | solution.py:82
  48.9 8.2 %copy-start.1 = (bf16[64,128,128]{2,1,0:T(8,128)(2,1)}, bf16[64,128,128]{2,1,0:T(8,128)(2,1)S(1)}, u32[]{:S(2)}) copy-start(bf16[64,128,128]{2,1,0:T(8,128)(2,1)S(1)} %all-to-all-done) | copy-start | bytes 6291460
  48.9 9.6 %all-to-all-start.2 = ((s32[8,8,128]{2,1,0:T(8,128)}), s32[8,8,128]{2,1,0:T(8,128)S(1)}, u32[]{:S(2)}, u32[]{:S(2)}) async-start(s32[8,8,128]{2,1,0:T(8,128)} %bitcast.10), calls=%async_computation.2 | async-start | bytes 65536 | tf_op jit(solution)/shard_map/all_to_all | solution.py:83
  58.6 100.4 %copy-start.9 = (s32[8,8,128]{2,1,0:T(8,128)}, s32[8,8,128]{2,1,0:T(8,128)S(1)}, u32[]{:S(2)}) copy-start(s32[8,8,128]{2,1,0:T(8,128)S(1)} %all-to-all-done.2) | copy-start | bytes 98308
  58.6 7.5 %copy-start.14 = (s32[1024]{0:T(1024)S(1)}, s32[1024]{0:T(1024)}, u32[]{:S(2)}) copy-start(s32[1024]{0:T(1024)} %param.18) | copy-start | bytes 12292
  58.6 8.1 %copy-start.7 = (bf16[64,192]{1,0:T(8,128)(2,1)S(1)}, bf16[64,192]{1,0:T(8,128)(2,1)}, u32[]{:S(2)}) copy-start(bf16[64,192]{1,0:T(8,128)(2,1)} %param.24) | copy-start | bytes 73732
  58.6 100.4 %all-to-all-start.1 = ((bf16[128,8,8,128]{3,2,1,0:T(8,128)(2,1)}), bf16[128,8,8,128]{3,2,1,0:T(8,128)(2,1)}, u32[]{:S(2)}, u32[]{:S(2)}) async-start(bf16[128,8,8,128]{3,2,1,0:T(8,128)(2,1)} %bitcast.109), calls=%async_computation.1 | async-start | bytes 4194304 | tf_op jit(solution)/shard_map/all_to_all | solution.py:89
  65.4 42.2 %copy-start.8 = (bf16[64,192]{1,0:T(8,128)(2,1)S(1)}, bf16[64,192]{1,0:T(8,128)(2,1)}, u32[]{:S(2)}) copy-start(bf16[64,192]{1,0:T(8,128)(2,1)} %param.26) | copy-start | bytes 73732
  65.4 66.6 %copy-start.15 = (f32[12]{0:T(128)S(1)}, f32[12]{0:T(128)}, u32[]{:S(2)}) copy-start(f32[12]{0:T(128)} %param.28) | copy-start | bytes 148
  65.4 68.2 %copy-start.5 = (bf16[64,288]{1,0:T(8,128)(2,1)S(1)}, bf16[64,288]{1,0:T(8,128)(2,1)}, u32[]{:S(2)}) copy-start(bf16[64,288]{1,0:T(8,128)(2,1)} %param.27) | copy-start | bytes 110596
  155.0 1.7 copy-start.11
  156.7 2.2 copy-start.16
  171.2 34.7 %all-to-all-start.3 = ((bf16[128,8,8,128]{3,2,1,0:T(8,128)(2,1)}), bf16[128,8,8,128]{3,2,1,0:T(8,128)(2,1)}, u32[]{:S(2)}, u32[]{:S(2)}) async-start(bf16[128,8,8,128]{3,2,1,0:T(8,128)(2,1)} %bitcast.110), calls=%async_computation.3 | async-start | bytes 4194304 | tf_op jit(solution)/shard_map/all_to_all | solution.py:118
  177.7 6.1 %copy-start.12 = (bf16[128,12]{0,1:T(8,128)(2,1)S(1)}, bf16[128,12]{0,1:T(8,128)(2,1)}, u32[]{:S(2)}) copy-start(bf16[128,12]{0,1:T(8,128)(2,1)} %param.21) | copy-start | bytes 9220
  184.5 4.2 %copy-start.2 = (bf16[1024,288]{0,1:T(8,128)(2,1)S(1)}, bf16[1024,288]{0,1:T(8,128)(2,1)}, u32[]{:S(2)}) copy-start(bf16[1024,288]{0,1:T(8,128)(2,1)} %copy.88) | copy-start | bytes 1769476
  186.8 1.8 copy-start.3
  188.0 1.1 copy-start.4
  189.4 16.5 %copy-start.13 = (bf16[128,12]{0,1:T(8,128)(2,1)S(1)}, bf16[128,12]{0,1:T(8,128)(2,1)}, u32[]{:S(2)}) copy-start(bf16[128,12]{0,1:T(8,128)(2,1)} %param.21) | copy-start | bytes 9220
  213.9 6.7 %copy-start.10 = (s32[8,8,128]{2,1,0:T(8,128)S(1)}, s32[8,8,128]{2,1,0:T(8,128)}, u32[]{:S(2)}) copy-start(s32[8,8,128]{2,1,0:T(8,128)} %copy-done.9) | copy-start | bytes 98308
  213.9 6.7 %copy-start.17 = (f32[64]{0:T(128)S(1)}, f32[64]{0:T(128)}, u32[]{:S(2)}) copy-start(f32[64]{0:T(128)} %param.20) | copy-start | bytes 772
  213.9 90.3 %all-to-all-start.4 = ((bf16[8,1024,128]{2,0,1:T(8,128)(2,1)}), bf16[8,1024,128]{2,0,1:T(8,128)(2,1)}, u32[]{:S(2)}, u32[]{:S(2)}) async-start(bf16[8,1024,128]{2,0,1:T(8,128)(2,1)} %copy.92), calls=%async_computation.4 | async-start | bytes 4194304 | tf_op jit(solution)/shard_map/all_to_all | solution.py:179
where the time goes:
time: 311 us; the launch traced here: 308 us
  blocking collectives  205 us (66%)
  starting transfers between devices  30.7 us (10%)
  matrix products  26.1 us (8%)
  local copies, waits for them, and re-layouts  25.2 us (8%)
  waiting for transfers between devices  15.1 us (5%)
  other arithmetic  4.93 us (2%)
    psum x1, blocking collectives, body(): weight_grad = lax.psum(weight_term, ('row', 'col'))  76.8 us
    all_gather x1, blocking collectives, body(): lax.all_gather(key_points, 'row', axis=0, tiled=True)  41.4 us
    all_gather x1, blocking collectives, body(): lax.all_gather(key_scalar, 'row', axis=0, tiled=True)  40.9 us
    all_gather x1, blocking collectives, body(): lax.all_gather(value_scalar, 'row', axis=0, tiled=True)  24.3 us
    all_gather x1, blocking collectives, body(): lax.all_gather(value_points, 'row', axis=0, tiled=True)  21.4 us
    all_to_all x1, waiting for transfers between devices, body(): lax.all_to_all(mirror_blocks(own_term, groups).astype(jnp.bfloat16), ('ro...  13.7 us
    all_to_all x1, starting transfers between devices, body(): lax.all_to_all(mirror_blocks(stripe_pairs, groups), ('row', 'col'), split...  6.78 us
    all_to_all x1, starting transfers between devices, body(): lax.all_to_all(stripe_grad, 'col', split_axis=1, concat_axis=0, tiled=True)  6.68 us
  transfers between devices with their start and end apart: 5, of which 2 were waited for; matrix products, arithmetic and copies ran while one was open for 11% of the time, Pallas kernels for 0%

commit v1 on v0

v1 whole, which is shorter than its diff:
```python
import functools
import math

import jax
import jax.numpy as jnp
import numpy as np
from jax import lax
from jax.experimental import pallas as pl
from jax.experimental.pallas import tpu as pltpu
from jax.sharding import PartitionSpec as P

AXES = ("row", "col")
LOGIT_WEIGHT = math.sqrt(1.0 / 3.0)
HEADS = 12
PAD_HEADS = 16
CHUNK = 8
QUANT = 32760.0

WIDTHS = (192, 144, 192, 288)
PER_HEAD = (16, 12, 16, 24)
CAT = 896
WINDOWS = ((0, 256), (128, 384), (256, 896))

NT = (((1,), (1,)), ((), ()))
TN = (((0,), (0,)), ((), ()))

CHIPS = [(x, y, z) for x in range(4) for y in range(4) for z in range(4)]
Y_SWAP = (0, 2, 1, 3)


def device_index(chip, core):
    x, y, z = chip
    return ((y // 2) * 8 + z * 2 + core) * 8 + (y % 2) * 4 + x


def mirror_chip(chip):
    x, y, z = chip
    return (z, Y_SWAP[y], x)


def halfway_chip(chip, core):
    x, y, z = chip
    if core == 0:
        return (x, y, (3 * x + 3 * z + 2) % 4)
    return (x, Y_SWAP[y], (3 * x + 3 * z) % 4)


FIRST_HOP = [(device_index(n, h), device_index(halfway_chip(n, h), h)) for n in CHIPS for h in (0, 1)]
SECOND_HOP = [
    [
        (device_index(halfway_chip(n, h), h), device_index(mirror_chip(n), (h + s) % 2))
        for n in CHIPS
        for h in (0, 1)
    ]
    for s in (0, 1)
]
MIRROR = [(device_index(n, h), device_index(mirror_chip(n), h)) for n in CHIPS for h in (0, 1)]
CORE_SWAP = [(device_index(n, h), device_index(n, 1 - h)) for n in CHIPS for h in (0, 1)]


def shift_map(axis, distance):
    pairs = []
    for n in CHIPS:
        m = list(n)
        m[axis] = (m[axis] + distance) % 4
        pairs += [(device_index(n, h), device_index(tuple(m), h)) for h in (0, 1)]
    return pairs


def head_masks():
    masks = np.zeros((3, PAD_HEADS, CAT), np.float32)
    start = 0
    for part, (width, size) in enumerate(zip(WIDTHS, PER_HEAD)):
        for column in range(width):
            masks[min(part, 2), column // size, start + column] = 1.0
        start += width
    return [masks[k][:, lo:hi] for k, (lo, hi) in enumerate(WINDOWS)]


def dot(a, b, dims=(((1,), (0,)), ((), ()))):
    return lax.dot_general(a, b, dims, preferred_element_type=jnp.float32)


def eye(n, dtype):
    return (
        lax.broadcasted_iota(jnp.int32, (n, n), 0) == lax.broadcasted_iota(jnp.int32, (n, n), 1)
    ).astype(dtype)


def flipped(weight, rows):
    k = weight.shape[1]
    pick = (
        lax.broadcasted_iota(jnp.int32, (rows, k), 0) == lax.broadcasted_iota(jnp.int32, (rows, k), 1)
    ).astype(jnp.bfloat16)
    return dot(pick, weight, NT).astype(jnp.bfloat16)


def own_core():
    return lax.rem(lax.axis_index("row"), 2)


def logits_kernel(pair_ref, weight_ref, labels_ref, own_ref, same_ref, other_ref, slabs, top):
    step = pl.program_id(0)
    weight_t = flipped(weight_ref[...], 64)
    flat = pair_ref[...].reshape(CHUNK * 128, 128)
    terms = dot(weight_t, flat, NT)
    for t in range(CHUNK):
        term = terms[:, t * 128 : (t + 1) * 128]
        row = step * CHUNK + t
        own_ref[t] = term
        slabs[pl.ds(row, 64, stride=64), :] = term
        top[pl.ds(row, 1), :] = jnp.max(jnp.abs(term), axis=0, keepdims=True)

    @pl.when(step == pl.num_programs(0) - 1)
    def _():
        core = own_core()
        level = jnp.ceil(16.0 * jnp.log2(jnp.maximum(top[...], 1e-30)))
        scale = jnp.exp2(level * (-1.0 / 16.0)) * QUANT

        def put(slab, upper, lower):
            turned = jnp.transpose(jnp.concatenate([upper, lower], axis=0))
            first, second = turned[:64], turned[64:]
            same_ref[slab] = narrow(jnp.where(core == 0, first, second))
            other_ref[slab] = narrow(jnp.where(core == 0, second, first))

        def narrow(values):
            return jnp.clip(jnp.round(values), -32767.0, 32767.0).astype(jnp.int32).astype(jnp.int16)

        def pair_of_bins(b, carry):
            upper = slabs[pl.ds(pl.multiple_of(b * 64, 64), 64), :] * scale
            lower = slabs[pl.ds(pl.multiple_of((b + 32) * 64, 64), 64), :] * scale
            put(b, upper, lower)
            return carry

        lax.fori_loop(0, 32, pair_of_bins, 0)
        put(32, level, labels_ref[...].astype(jnp.float32))


def own_logits(pair_tile, dist_weight, labels):
    rows = pair_tile.shape[0]
    block = jax.ShapeDtypeStruct((33, 64, 128), jnp.int16)
    whole = lambda *shape: pl.BlockSpec(shape, lambda i: (0,) * len(shape))
    return pl.pallas_call(
        logits_kernel,
        grid=(rows // CHUNK,),
        in_specs=[
            pl.BlockSpec((CHUNK, 128, 128), lambda i: (i, 0, 0)),
            whole(128, 64),
            whole(64, 128),
        ],
        out_specs=[
            pl.BlockSpec((CHUNK, 64, 128), lambda i: (i, 0, 0)),
            whole(33, 64, 128),
            whole(33, 64, 128),
        ],
        out_shape=[jax.ShapeDtypeStruct((rows, 64, 128), jnp.float32), block, block],
        scratch_shapes=[pltpu.VMEM((64 * 64, 128), jnp.float32), pltpu.VMEM((64, 128), jnp.float32)],
        compiler_params=pltpu.CompilerParams(vmem_limit_bytes=32 * 1024 * 1024),
        cost_estimate=pl.CostEstimate(flops=200_000_000, bytes_accessed=6_000_000, transcendentals=8192),
        name="own_logits",
    )(pair_tile, dist_weight, labels)


def attention_kernel(
    pair_ref, cat_ref, near_ref, far_ref, cot_ref, bias_ref, point_ref, mask_ref, scalar_mask_ref, point_mask_ref,
    value_mask_ref, exp_ref, grad_ref, cot_out_ref, stats_ref, keys, cot_rows,
):
    step = pl.program_id(0)
    length = CHUNK * PAD_HEADS

    @pl.when(step == 0)
    def _():
        core = own_core()
        near, far = near_ref[...].astype(jnp.float32), far_ref[...].astype(jnp.float32)
        keys[:64] = jnp.where(core == 0, near, far).astype(jnp.bfloat16)
        keys[64:] = jnp.where(core == 0, far, near).astype(jnp.bfloat16)
        for h in range(HEADS):
            cot_rows[h * 64 : (h + 1) * 64] = cot_ref[:, h * 128 : (h + 1) * 128]

    def iota(shape, dim):
        return lax.broadcasted_iota(jnp.int32, shape, dim)

    residue = step * CHUNK + iota((length, 64), 0) // PAD_HEADS
    pick = (residue == iota((length, 64), 1)).astype(jnp.bfloat16)
    spread = dot(pick, cat_ref[...])
    left = []
    for (lo, hi), mask in zip(WINDOWS, (scalar_mask_ref, point_mask_ref, value_mask_ref)):
        head_columns = jnp.concatenate([mask[...]] * CHUNK, axis=0)
        left.append(spread[:, lo:hi] * head_columns)
    right = [keys[:, lo:hi] for lo, hi in WINDOWS]
    scalar_term, cross_term, value_term = [dot(a.astype(jnp.bfloat16), b, NT) for a, b in zip(left, right)]
    query_sq = jnp.sum(left[1] * left[1], axis=1, keepdims=True)
    key_points = right[1].astype(jnp.float32)
    key_sq = lax.dot_general(
        point_mask_ref[...],
        key_points * key_points,
        NT,
        precision=lax.Precision.HIGHEST,
        preferred_element_type=jnp.float32,
    )
    key_sq = jnp.concatenate([key_sq] * CHUNK, axis=0)

    row_of = iota((length, 768), 0)
    column_of = iota((length, 768), 1)
    cot_pick = (step * CHUNK + row_of // PAD_HEADS == column_of % 64) & (row_of % PAD_HEADS == column_of // 64)
    cot = dot(cot_pick.astype(jnp.bfloat16), cot_rows[...]).astype(jnp.bfloat16)
    cot_out_ref[...] = cot.reshape(CHUNK, PAD_HEADS, 128)

    bias_t = flipped(bias_ref[...], PAD_HEADS)
    pair_bias, pair_value = [], []
    for t in range(CHUNK):
        both = jnp.concatenate([bias_t, cot[t * PAD_HEADS : (t + 1) * PAD_HEADS]], axis=0)
        result = dot(both, pair_ref[t], NT)
        pair_bias.append(result[:PAD_HEADS])
        pair_value.append(result[PAD_HEADS:])
    pair_bias = jnp.concatenate(pair_bias, axis=0)
    value_grad = value_term + jnp.concatenate(pair_value, axis=0)

    head_of = iota((length, 128), 0) % PAD_HEADS
    raw = jnp.sum(jnp.where(head_of == iota((length, 128), 1), point_ref[...], 0.0), axis=1, keepdims=True)
    softplus = jnp.maximum(raw, 0.0) + jnp.log1p(jnp.exp(-jnp.abs(raw)))
    point_scale = softplus * (math.sqrt(2.0 / 36.0) / 2.0)

    column_mask = mask_ref[pl.ds(lax.axis_index("col"), 1), :]
    key_bias = jnp.where(column_mask > 0, 0.0, -1000000000.0)
    logits = (
        LOGIT_WEIGHT
        * (scalar_term * 0.25 + pair_bias - point_scale * (query_sq + key_sq - 2.0 * cross_term))
        + key_bias
    )
    top = jnp.max(logits, axis=1, keepdims=True)
    weights = jnp.exp(logits - top)
    total = jnp.sum(weights, axis=1, keepdims=True)
    weighted = jnp.sum(weights * value_grad, axis=1, keepdims=True)
    exp_ref[...] = weights.reshape(CHUNK, PAD_HEADS, 128)
    grad_ref[...] = value_grad.reshape(CHUNK, PAD_HEADS, 128)
    lane = iota((length, 128), 1)
    packed = jnp.where(lane == 0, top, jnp.where(lane == 1, total, jnp.where(lane == 2, weighted, 0.0)))
    packed = jnp.transpose(packed)
    for q in range(3):
        stats_ref[pl.ds(q * 8 + step, 1), :] = packed[q : q + 1]


def attention_parts(pair_tile, cat, near, far, cot_pair, bias_weight, point_row, mask_rows):
    rows = pair_tile.shape[0]
    whole = lambda *shape: pl.BlockSpec(shape, lambda i: (0,) * len(shape))
    part = pl.BlockSpec((CHUNK, PAD_HEADS, 128), lambda i: (i, 0, 0))
    masks = [jnp.asarray(m) for m in head_masks()]
    return pl.pallas_call(
        attention_kernel,
        grid=(rows // CHUNK,),
        in_specs=[
            pl.BlockSpec((CHUNK, 128, 128), lambda i: (i, 0, 0)),
            whole(64, CAT),
            whole(64, CAT),
            whole(64, CAT),
            whole(64, 1536),
            whole(128, HEADS),
            whole(1, 128),
            whole(8, 128),
        ]
        + [whole(*m.shape) for m in masks],
        out_specs=[part, part, part, whole(24, 128)],
        out_shape=[
            jax.ShapeDtypeStruct((rows, PAD_HEADS, 128), jnp.float32),
            jax.ShapeDtypeStruct((rows, PAD_HEADS, 128), jnp.float32),
            jax.ShapeDtypeStruct((rows, PAD_HEADS, 128), jnp.bfloat16),
            jax.ShapeDtypeStruct((24, 128), jnp.float32),
        ],
        scratch_shapes=[pltpu.VMEM((128, CAT), jnp.bfloat16), pltpu.VMEM((768, 128), jnp.bfloat16)],
        compiler_params=pltpu.CompilerParams(vmem_limit_bytes=32 * 1024 * 1024),
        cost_estimate=pl.CostEstimate(flops=1_000_000_000, bytes_accessed=4_000_000, transcendentals=200_000),
        name="attention_parts",
    )(pair_tile, cat, near, far, cot_pair, bias_weight, point_row, mask_rows, *masks)


def bins_kernel(
    mask_smem, pair_ref, own_ref, near_ref, far_ref, labels_ref, bias_ref, mask_ref, bins_ref, weight_ref, mirror,
    mirror_labels,
):
    step = pl.program_id(0)

    @pl.when(step == 0)
    def _():
        core = own_core()
        low_lanes = lax.broadcasted_iota(jnp.int32, (64, 128), 1) < 64

        def halves(slab):
            near = near_ref[slab].astype(jnp.int32).astype(jnp.float32)
            far = far_ref[slab].astype(jnp.int32).astype(jnp.float32)
            first = jnp.where(core == 0, near, far)
            second = jnp.where(core == 0, far, near)
            upper = jnp.where(low_lanes, first, pltpu.roll(second, 64, 1))
            lower = jnp.where(low_lanes, pltpu.roll(first, 64, 1), second)
            return upper, lower

        level, other_labels = halves(32)
        mirror_labels[...] = other_labels
        scale = jnp.exp2(level * (1.0 / 16.0)) * (1.0 / QUANT)

        def pair_of_bins(b, carry):
            upper, lower = halves(b)
            mirror[pl.ds(pl.multiple_of(b * 64, 64), 64), :] = upper * scale
            mirror[pl.ds(pl.multiple_of((b + 32) * 64, 64), 64), :] = lower * scale
            return carry

        lax.fori_loop(0, 32, pair_of_bins, 0)
        weight_ref[...] = jnp.zeros_like(weight_ref)

    bias = jnp.sum(eye(64, jnp.float32) * bias_ref[...], axis=1, keepdims=True)
    column_mask = mask_ref[pl.ds(lax.axis_index("col"), 1), :].astype(jnp.float32)
    bin_of = lax.broadcasted_iota(jnp.int32, (64, 128), 0)
    first_row = lax.axis_index("row") * 64
    grads = []
    for t in range(CHUNK):
        row = step * CHUNK + t
        logits = own_ref[t] + mirror[pl.ds(row, 64, stride=64), :] + bias
        weights = jnp.exp(logits - jnp.max(logits, axis=0, keepdims=True))
        valid = column_mask * mask_smem[first_row + row].astype(jnp.float32)
        share = 2.0 * valid / jnp.sum(weights, axis=0, keepdims=True)
        own_label = labels_ref[pl.ds(row, 1), :]
        other_label = mirror_labels[pl.ds(row, 1), :].astype(jnp.int32)
        hits = jnp.where(bin_of == own_label, valid, 0.0) + jnp.where(bin_of == other_label, valid, 0.0)
        grad = (weights * share - hits).astype(jnp.bfloat16)
        bins_ref[t] = grad
        grads.append(grad)
    flat = pair_ref[...].reshape(CHUNK * 128, 128)
    weight_ref[...] += dot(jnp.concatenate(grads, axis=1), flat)


def bin_gradient(pair_tile, own, near, far, labels, dist_bias, mask_rows, residue_mask):
    rows = pair_tile.shape[0]
    whole = lambda *shape: pl.BlockSpec(shape, lambda i: (0,) * len(shape))
    return pl.pallas_call(
        bins_kernel,
        grid=(rows // CHUNK,),
        in_specs=[
            pl.BlockSpec(memory_space=pltpu.SMEM),
            pl.BlockSpec((CHUNK, 128, 128), lambda i: (i, 0, 0)),
            pl.BlockSpec((CHUNK, 64, 128), lambda i: (i, 0, 0)),
            whole(33, 64, 128),
            whole(33, 64, 128),
            whole(64, 128),
            whole(1, 64),
            whole(8, 128),
        ],
        out_specs=[pl.BlockSpec((CHUNK, 64, 128), lambda i: (i, 0, 0)), whole(64, 128)],
        out_shape=[
            jax.ShapeDtypeStruct((rows, 64, 128), jnp.bfloat16),
            jax.ShapeDtypeStruct((64, 128), jnp.float32),
        ],
        scratch_shapes=[pltpu.VMEM((64 * 64, 128), jnp.float32), pltpu.VMEM((64, 128), jnp.float32)],
        compiler_params=pltpu.CompilerParams(vmem_limit_bytes=32 * 1024 * 1024),
        cost_estimate=pl.CostEstimate(flops=200_000_000, bytes_accessed=6_000_000, transcendentals=600_000),
        name="bin_gradient",
    )(residue_mask, pair_tile, own, near, far, labels, dist_bias, mask_rows)


def output_kernel(exp_ref, grad_ref, stats_ref, bins_ref, cot_ref, weight_ref, bias_ref, out_ref):
    step = pl.program_id(0)
    length = CHUNK * PAD_HEADS
    tops = [stats_ref[c, pl.ds(step, 1), :] for c in range(8)]
    totals = [stats_ref[c, pl.ds(8 + step, 1), :] for c in range(8)]
    weighted = [stats_ref[c, pl.ds(16 + step, 1), :] for c in range(8)]
    top = functools.reduce(jnp.maximum, tops)
    factors = [jnp.exp(m - top) for m in tops]
    total = sum(f * s for f, s in zip(factors, totals))
    mean = sum(f * s for f, s in zip(factors, weighted)) / total
    own_top = stats_ref[lax.axis_index("col"), pl.ds(step, 1), :]
    share = jnp.exp(own_top - top) / total
    share = jnp.transpose(jnp.broadcast_to(share, (length, 128)))
    mean = jnp.transpose(jnp.broadcast_to(mean, (length, 128)))
    attention = exp_ref[...].reshape(length, 128) * share
    logit_grad = attention * (grad_ref[...].reshape(length, 128) - mean)
    attention = attention.astype(jnp.bfloat16)
    logit_grad = (logit_grad * LOGIT_WEIGHT).astype(jnp.bfloat16)
    weight_t = flipped(weight_ref[...], 64)
    bias_t = flipped(bias_ref[...], PAD_HEADS)
    for t in range(CHUNK):
        rows = slice(t * PAD_HEADS, (t + 1) * PAD_HEADS)
        left = jnp.concatenate([bins_ref[t], attention[rows], logit_grad[rows]], axis=0)
        right = jnp.concatenate([weight_t, cot_ref[t], bias_t], axis=0)
        out_ref[t] = dot(left, right, TN).astype(jnp.bfloat16)


def pair_gradient(weights, value_grad, stats, bins, cot, dist_weight, bias_weight):
    rows = bins.shape[0]
    whole = lambda *shape: pl.BlockSpec(shape, lambda i: (0,) * len(shape))
    part = pl.BlockSpec((CHUNK, PAD_HEADS, 128), lambda i: (i, 0, 0))
    return pl.pallas_call(
        output_kernel,
        grid=(rows // CHUNK,),
        in_specs=[
            part,
            part,
            whole(8, 24, 128),
            pl.BlockSpec((CHUNK, 64, 128), lambda i: (i, 0, 0)),
            part,
            whole(128, 64),
            whole(128, HEADS),
        ],
        out_specs=pl.BlockSpec((CHUNK, 128, 128), lambda i: (i, 0, 0)),
        out_shape=jax.ShapeDtypeStruct((rows, 128, 128), jnp.bfloat16),
        compiler_params=pltpu.CompilerParams(vmem_limit_bytes=32 * 1024 * 1024),
        cost_estimate=pl.CostEstimate(flops=300_000_000, bytes_accessed=5_000_000, transcendentals=10_000),
        name="pair_gradient",
    )(weights, value_grad, stats, bins, cot, dist_weight, bias_weight)


def sum_over_devices(term):
    term = term + lax.ppermute(term, AXES, CORE_SWAP)
    for axis in range(3):
        one, two, three = [lax.ppermute(term, AXES, shift_map(axis, d)) for d in (1, 2, 3)]
        term = (term + two) + (one + three)
    return term


def body(
    pair_rep,
    labels,
    residue_mask,
    dist_weight,
    dist_bias,
    bias_weight,
    query_scalar,
    query_points,
    key_scalar,
    key_points,
    value_scalar,
    value_points,
    point_weight,
    cot_scalar,
    cot_points,
    cot_pair,
):
    pad = jnp.zeros((query_scalar.shape[0], CAT - sum(WIDTHS)), jnp.bfloat16)
    own_keys = jnp.concatenate([key_scalar, key_points, value_scalar, value_points, pad], axis=1)
    near_keys = lax.ppermute(own_keys, AXES, MIRROR)
    far_keys = lax.ppermute(near_keys, AXES, CORE_SWAP)
    cat = jnp.concatenate([query_scalar, query_points, cot_scalar, cot_points, pad], axis=1)
    mask_rows = residue_mask.reshape(8, 128)
    point_row = jnp.concatenate([point_weight, jnp.zeros((128 - HEADS,), jnp.float32)]).reshape(1, 128)

    own, same, other = own_logits(pair_rep, dist_weight, labels)
    same = lax.ppermute(same, AXES, FIRST_HOP)
    other = lax.ppermute(other, AXES, FIRST_HOP)
    same = lax.ppermute(same, AXES, SECOND_HOP[0])
    other = lax.ppermute(other, AXES, SECOND_HOP[1])

    weights, value_grad, cot, stats = attention_parts(
        pair_rep, cat, near_keys, far_keys, cot_pair, bias_weight, point_row, mask_rows
    )
    stats = lax.all_to_all(
        jnp.broadcast_to(stats[None], (8,) + stats.shape), "col", split_axis=0, concat_axis=0, tiled=True
    )
    bins, weight_term = bin_gradient(
        pair_rep, own, same, other, labels, dist_bias.reshape(1, 64), mask_rows, residue_mask
    )
    weight_grad = jnp.transpose(sum_over_devices(weight_term))
    pair_grad = pair_gradient(weights, value_grad, stats, bins, cot, dist_weight, bias_weight)
    return (pair_grad, weight_grad)


def solution(mesh):
    placed = (
        P("row", "col", None),
        P("row", "col"),
        P(),
        P(),
        P(),
        P(),
        P("row", None),
        P("row", None),
        P("row", None),
        P("row", None),
        P("row", None),
        P("row", None),
        P(),
        P("row", None),
        P("row", None),
        P("row", None),
    )
    return jax.shard_map(
        body, mesh=mesh, in_specs=placed, out_specs=(P("row", "col", None), P()), check_vma=False
    )
```

time: 311 us -> 111 us (0.36)
  blocking collectives: 205 us -> 0 us
  Pallas kernels: 0 us -> 26.2 us
  matrix products: 26.1 us -> 0 us
  starting transfers between devices: 30.7 us -> 46.3 us
  local copies, waits for them, and re-layouts: 25.2 us -> 12.8 us
  waiting for transfers between devices: 15.1 us -> 20.7 us
    all_gather x4 -> x0, blocking collectives: 128 us -> none  [the longest x1 41.4 us: body(): lax.all_gather(key_points, 'row', axis=0, tiled=True)]
    psum x1 -> x0, blocking collectives: 76.8 us -> none  [body(): weight_grad = lax.psum(weight_term, ('row', 'col'))]
    ppermute x0 -> x16, starting transfers between devices: none -> 40.6 us  [the longest x9 26.9 us: sum_over_devices(): lax.ppermute(term, AXES, shift_map(axis, d))]
    pallas_call x0 -> x4, Pallas kernels: none -> 26.2 us  [the longest x1 7.4 us: bin_gradient(): pl.pallas_call(bins_kernel, grid=(rows // CHUNK,), in_specs=[pl.BlockSpec...]
    all_to_all x5 -> x1, starting transfers between devices: 30.7 us -> 5.67 us  [body(): lax.all_to_all(jnp.broadcast_to(stats[None], (8,) + stats.shape), 'col',...]
    ppermute x0 -> x16, waiting for transfers between devices: none -> 20.7 us  [the longest x1 7.02 us: body(): other = lax.ppermute(other, AXES, SECOND_HOP[1])]
    dot_general x10 -> x0, matrix products: 20 us -> none  [the longest x1 5.97 us: body(): jnp.dot(grad_bins, weight_flip, preferred_element_type=jnp.float32)]
    all_to_all x5 -> x1, waiting for transfers between devices: 15.1 us -> 0.01 us  [body(): lax.all_to_all(jnp.broadcast_to(stats[None], (8,) + stats.shape), 'col',...]
  transfers between devices with their start and end apart: 5 -> 17, of which waited for: 2 -> 5; matrix products, arithmetic and copies ran while one was open for 11% -> 5% of each run, Pallas kernels for 0% -> 11%
where the time goes in v1:
time: 111 us; the launch traced here: 110 us
  starting transfers between devices  46.3 us (42%)
  Pallas kernels  26.2 us (24%)
  waiting for transfers between devices  20.7 us (19%)
  local copies, waits for them, and re-layouts  12.8 us (12%)
  other arithmetic  2.85 us (3%)
    ppermute x9, starting transfers between devices, sum_over_devices(): lax.ppermute(term, AXES, shift_map(axis, d))  26.9 us
    unnamed x50, local copies, waits for them, and re-layouts  9.82 us
    pallas_call x1, Pallas kernels, bin_gradient(): pl.pallas_call(bins_kernel, grid=(rows // CHUNK,), in_specs=[pl.BlockSpec...  7.4 us
    pallas_call x1, Pallas kernels, attention_parts(): pl.pallas_call(attention_kernel, grid=(rows // CHUNK,), in_specs=[pl.Bloc...  7.08 us
    pallas_call x1, Pallas kernels, own_logits(): pl.pallas_call(logits_kernel, grid=(rows // CHUNK,), in_specs=[pl.BlockSp...  7.05 us
    ppermute x1, waiting for transfers between devices, body(): other = lax.ppermute(other, AXES, SECOND_HOP[1])  7.02 us
    all_to_all x1, starting transfers between devices, body(): lax.all_to_all(jnp.broadcast_to(stats[None], (8,) + stats.shape), 'col',...  5.67 us
    ppermute x1, waiting for transfers between devices, body(): same = lax.ppermute(same, AXES, SECOND_HOP[0])  5.66 us
  transfers between devices with their start and end apart: 17, of which 5 were waited for; matrix products, arithmetic and copies ran while one was open for 5% of the time, Pallas kernels for 11%

profile of v1, /device:TPU:2, one launch (start us, length us, event | category | flops | bytes accessed | tf_op | source)
XLA Modules:
  0.0 109.8 jit_solution(4105935043257094316)
XLA Ops:
  0.7 0.8 copy.22.weight_ref
  1.5 1.6 %copy-done = bf16[64,128,128]{2,1,0:T(8,128)(2,1)S(1)} copy-done((bf16[64,128,128]{2,1,0:T(8,128)(2,1)S(1)}, bf16[64,128,128]{2,1,0:T(8,128)(2,1)}, u32[]{:S(2)}) %copy-start) | copy-done | bytes 2097176
  3.9 7.1 %own_logits.1 = (f32[64,64,128]{2,1,0:T(8,128)S(1)}, s16[33,64,128]{2,1,0:T(8,128)(2,1)S(1)}, s16[33,64,128]{2,1,0:T(8,128)(2,1)S(1)}) custom-call(bf16[64,128,128]{2,1,0:T(8,128)(2,1)S(1)} %copy-done, bf16[128,64]{1,0:T(8,128)(2,1)S(1)} %copy.22.weight_ref, s32[64,128]{1,0:T(8,128)S(1)} %copy-done.6), custom_call_target="tpu_custom_call" | custom-call | flops 200000000 | bytes 6000000 | tf_op jit(solution)/shard_map/own_logits/pallas_call | solution.py:143
  10.9 3.8 %collective-permute-start.2 = (s16[33,64,128]{2,1,0:T(8,128)(2,1)S(1)}, s16[33,64,128]{2,1,0:T(8,128)(2,1)S(1)}, u32[]{:S(2)}, u32[]{:S(2)}) collective-permute-start(s16[33,64,128]{2,1,0:T(8,128)(2,1)S(1)} %get-tuple-element.15), channel_id=1, source_target_pairs={{0,32},{8,8},{16,16},{24,56},{32,0},{40,40},{48,48},{56,24},{4,36}... | collective-permute-start | bytes 1622024 | tf_op jit(solution)/shard_map/ppermute | solution.py:445
  14.8 2.0 %collective-permute-start.4 = (s16[33,64,128]{2,1,0:T(8,128)(2,1)S(1)}, s16[33,64,128]{2,1,0:T(8,128)(2,1)S(1)}, u32[]{:S(2)}, u32[]{:S(2)}) collective-permute-start(s16[33,64,128]{2,1,0:T(8,128)(2,1)S(1)} %get-tuple-element.16), channel_id=1, source_target_pairs={{0,32},{8,8},{16,16},{24,56},{32,0},{40,40},{48,48},{56,24},{4,36}... | collective-permute-start | bytes 1622024 | tf_op jit(solution)/shard_map/ppermute | solution.py:446
  16.8 5.4 %collective-permute-done.2 = s16[33,64,128]{2,1,0:T(8,128)(2,1)S(1)} collective-permute-done((s16[33,64,128]{2,1,0:T(8,128)(2,1)S(1)}, s16[33,64,128]{2,1,0:T(8,128)(2,1)S(1)}, u32[]{:S(2)}, u32[]{:S(2)}) %collective-permute-start.2) | collective-permute-done | bytes 540704 | tf_op jit(solution)/shard_map/ppermute | solution.py:445
  22.2 3.8 %collective-permute-start.3 = (s16[33,64,128]{2,1,0:T(8,128)(2,1)S(1)}, s16[33,64,128]{2,1,0:T(8,128)(2,1)S(1)}, u32[]{:S(2)}, u32[]{:S(2)}) collective-permute-start(s16[33,64,128]{2,1,0:T(8,128)(2,1)S(1)} %collective-permute-done.2), channel_id=1, source_target_pairs={{32,0},{8,8},{16,1},{56,9},{0,2},{40,10},{48,3},{24,11},{36,64},{7... | collective-permute-start | bytes 1622024 | tf_op jit(solution)/shard_map/ppermute | solution.py:447
  26.0 2.0 %collective-permute-done.4 = s16[33,64,128]{2,1,0:T(8,128)(2,1)S(1)} collective-permute-done((s16[33,64,128]{2,1,0:T(8,128)(2,1)S(1)}, s16[33,64,128]{2,1,0:T(8,128)(2,1)S(1)}, u32[]{:S(2)}, u32[]{:S(2)}) %collective-permute-start.4) | collective-permute-done | bytes 540704 | tf_op jit(solution)/shard_map/ppermute | solution.py:446
  28.7 5.7 %collective-permute-done.3.near_ref = s16[33,64,128]{2,1,0:T(8,128)(2,1)S(1)} collective-permute-done((s16[33,64,128]{2,1,0:T(8,128)(2,1)S(1)}, s16[33,64,128]{2,1,0:T(8,128)(2,1)S(1)}, u32[]{:S(2)}, u32[]{:S(2)}) %collective-permute-start.3) | collective-permute-done | bytes 540704 | tf_op jit(solution)/shard_map/ppermute | solution.py:447
  34.3 7.0 %collective-permute-done.5.far_ref = s16[33,64,128]{2,1,0:T(8,128)(2,1)S(1)} collective-permute-done((s16[33,64,128]{2,1,0:T(8,128)(2,1)S(1)}, s16[33,64,128]{2,1,0:T(8,128)(2,1)S(1)}, u32[]{:S(2)}, u32[]{:S(2)}) %collective-permute-start.5) | collective-permute-done | bytes 540704 | tf_op jit(solution)/shard_map/ppermute | solution.py:448
  41.5 7.4 %bin_gradient.1 = (bf16[64,64,128]{2,1,0:T(8,128)(2,1)S(1)}, f32[64,128]{1,0:T(8,128)S(1)}) custom-call(s32[1024]{0:T(1024)S(1)} %copy-done.9, bf16[64,128,128]{2,1,0:T(8,128)(2,1)S(1)} %copy-done, f32[64,64,128]{2,1,0:T(8,128)S(1)} %get-tuple-element.14.own_ref, s16[33,64,128]{2,1,0:T(8,128)(2,1)S(1)} %collective-permute-done.3.near_ref, ...), custom_call_target="tpu_custom_call" | custom-call | flops 200000000 | bytes 6000000 | tf_op jit(solution)/shard_map/bin_gradient/pallas_call | solution.py:334
  49.8 3.3 %collective-permute-start = (bf16[64,896]{1,0:T(8,128)(2,1)}, bf16[64,896]{1,0:T(8,128)(2,1)S(1)}, u32[]{:S(2)}, u32[]{:S(2)}) collective-permute-start(bf16[64,896]{1,0:T(8,128)(2,1)} %concatenate.10), channel_id=1, source_target_pairs={{0,0},{8,8},{16,1},{24,9},{32,2},{40,10},{48,3},{56,11},{4,64},{12... | collective-permute-start | bytes 344072 | tf_op jit(solution)/shard_map/ppermute | solution.py:438
  53.1 5.5 %collective-permute-start.7 = (f32[64,128]{1,0:T(8,128)S(1)}, f32[64,128]{1,0:T(8,128)S(1)}, u32[]{:S(2)}, u32[]{:S(2)}) collective-permute-start(f32[64,128]{1,0:T(8,128)S(1)} %add.32), channel_id=1, source_target_pairs={{0,2},{8,10},{16,18},{24,26},{32,34},{40,42},{48,50},{56,58},{4,6}... | collective-permute-start | bytes 98312 | tf_op jit(solution)/shard_map/ppermute | solution.py:413
  58.6 1.7 %collective-permute-start.8 = (f32[64,128]{1,0:T(8,128)S(1)}, f32[64,128]{1,0:T(8,128)}, u32[]{:S(2)}, u32[]{:S(2)}) collective-permute-start(f32[64,128]{1,0:T(8,128)S(1)} %add.32), channel_id=1, source_target_pairs={{0,1},{8,9},{16,17},{24,25},{32,33},{40,41},{48,49},{56,57},{4,5},... | collective-permute-start | bytes 98312 | tf_op jit(solution)/shard_map/ppermute | solution.py:413
  60.3 2.0 %collective-permute-start.9 = (f32[64,128]{1,0:T(8,128)S(1)}, f32[64,128]{1,0:T(8,128)}, u32[]{:S(2)}, u32[]{:S(2)}) collective-permute-start(f32[64,128]{1,0:T(8,128)S(1)} %add.32), channel_id=1, source_target_pairs={{0,3},{8,11},{16,19},{24,27},{32,35},{40,43},{48,51},{56,59},{4,7}... | collective-permute-start | bytes 98312 | tf_op jit(solution)/shard_map/ppermute | solution.py:413
  62.4 1.6 %concatenate.9.cat_ref = bf16[64,896]{1,0:T(8,128)(2,1)} concatenate(bf16[64,192]{1,0:T(8,128)(2,1)} %param.25, bf16[64,144]{1,0:T(8,128)(2,1)} %param.26, bf16[64,192]{1,0:T(8,128)(2,1)} %param.32, bf16[64,288]{1,0:T(8,128)(2,1)S(1)} %copy-done.18, bf16[64,80]{1,0:T(8,128)(2,1)S(1)} %broadcast_in_dim.4), dimensions={1} | concatenate | bytes 229376 | tf_op jit(solution)/shard_map/concatenate | solution.py:440
  64.6 1.4 %add_add_fusion.1 = f32[64,128]{1,0:T(8,128)} fusion(f32[64,128]{1,0:T(8,128)} %collective-permute-done.8, f32[64,128]{1,0:T(8,128)} %collective-permute-done.9, f32[64,128]{1,0:T(8,128)S(1)} %add.32, f32[64,128]{1,0:T(8,128)S(1)} %collective-permute-done.7), kind=kLoop, calls=%fused_computation.2 | loop fusion | flops 24576 | bytes 163840 | tf_op jit(solution)/shard_map/add | solution.py:414
  66.0 6.8 %collective-permute-start.10 = (f32[64,128]{1,0:T(8,128)}, f32[64,128]{1,0:T(8,128)}, u32[]{:S(2)}, u32[]{:S(2)}) collective-permute-start(f32[64,128]{1,0:T(8,128)} %add_add_fusion.1), channel_id=1, source_target_pairs={{0,64},{8,72},{16,80},{24,88},{32,96},{40,104},{48,112},{56,120},{... | collective-permute-start | bytes 98312 | tf_op jit(solution)/shard_map/ppermute | solution.py:413
  73.2 2.9 %collective-permute-start.12 = (f32[64,128]{1,0:T(8,128)}, f32[64,128]{1,0:T(8,128)}, u32[]{:S(2)}, u32[]{:S(2)}) collective-permute-start(f32[64,128]{1,0:T(8,128)} %add_add_fusion.1), channel_id=1, source_target_pairs={{0,68},{8,76},{16,84},{24,92},{32,100},{40,108},{48,116},{56,124},... | collective-permute-start | bytes 98312 | tf_op jit(solution)/shard_map/ppermute | solution.py:413
  76.1 0.9 copy-done.8
  77.0 0.9 copy-done.11
  77.9 0.9 copy-done.13
  78.8 7.1 %attention_parts.1 = (f32[64,16,128]{2,1,0:T(8,128)S(1)}, f32[64,16,128]{2,1,0:T(8,128)S(1)}, bf16[64,16,128]{2,1,0:T(8,128)(2,1)S(1)}, f32[24,128]{1,0:T(8,128)S(1)}) custom-call(bf16[64,128,128]{2,1,0:T(8,128)(2,1)S(1)} %copy-done.1, bf16[64,896]{1,0:T(8,128)(2,1)S(1)} %copy-done.8, bf16[64,896]{1,0:T(8,128)(2,1)S(1)} %copy-done.13, ...), custom_call_target="tpu_custom_call" | custom-call | flops 1000000000 | bytes 4000000 | tf_op jit(solution)/shard_map/attention_parts/pallas_call | solution.py:249
  85.9 0.8 copy-done.2
  86.7 0.8 copy-done.4
  88.2 5.7 %all-to-all-start = ((f32[8,24,128]{2,1,0:T(8,128)}), f32[8,24,128]{2,1,0:T(8,128)S(1)}, u32[]{:S(2)}, u32[]{:S(2)}) async-start(f32[8,24,128]{2,1,0:T(8,128)} %broadcast_in_dim.5), calls=%async_computation | async-start | bytes 196608 | tf_op jit(solution)/shard_map/all_to_all | solution.py:453
  93.8 0.8 add_add_fusion
  94.7 4.5 %collective-permute-start.13 = (f32[64,128]{1,0:T(8,128)S(1)}, f32[64,128]{1,0:T(8,128)S(1)}, u32[]{:S(2)}, u32[]{:S(2)}) collective-permute-start(f32[64,128]{1,0:T(8,128)S(1)} %add_add_fusion), channel_id=1, source_target_pairs={{0,32},{8,40},{16,48},{24,56},{32,0},{40,8},{48,16},{56,24},{4,36}... | collective-permute-start | bytes 98312 | tf_op jit(solution)/shard_map/ppermute | solution.py:413
  99.1 3.2 %collective-permute-start.15 = (f32[64,128]{1,0:T(8,128)S(1)}, f32[64,128]{1,0:T(8,128)S(1)}, u32[]{:S(2)}, u32[]{:S(2)}) collective-permute-start(f32[64,128]{1,0:T(8,128)S(1)} %add_add_fusion), channel_id=1, source_target_pairs={{0,48},{8,56},{16,0},{24,8},{32,16},{40,24},{48,32},{56,40},{4,52}... | collective-permute-start | bytes 98312 | tf_op jit(solution)/shard_map/ppermute | solution.py:413
  102.4 1.0 copy-done.3
  103.4 1.0 copy-done.5
  104.5 4.7 %pair_gradient.1 = bf16[64,128,128]{2,1,0:T(8,128)(2,1)} custom-call(f32[64,16,128]{2,1,0:T(8,128)S(1)} %copy-done.3, f32[64,16,128]{2,1,0:T(8,128)S(1)} %copy-done.5, f32[8,24,128]{2,1,0:T(8,128)S(1)} %all-to-all-done.stats_ref, bf16[64,64,128]{2,1,0:T(8,128)(2,1)S(1)} %get-tuple-element.17.bins_ref, bf16[64,16,128]{2,1,0:T(8,128)(2,1)S(1)} %get-tuple-element.18.cot_ref, ...), custom_call_target="tpu_custom_call" | custom-call | flops 300000000 | bytes 5000000 | tf_op jit(solution)/shard_map/pair_gradient/pallas_call | solution.py:390
  (65 shorter events, 4.8 us)
Async XLA Ops:
  0.6 40.7 %copy-start.7 = (s32[64,128]{1,0:T(8,128)S(1)}, s32[64,128]{1,0:T(8,128)}, u32[]{:S(2)}) copy-start(s32[64,128]{1,0:T(8,128)} %labels_ref.3) | copy-start | bytes 98308
  0.6 40.7 %copy-start.9 = (s32[1024]{0:T(1024)S(1)}, s32[1024]{0:T(1024)}, u32[]{:S(2)}) copy-start(s32[1024]{0:T(1024)} %mask_smem.1) | copy-start | bytes 12292
  0.7 40.7 %copy-start.10 = (f32[64]{0:T(128)S(1)}, f32[64]{0:T(128)}, u32[]{:S(2)}) copy-start(f32[64]{0:T(128)} %param.23) | copy-start | bytes 772
  10.9 11.3 %collective-permute-start.2 = (s16[33,64,128]{2,1,0:T(8,128)(2,1)S(1)}, s16[33,64,128]{2,1,0:T(8,128)(2,1)S(1)}, u32[]{:S(2)}, u32[]{:S(2)}) collective-permute-start(s16[33,64,128]{2,1,0:T(8,128)(2,1)S(1)} %get-tuple-element.15), channel_id=1, source_target_pairs={{0,32},{8,8},{16,16},{24,56},{32,0},{40,40},{48,48},{56,24},{4,36}... | collective-permute-start | bytes 1622024 | tf_op jit(solution)/shard_map/ppermute | solution.py:445
  14.8 13.2 %collective-permute-start.4 = (s16[33,64,128]{2,1,0:T(8,128)(2,1)S(1)}, s16[33,64,128]{2,1,0:T(8,128)(2,1)S(1)}, u32[]{:S(2)}, u32[]{:S(2)}) collective-permute-start(s16[33,64,128]{2,1,0:T(8,128)(2,1)S(1)} %get-tuple-element.16), channel_id=1, source_target_pairs={{0,32},{8,8},{16,16},{24,56},{32,0},{40,40},{48,48},{56,24},{4,36}... | collective-permute-start | bytes 1622024 | tf_op jit(solution)/shard_map/ppermute | solution.py:446
  22.2 12.1 %collective-permute-start.3 = (s16[33,64,128]{2,1,0:T(8,128)(2,1)S(1)}, s16[33,64,128]{2,1,0:T(8,128)(2,1)S(1)}, u32[]{:S(2)}, u32[]{:S(2)}) collective-permute-start(s16[33,64,128]{2,1,0:T(8,128)(2,1)S(1)} %collective-permute-done.2), channel_id=1, source_target_pairs={{32,0},{8,8},{16,1},{56,9},{0,2},{40,10},{48,3},{24,11},{36,64},{7... | collective-permute-start | bytes 1622024 | tf_op jit(solution)/shard_map/ppermute | solution.py:447
  28.0 13.4 %collective-permute-start.5 = (s16[33,64,128]{2,1,0:T(8,128)(2,1)S(1)}, s16[33,64,128]{2,1,0:T(8,128)(2,1)S(1)}, u32[]{:S(2)}, u32[]{:S(2)}) collective-permute-start(s16[33,64,128]{2,1,0:T(8,128)(2,1)S(1)} %collective-permute-done.4), channel_id=1, source_target_pairs={{32,8},{8,0},{16,9},{56,1},{0,10},{40,2},{48,11},{24,3},{36,72},{7... | collective-permute-start | bytes 1622024 | tf_op jit(solution)/shard_map/ppermute | solution.py:448
  41.4 7.7 %copy-start.17 = (bf16[64,288]{1,0:T(8,128)(2,1)S(1)}, bf16[64,288]{1,0:T(8,128)(2,1)}, u32[]{:S(2)}) copy-start(bf16[64,288]{1,0:T(8,128)(2,1)} %param.30) | copy-start | bytes 110596
  41.4 7.7 %copy-start.19 = (bf16[64,192]{1,0:T(8,128)(2,1)S(1)}, bf16[64,192]{1,0:T(8,128)(2,1)}, u32[]{:S(2)}) copy-start(bf16[64,192]{1,0:T(8,128)(2,1)} %param.27) | copy-start | bytes 73732
  41.4 7.7 %copy-start.20 = (bf16[64,144]{1,0:T(8,128)(2,1)S(1)}, bf16[64,144]{1,0:T(8,128)(2,1)}, u32[]{:S(2)}) copy-start(bf16[64,144]{1,0:T(8,128)(2,1)} %param.28) | copy-start | bytes 55300
  41.4 7.6 %copy-start.21 = (bf16[64,192]{1,0:T(8,128)(2,1)S(1)}, bf16[64,192]{1,0:T(8,128)(2,1)}, u32[]{:S(2)}) copy-start(bf16[64,192]{1,0:T(8,128)(2,1)} %param.29) | copy-start | bytes 73732
  41.4 20.9 %copy-start.23 = (f32[12]{0:T(128)S(1)}, f32[12]{0:T(128)}, u32[]{:S(2)}) copy-start(f32[12]{0:T(128)} %param.31) | copy-start | bytes 148
  41.4 20.9 %copy-start.22 = (bf16[128,12]{0,1:T(8,128)(2,1)S(1)}, bf16[128,12]{0,1:T(8,128)(2,1)}, u32[]{:S(2)}) copy-start(bf16[128,12]{0,1:T(8,128)(2,1)} %param.24) | copy-start | bytes 9220
  41.4 21.0 %copy-start.18 = (bf16[64,288]{1,0:T(8,128)(2,1)S(1)}, bf16[64,288]{1,0:T(8,128)(2,1)}, u32[]{:S(2)}) copy-start(bf16[64,288]{1,0:T(8,128)(2,1)} %param.33) | copy-start | bytes 110596
  41.4 34.6 %copy-start.1 = (bf16[64,128,128]{2,1,0:T(8,128)(2,1)S(1)}, bf16[64,128,128]{2,1,0:T(8,128)(2,1)}, u32[]{:S(2)}) copy-start(bf16[64,128,128]{2,1,0:T(8,128)(2,1)} %pair_ref.5) | copy-start | bytes 6291460
  41.4 34.6 %copy-start.14 = (f32[16,640]{1,0:T(8,128)S(1)}, f32[16,640]{1,0:T(8,128)}, u32[]{:S(2)}) copy-start(f32[16,640]{1,0:T(8,128)} %constant.12.clone.value_mask_ref) | copy-start | bytes 122884
  41.5 34.6 %copy-start.15 = (f32[16,256]{1,0:T(8,128)S(1)}, f32[16,256]{1,0:T(8,128)}, u32[]{:S(2)}) copy-start(f32[16,256]{1,0:T(8,128)} %constant.10.clone.scalar_mask_ref) | copy-start | bytes 49156
  41.5 34.6 %copy-start.16 = (f32[16,256]{1,0:T(8,128)S(1)}, f32[16,256]{1,0:T(8,128)}, u32[]{:S(2)}) copy-start(f32[16,256]{1,0:T(8,128)} %constant.11.clone.point_mask_ref) | copy-start | bytes 49156
  48.9 4.2 %collective-permute-start.6 = (f32[64,128]{1,0:T(8,128)S(1)}, f32[64,128]{1,0:T(8,128)S(1)}, u32[]{:S(2)}, u32[]{:S(2)}) collective-permute-start(f32[64,128]{1,0:T(8,128)S(1)} %get-tuple-element.19), channel_id=1, source_target_pairs={{0,8},{8,0},{16,24},{24,16},{32,40},{40,32},{48,56},{56,48},{4,12}... | collective-permute-start | bytes 98312 | tf_op jit(solution)/shard_map/ppermute | solution.py:411
  49.8 14.2 %collective-permute-start = (bf16[64,896]{1,0:T(8,128)(2,1)}, bf16[64,896]{1,0:T(8,128)(2,1)S(1)}, u32[]{:S(2)}, u32[]{:S(2)}) collective-permute-start(bf16[64,896]{1,0:T(8,128)(2,1)} %concatenate.10), channel_id=1, source_target_pairs={{0,0},{8,8},{16,1},{24,9},{32,2},{40,10},{48,3},{56,11},{4,64},{12... | collective-permute-start | bytes 344072 | tf_op jit(solution)/shard_map/ppermute | solution.py:438
  53.1 10.9 %collective-permute-start.7 = (f32[64,128]{1,0:T(8,128)S(1)}, f32[64,128]{1,0:T(8,128)S(1)}, u32[]{:S(2)}, u32[]{:S(2)}) collective-permute-start(f32[64,128]{1,0:T(8,128)S(1)} %add.32), channel_id=1, source_target_pairs={{0,2},{8,10},{16,18},{24,26},{32,34},{40,42},{48,50},{56,58},{4,6}... | collective-permute-start | bytes 98312 | tf_op jit(solution)/shard_map/ppermute | solution.py:413
  58.6 6.0 %collective-permute-start.8 = (f32[64,128]{1,0:T(8,128)S(1)}, f32[64,128]{1,0:T(8,128)}, u32[]{:S(2)}, u32[]{:S(2)}) collective-permute-start(f32[64,128]{1,0:T(8,128)S(1)} %add.32), channel_id=1, source_target_pairs={{0,1},{8,9},{16,17},{24,25},{32,33},{40,41},{48,49},{56,57},{4,5},... | collective-permute-start | bytes 98312 | tf_op jit(solution)/shard_map/ppermute | solution.py:413
  60.3 4.3 %collective-permute-start.9 = (f32[64,128]{1,0:T(8,128)S(1)}, f32[64,128]{1,0:T(8,128)}, u32[]{:S(2)}, u32[]{:S(2)}) collective-permute-start(f32[64,128]{1,0:T(8,128)S(1)} %add.32), channel_id=1, source_target_pairs={{0,3},{8,11},{16,19},{24,27},{32,35},{40,43},{48,51},{56,59},{4,7}... | collective-permute-start | bytes 98312 | tf_op jit(solution)/shard_map/ppermute | solution.py:413
  64.0 12.1 %copy-start.12 = (bf16[64,896]{1,0:T(8,128)(2,1)}, bf16[64,896]{1,0:T(8,128)(2,1)S(1)}, u32[]{:S(2)}) copy-start(bf16[64,896]{1,0:T(8,128)(2,1)S(1)} %collective-permute-done.near_ref) | copy-start | bytes 344068
  64.0 12.1 %collective-permute-start.1 = (bf16[64,896]{1,0:T(8,128)(2,1)S(1)}, bf16[64,896]{1,0:T(8,128)(2,1)S(1)}, u32[]{:S(2)}, u32[]{:S(2)}) collective-permute-start(bf16[64,896]{1,0:T(8,128)(2,1)S(1)} %collective-permute-done.near_ref), channel_id=1, source_target_pairs={{0,8},{8,0},{16,24},{24,16},{32,40},{40,32},{48,56},{56,48},{4,12}... | collective-permute-start | bytes 344072 | tf_op jit(solution)/shard_map/ppermute | solution.py:439
  66.0 27.8 %collective-permute-start.10 = (f32[64,128]{1,0:T(8,128)}, f32[64,128]{1,0:T(8,128)}, u32[]{:S(2)}, u32[]{:S(2)}) collective-permute-start(f32[64,128]{1,0:T(8,128)} %add_add_fusion.1), channel_id=1, source_target_pairs={{0,64},{8,72},{16,80},{24,88},{32,96},{40,104},{48,112},{56,120},{... | collective-permute-start | bytes 98312 | tf_op jit(solution)/shard_map/ppermute | solution.py:413
  72.8 21.0 %collective-permute-start.11 = (f32[64,128]{1,0:T(8,128)}, f32[64,128]{1,0:T(8,128)}, u32[]{:S(2)}, u32[]{:S(2)}) collective-permute-start(f32[64,128]{1,0:T(8,128)} %add_add_fusion.1), channel_id=1, source_target_pairs={{0,4},{8,12},{16,20},{24,28},{32,36},{40,44},{48,52},{56,60},{4,64... | collective-permute-start | bytes 98312 | tf_op jit(solution)/shard_map/ppermute | solution.py:413
  73.2 20.7 %collective-permute-start.12 = (f32[64,128]{1,0:T(8,128)}, f32[64,128]{1,0:T(8,128)}, u32[]{:S(2)}, u32[]{:S(2)}) collective-permute-start(f32[64,128]{1,0:T(8,128)} %add_add_fusion.1), channel_id=1, source_target_pairs={{0,68},{8,76},{16,84},{24,92},{32,100},{40,108},{48,116},{56,124},... | collective-permute-start | bytes 98312 | tf_op jit(solution)/shard_map/ppermute | solution.py:413
  88.2 14.2 %all-to-all-start = ((f32[8,24,128]{2,1,0:T(8,128)}), f32[8,24,128]{2,1,0:T(8,128)S(1)}, u32[]{:S(2)}, u32[]{:S(2)}) async-start(f32[8,24,128]{2,1,0:T(8,128)} %broadcast_in_dim.5), calls=%async_computation | async-start | bytes 196608 | tf_op jit(solution)/shard_map/all_to_all | solution.py:453
  94.7 14.5 %collective-permute-start.13 = (f32[64,128]{1,0:T(8,128)S(1)}, f32[64,128]{1,0:T(8,128)S(1)}, u32[]{:S(2)}, u32[]{:S(2)}) collective-permute-start(f32[64,128]{1,0:T(8,128)S(1)} %add_add_fusion), channel_id=1, source_target_pairs={{0,32},{8,40},{16,48},{24,56},{32,0},{40,8},{48,16},{56,24},{4,36}... | collective-permute-start | bytes 98312 | tf_op jit(solution)/shard_map/ppermute | solution.py:413
  99.1 10.0 %collective-permute-start.14 = (f32[64,128]{1,0:T(8,128)S(1)}, f32[64,128]{1,0:T(8,128)S(1)}, u32[]{:S(2)}, u32[]{:S(2)}) collective-permute-start(f32[64,128]{1,0:T(8,128)S(1)} %add_add_fusion), channel_id=1, source_target_pairs={{0,16},{8,24},{16,32},{24,40},{32,48},{40,56},{48,0},{56,8},{4,20}... | collective-permute-start | bytes 98312 | tf_op jit(solution)/shard_map/ppermute | solution.py:413
  99.1 10.0 %collective-permute-start.15 = (f32[64,128]{1,0:T(8,128)S(1)}, f32[64,128]{1,0:T(8,128)S(1)}, u32[]{:S(2)}, u32[]{:S(2)}) collective-permute-start(f32[64,128]{1,0:T(8,128)S(1)} %add_add_fusion), channel_id=1, source_target_pairs={{0,48},{8,56},{16,0},{24,8},{32,16},{40,24},{48,32},{56,40},{4,52}... | collective-permute-start | bytes 98312 | tf_op jit(solution)/shard_map/ppermute | solution.py:413
  (9 other events, 8.8 us)

commit v2 on v1

v2 whole, which is shorter than its diff:
```python
import functools
import math

import jax
import jax.numpy as jnp
import numpy as np
from jax import lax
from jax.experimental import pallas as pl
from jax.experimental.pallas import tpu as pltpu
from jax.sharding import PartitionSpec as P

AXES = ("row", "col")
LOGIT_WEIGHT = math.sqrt(1.0 / 3.0)
HEADS = 12
PAD_HEADS = 16
CHUNK = 8
QUANT = 32760.0

WIDTHS = (192, 144, 192, 288)
PER_HEAD = (16, 12, 16, 24)
CAT = 896
WINDOWS = ((0, 256), (128, 384), (256, 896))

NT = (((1,), (1,)), ((), ()))
TN = (((0,), (0,)), ((), ()))

CHIPS = [(x, y, z) for x in range(4) for y in range(4) for z in range(4)]
Y_SWAP = (0, 2, 1, 3)


def device_index(chip, core):
    x, y, z = chip
    return ((y // 2) * 8 + z * 2 + core) * 8 + (y % 2) * 4 + x


def mirror_chip(chip):
    x, y, z = chip
    return (z, Y_SWAP[y], x)


def halfway_chip(chip, core):
    x, y, z = chip
    if core == 0:
        return (x, y, (x + z) % 4)
    return ((x + 3 * z + 2) % 4, Y_SWAP[y], x)


FIRST_HOP = [(device_index(n, h), device_index(halfway_chip(n, h), h)) for n in CHIPS for h in (0, 1)]
SECOND_HOP = [
    [
        (device_index(halfway_chip(n, h), h), device_index(mirror_chip(n), (h + s) % 2))
        for n in CHIPS
        for h in (0, 1)
    ]
    for s in (0, 1)
]
MIRROR = [(device_index(n, h), device_index(mirror_chip(n), h)) for n in CHIPS for h in (0, 1)]
CORE_SWAP = [(device_index(n, h), device_index(n, 1 - h)) for n in CHIPS for h in (0, 1)]


Y_PAIR = [(device_index((x, y, z), h), device_index((x, y ^ 1, z), h)) for x, y, z in CHIPS for h in (0, 1)]


def shift_map(axis, distance):
    pairs = []
    for n in CHIPS:
        m = list(n)
        m[axis] = (m[axis] + distance) % 4
        pairs += [(device_index(n, h), device_index(tuple(m), h)) for h in (0, 1)]
    return pairs


def head_masks():
    masks = np.zeros((3, PAD_HEADS, CAT), np.float32)
    start = 0
    for part, (width, size) in enumerate(zip(WIDTHS, PER_HEAD)):
        for column in range(width):
            masks[min(part, 2), column // size, start + column] = 1.0
        start += width
    return [masks[k][:, lo:hi] for k, (lo, hi) in enumerate(WINDOWS)]


def dot(a, b, dims=(((1,), (0,)), ((), ()))):
    return lax.dot_general(a, b, dims, preferred_element_type=jnp.float32)


def eye(n, dtype):
    return (
        lax.broadcasted_iota(jnp.int32, (n, n), 0) == lax.broadcasted_iota(jnp.int32, (n, n), 1)
    ).astype(dtype)


def padded_heads(bias_ref):
    heads = bias_ref.shape[0]
    pick = (
        lax.broadcasted_iota(jnp.int32, (PAD_HEADS, heads), 0)
        == lax.broadcasted_iota(jnp.int32, (PAD_HEADS, heads), 1)
    ).astype(jnp.bfloat16)
    return dot(pick, bias_ref[...]).astype(jnp.bfloat16)


def own_core():
    return lax.rem(lax.axis_index("row"), 2)


def lay_out(cat_ref, parts):
    start = 0
    for part in parts:
        width = part.shape[1]
        cat_ref[:, start : start + width] = part[...]
        start += width
    cat_ref[:, start:] = jnp.zeros((cat_ref.shape[0], cat_ref.shape[1] - start), cat_ref.dtype)


def chunk_copies(source, target, arrived):
    count = arrived.shape[0]
    size = source.shape[0] // count
    return [
        pltpu.make_async_copy(
            source.at[pl.ds(k * size, size)], target.at[pl.ds(k * size, size)], arrived.at[k]
        )
        for k in range(count)
    ]


HBM = pl.BlockSpec(memory_space=pltpu.HBM)
VMEM = pl.BlockSpec(memory_space=pltpu.VMEM)
SMEM = pl.BlockSpec(memory_space=pltpu.SMEM)
PARAMS = pltpu.CompilerParams(vmem_limit_bytes=16 * 1024 * 1024)


def logits_kernel(
    pair_hbm, weight_hbm, labels_hbm, own_hbm, same_ref, other_ref, pair_ref, weight_ref, labels_ref, own_ref, slabs,
    top, pair_sem, own_sem, small_sem,
):
    small = [
        pltpu.make_async_copy(weight_hbm, weight_ref, small_sem.at[0]),
        pltpu.make_async_copy(labels_hbm, labels_ref, small_sem.at[1]),
    ]
    coming = chunk_copies(pair_hbm, pair_ref, pair_sem)
    going = chunk_copies(own_ref, own_hbm, own_sem)
    small[0].start()
    coming[0].start()
    for copy in coming[1:] + small[1:]:
        copy.start()
    small[0].wait()
    weight_t = weight_ref[...]
    size = pair_ref.shape[0] // len(coming)
    for k in range(len(coming)):
        coming[k].wait()
        for first in range(k * size, (k + 1) * size, 4):
            flat = pair_ref[first : first + 4].reshape(4 * 128, 128)
            terms = dot(weight_t, flat, NT)
            for t in range(4):
                term = terms[:, t * 128 : (t + 1) * 128]
                row = first + t
                own_ref[row] = term
                slabs[pl.ds(row, 64, stride=64), :] = term
                top[pl.ds(row, 1), :] = jnp.max(jnp.abs(term), axis=0, keepdims=True)
        going[k].start()
    small[1].wait()

    core = own_core()
    level = jnp.ceil(16.0 * jnp.log2(jnp.maximum(top[...], 1e-30)))
    scale = jnp.exp2(level * (-1.0 / 16.0)) * QUANT

    def narrow(values):
        return jnp.clip(jnp.round(values), -32767.0, 32767.0).astype(jnp.int32).astype(jnp.int16)

    def put(slab, upper, lower):
        turned = jnp.transpose(jnp.concatenate([upper, lower], axis=0))
        first, second = turned[:64], turned[64:]
        same_ref[slab] = narrow(jnp.where(core == 0, first, second))
        other_ref[slab] = narrow(jnp.where(core == 0, second, first))

    def pair_of_bins(b, carry):
        upper = slabs[pl.ds(pl.multiple_of(b * 64, 64), 64), :] * scale
        lower = slabs[pl.ds(pl.multiple_of((b + 32) * 64, 64), 64), :] * scale
        put(b, upper, lower)
        return carry

    lax.fori_loop(0, 32, pair_of_bins, 0, unroll=8)
    put(32, level, labels_ref[...].astype(jnp.float32))
    for copy in going:
        copy.wait()


def own_logits(pair_tile, weight_rows, labels):
    rows = pair_tile.shape[0]
    block = jax.ShapeDtypeStruct((33, 64, 128), jnp.int16)
    return pl.pallas_call(
        logits_kernel,
        in_specs=[HBM] * 3,
        out_specs=[HBM, VMEM, VMEM],
        out_shape=[
            jax.ShapeDtypeStruct((rows, 64, 128), jnp.float32),
            block,
            block,
        ],
        scratch_shapes=[
            pltpu.VMEM(pair_tile.shape, jnp.bfloat16),
            pltpu.VMEM(weight_rows.shape, jnp.bfloat16),
            pltpu.VMEM(labels.shape, jnp.int32),
            pltpu.VMEM((rows, 64, 128), jnp.float32),
            pltpu.VMEM((64 * 64, 128), jnp.float32),
            pltpu.VMEM((64, 128), jnp.float32),
            pltpu.SemaphoreType.DMA((8,)),
            pltpu.SemaphoreType.DMA((8,)),
            pltpu.SemaphoreType.DMA((2,)),
        ],
        compiler_params=pltpu.CompilerParams(vmem_limit_bytes=60 * 1024 * 1024),
        cost_estimate=pl.CostEstimate(flops=200_000_000, bytes_accessed=6_000_000, transcendentals=8192),
        name="own_logits",
    )(pair_tile, weight_rows, labels)


def attention_kernel(point_smem, pair_ref, near_ref, far_ref, cot_ref, bias_ref, mask_ref, *refs):
    scalar_mask_ref, point_mask_ref, value_mask_ref = refs[:3]
    query_refs = refs[3:7]
    exp_ref, grad_ref, cot_out_ref, stats_ref, keys, cot_rows, cat_ref = refs[7:]
    length = CHUNK * PAD_HEADS

    def iota(shape, dim):
        return lax.broadcasted_iota(jnp.int32, shape, dim)

    core = own_core()
    near, far = near_ref[...].astype(jnp.float32), far_ref[...].astype(jnp.float32)
    keys[:64] = jnp.where(core == 0, near, far).astype(jnp.bfloat16)
    keys[64:] = jnp.where(core == 0, far, near).astype(jnp.bfloat16)
    lay_out(cat_ref, query_refs)
    for h in range(HEADS):
        cot_rows[h * 64 : (h + 1) * 64] = cot_ref[:, h * 128 : (h + 1) * 128]
    bias_t = padded_heads(bias_ref)

    right = [keys[:, lo:hi] for lo, hi in WINDOWS]
    key_points = right[1].astype(jnp.float32)
    key_sq = lax.dot_general(
        point_mask_ref[...],
        key_points * key_points,
        NT,
        precision=lax.Precision.HIGHEST,
        preferred_element_type=jnp.float32,
    )
    key_sq = jnp.concatenate([key_sq] * CHUNK, axis=0)
    head_masks = [
        jnp.concatenate([mask[...]] * CHUNK, axis=0) for mask in (scalar_mask_ref, point_mask_ref, value_mask_ref)
    ]

    head_of = iota((length, 128), 0) % PAD_HEADS
    raw = jnp.zeros((length, 128), jnp.float32)
    for h in range(HEADS):
        raw = jnp.where(head_of == h, point_smem[h], raw)
    softplus = jnp.maximum(raw, 0.0) + jnp.log1p(jnp.exp(-jnp.abs(raw)))
    point_scale = softplus * (math.sqrt(2.0 / 36.0) / 2.0)
    column_mask = mask_ref[pl.ds(lax.axis_index("col"), 1), :]
    key_bias = jnp.where(column_mask > 0, 0.0, -1000000000.0)
    lane = iota((length, 128), 1)

    for step in range(pair_ref.shape[0] // CHUNK):
        residue = step * CHUNK + iota((length, 64), 0) // PAD_HEADS
        pick = (residue == iota((length, 64), 1)).astype(jnp.bfloat16)
        spread = dot(pick, cat_ref[...])
        left = [spread[:, lo:hi] * mask for (lo, hi), mask in zip(WINDOWS, head_masks)]
        scalar_term, cross_term, value_term = [dot(a.astype(jnp.bfloat16), b, NT) for a, b in zip(left, right)]
        query_sq = jnp.sum(left[1] * left[1], axis=1, keepdims=True)

        row_of = iota((length, 768), 0)
        column_of = iota((length, 768), 1)
        cot_pick = (step * CHUNK + row_of // PAD_HEADS == column_of % 64) & (row_of % PAD_HEADS == column_of // 64)
        cot = dot(cot_pick.astype(jnp.bfloat16), cot_rows[...]).astype(jnp.bfloat16)
        rows = slice(step * CHUNK, (step + 1) * CHUNK)
        cot_out_ref[rows] = cot.reshape(CHUNK, PAD_HEADS, 128)

        pair_bias, pair_value = [], []
        for t in range(CHUNK):
            both = jnp.concatenate([bias_t, cot[t * PAD_HEADS : (t + 1) * PAD_HEADS]], axis=0)
            result = dot(both, pair_ref[step * CHUNK + t], NT)
            pair_bias.append(result[:PAD_HEADS])
            pair_value.append(result[PAD_HEADS:])
        pair_bias = jnp.concatenate(pair_bias, axis=0)
        value_grad = value_term + jnp.concatenate(pair_value, axis=0)

        logits = (
            LOGIT_WEIGHT
            * (scalar_term * 0.25 + pair_bias - point_scale * (query_sq + key_sq - 2.0 * cross_term))
            + key_bias
        )
        top = jnp.max(logits, axis=1, keepdims=True)
        weights = jnp.exp(logits - top)
        total = jnp.sum(weights, axis=1, keepdims=True)
        weighted = jnp.sum(weights * value_grad, axis=1, keepdims=True)
        exp_ref[rows] = weights.reshape(CHUNK, PAD_HEADS, 128)
        grad_ref[rows] = value_grad.reshape(CHUNK, PAD_HEADS, 128)
        packed = jnp.where(lane == 0, top, jnp.where(lane == 1, total, jnp.where(lane == 2, weighted, 0.0)))
        packed = jnp.transpose(packed)
        for q in range(3):
            stats_ref[q * 8 + step : q * 8 + step + 1, :] = packed[q : q + 1]


def attention_parts(pair_tile, queries, near, far, cot_pair, bias_rows, point_weight, mask_rows):
    rows = pair_tile.shape[0]
    masks = [jnp.asarray(m) for m in head_masks()]
    return pl.pallas_call(
        attention_kernel,
        in_specs=[SMEM] + [VMEM] * (6 + len(masks) + len(queries)),
        out_specs=[VMEM] * 4,
        out_shape=[
            jax.ShapeDtypeStruct((rows, PAD_HEADS, 128), jnp.float32),
            jax.ShapeDtypeStruct((rows, PAD_HEADS, 128), jnp.float32),
            jax.ShapeDtypeStruct((rows, PAD_HEADS, 128), jnp.bfloat16),
            jax.ShapeDtypeStruct((24, 128), jnp.float32),
        ],
        scratch_shapes=[
            pltpu.VMEM((128, CAT), jnp.bfloat16),
            pltpu.VMEM((768, 128), jnp.bfloat16),
            pltpu.VMEM((64, CAT), jnp.bfloat16),
        ],
        compiler_params=PARAMS,
        cost_estimate=pl.CostEstimate(flops=1_000_000_000, bytes_accessed=4_000_000, transcendentals=200_000),
        name="attention_parts",
    )(point_weight, pair_tile, near, far, cot_pair, bias_rows, mask_rows, *masks, *queries)


def bins_kernel(
    mask_smem, pair_ref, own_ref, labels_ref, near_ref, far_ref, bias_ref, mask_ref, bins_ref, weight_ref, mirror,
    mirror_labels,
):
    core = own_core()
    low_lanes = lax.broadcasted_iota(jnp.int32, (64, 128), 1) < 64

    def halves(slab):
        near = near_ref[slab].astype(jnp.int32).astype(jnp.float32)
        far = far_ref[slab].astype(jnp.int32).astype(jnp.float32)
        first = jnp.where(core == 0, near, far)
        second = jnp.where(core == 0, far, near)
        upper = jnp.where(low_lanes, first, pltpu.roll(second, 64, 1))
        lower = jnp.where(low_lanes, pltpu.roll(first, 64, 1), second)
        return upper, lower

    level, other_labels = halves(32)
    mirror_labels[...] = other_labels
    scale = jnp.exp2(level * (1.0 / 16.0)) * (1.0 / QUANT)

    def pair_of_bins(b, carry):
        upper, lower = halves(b)
        mirror[pl.ds(pl.multiple_of(b * 64, 64), 64), :] = upper * scale
        mirror[pl.ds(pl.multiple_of((b + 32) * 64, 64), 64), :] = lower * scale
        return carry

    lax.fori_loop(0, 32, pair_of_bins, 0, unroll=8)
    bias = jnp.sum(eye(64, jnp.float32) * bias_ref[...], axis=1, keepdims=True)
    bias = jnp.broadcast_to(bias, (64, 128))
    column_mask = mask_ref[pl.ds(lax.axis_index("col"), 1), :].astype(jnp.float32)
    bin_of = lax.broadcasted_iota(jnp.int32, (64, 128), 0)
    first_row = lax.axis_index("row") * 64

    total = jnp.zeros((64, 128), jnp.float32)
    for step in range(pair_ref.shape[0] // CHUNK):
        grads = []
        for t in range(CHUNK):
            row = step * CHUNK + t
            logits = own_ref[row] + mirror[pl.ds(row, 64, stride=64), :] + bias
            weights = jnp.exp(logits - jnp.max(logits, axis=0, keepdims=True))
            valid = column_mask * mask_smem[first_row + row].astype(jnp.float32)
            share = 2.0 * valid / jnp.sum(weights, axis=0, keepdims=True)
            own_label = labels_ref[pl.ds(row, 1), :]
            other_label = mirror_labels[pl.ds(row, 1), :].astype(jnp.int32)
            hits = jnp.where(bin_of == own_label, valid, 0.0) + jnp.where(bin_of == other_label, valid, 0.0)
            grad = (weights * share - hits).astype(jnp.bfloat16)
            bins_ref[row] = grad
            grads.append(grad)
        flat = pair_ref[step * CHUNK : (step + 1) * CHUNK].reshape(CHUNK * 128, 128)
        total += dot(jnp.concatenate(grads, axis=1), flat)
    weight_ref[...] = total


def bin_gradient(pair_tile, own, near, far, labels, dist_bias, mask_rows, residue_mask):
    rows = pair_tile.shape[0]
    return pl.pallas_call(
        bins_kernel,
        in_specs=[SMEM] + [VMEM] * 7,
        out_specs=[VMEM, VMEM],
        out_shape=[
            jax.ShapeDtypeStruct((rows, 64, 128), jnp.bfloat16),
            jax.ShapeDtypeStruct((64, 128), jnp.float32),
        ],
        scratch_shapes=[
            pltpu.VMEM((64 * 64, 128), jnp.float32),
            pltpu.VMEM((64, 128), jnp.float32),
        ],
        compiler_params=PARAMS,
        cost_estimate=pl.CostEstimate(flops=200_000_000, bytes_accessed=6_000_000, transcendentals=600_000),
        name="bin_gradient",
    )(residue_mask, pair_tile, own, labels, near, far, dist_bias, mask_rows)


def output_kernel(exp_ref, grad_ref, *refs):
    stats_refs, (bins_ref, cot_ref, weight_ref, bias_ref, out_hbm, out_ref, sent) = refs[:4], refs[4:]
    length = CHUNK * PAD_HEADS
    weight_t = weight_ref[...]
    bias_t = padded_heads(bias_ref)
    places = [(ref, y) for ref in stats_refs for y in (0, 1)]
    tops = [ref[y, 0:8, :] for ref, y in places]
    totals = [ref[y, 8:16, :] for ref, y in places]
    weighted = [ref[y, 16:24, :] for ref, y in places]
    top = functools.reduce(jnp.maximum, tops)
    factors = [jnp.exp(m - top) for m in tops]
    total = sum(f * s for f, s in zip(factors, totals))
    means = sum(f * s for f, s in zip(factors, weighted)) / total
    shares = factors[0] / total
    going = chunk_copies(out_ref, out_hbm, sent)
    for step in range(out_ref.shape[0] // CHUNK):
        share = jnp.transpose(jnp.broadcast_to(shares[step : step + 1], (length, 128)))
        mean = jnp.transpose(jnp.broadcast_to(means[step : step + 1], (length, 128)))
        rows = slice(step * CHUNK, (step + 1) * CHUNK)
        attention = exp_ref[rows].reshape(length, 128) * share
        logit_grad = attention * (grad_ref[rows].reshape(length, 128) - mean)
        attention = attention.astype(jnp.bfloat16)
        logit_grad = (logit_grad * LOGIT_WEIGHT).astype(jnp.bfloat16)
        for t in range(CHUNK):
            heads = slice(t * PAD_HEADS, (t + 1) * PAD_HEADS)
            row = step * CHUNK + t
            left = jnp.concatenate([bins_ref[row], attention[heads], logit_grad[heads]], axis=0)
            right = jnp.concatenate([weight_t, cot_ref[row], bias_t], axis=0)
            out_ref[row] = dot(left, right, TN).astype(jnp.bfloat16)
        going[step].start()
    for copy in going:
        copy.wait()


def pair_gradient(weights, value_grad, stats, bins, cot, weight_rows, bias_rows):
    rows = bins.shape[0]
    return pl.pallas_call(
        output_kernel,
        in_specs=[VMEM] * 10,
        out_specs=HBM,
        out_shape=jax.ShapeDtypeStruct((rows, 128, 128), jnp.bfloat16),
        scratch_shapes=[
            pltpu.VMEM((rows, 128, 128), jnp.bfloat16),
            pltpu.SemaphoreType.DMA((rows // CHUNK,)),
        ],
        compiler_params=PARAMS,
        cost_estimate=pl.CostEstimate(flops=300_000_000, bytes_accessed=5_000_000, transcendentals=10_000),
        name="pair_gradient",
    )(weights, value_grad, *stats, bins, cot, weight_rows, bias_rows)


def sum_over_devices(term):
    term = term + lax.ppermute(term, AXES, CORE_SWAP)
    for axis in range(3):
        one, two, three = [lax.ppermute(term, AXES, shift_map(axis, d)) for d in (1, 2, 3)]
        term = (term + two) + (one + three)
    return term


def body(
    pair_rep,
    labels,
    residue_mask,
    dist_weight,
    dist_bias,
    bias_weight,
    query_scalar,
    query_points,
    key_scalar,
    key_points,
    value_scalar,
    value_points,
    point_weight,
    cot_scalar,
    cot_points,
    cot_pair,
):
    mask_rows = residue_mask.reshape(8, 128)
    weight_rows = jnp.transpose(dist_weight)
    bias_rows = jnp.transpose(bias_weight)

    pad = jnp.zeros((query_scalar.shape[0], CAT - sum(WIDTHS)), jnp.bfloat16)
    own_keys = jnp.concatenate([key_scalar, key_points, value_scalar, value_points, pad], axis=1)
    near_keys = lax.ppermute(own_keys, AXES, MIRROR)
    own, same, other = own_logits(pair_rep, weight_rows, labels)
    same, other, near_keys = lax.optimization_barrier((same, other, near_keys))
    same = lax.ppermute(same, AXES, FIRST_HOP)
    other = lax.ppermute(other, AXES, FIRST_HOP)
    far_keys = lax.ppermute(near_keys, AXES, CORE_SWAP)
    weights, value_grad, cot, stats = attention_parts(
        pair_rep,
        (query_scalar, query_points, cot_scalar, cot_points),
        near_keys,
        far_keys,
        cot_pair,
        bias_rows,
        point_weight,
        mask_rows,
    )
    same, other, stats = lax.optimization_barrier((same, other, stats))
    same = lax.ppermute(same, AXES, SECOND_HOP[0])
    other = lax.ppermute(other, AXES, SECOND_HOP[1])
    two_stats = jnp.stack([stats, lax.ppermute(stats, AXES, Y_PAIR)])
    stats = [two_stats] + [lax.ppermute(two_stats, AXES, shift_map(0, d)) for d in (1, 2, 3)]
    same, other, stats = lax.optimization_barrier((same, other, stats))
    bins, weight_term = bin_gradient(
        pair_rep, own, same, other, labels, dist_bias.reshape(1, 64), mask_rows, residue_mask
    )
    weight_grad = jnp.transpose(sum_over_devices(weight_term))
    pair_grad = pair_gradient(weights, value_grad, stats, bins, cot, weight_rows, bias_rows)
    return (pair_grad, weight_grad)


def solution(mesh):
    placed = (
        P("row", "col", None),
        P("row", "col"),
        P(),
        P(),
        P(),
        P(),
        P("row", None),
        P("row", None),
        P("row", None),
        P("row", None),
        P("row", None),
        P("row", None),
        P(),
        P("row", None),
        P("row", None),
        P("row", None),
    )
    return jax.shard_map(
        body, mesh=mesh, in_specs=placed, out_specs=(P("row", "col", None), P()), check_vma=False
    )
```

time: 111 us -> 87.3 us (0.79)
  local copies, waits for them, and re-layouts: 12.8 us -> 3.4 us
  waiting for transfers between devices: 20.7 us -> 12.3 us
  Pallas kernels: 26.2 us -> 17.9 us
  starting transfers between devices: 46.3 us -> 50.6 us
  other arithmetic: 2.85 us -> 0.65 us
    ppermute x0 -> x4, starting transfers between devices: none -> 13 us  [the longest x3 8.33 us: body(): lax.ppermute(two_stats, AXES, shift_map(0, d))]
    ppermute x9, starting transfers between devices: 26.9 us -> 17 us  [sum_over_devices(): lax.ppermute(term, AXES, shift_map(axis, d))]
    pallas_call x4, Pallas kernels: 26.2 us -> 17.9 us  [the longest x1 5.92 us: own_logits(): pl.pallas_call(logits_kernel, in_specs=[HBM] * 3, out_specs=[HBM, VMEM, V...]
    unnamed x50 -> x32, local copies, waits for them, and re-layouts: 9.82 us -> 2.27 us
    ppermute x1, waiting for transfers between devices: 7.02 us -> 0.01 us  [body(): other = lax.ppermute(other, AXES, SECOND_HOP[1])]
    ppermute x9, waiting for transfers between devices: 0.62 us -> 6.84 us  [sum_over_devices(): lax.ppermute(term, AXES, shift_map(axis, d))]
    all_to_all x1 -> x0, starting transfers between devices: 5.67 us -> none  [body(): lax.all_to_all(jnp.broadcast_to(stats[None], (8,) + stats.shape), 'col',...]
    ppermute x1, waiting for transfers between devices: 5.66 us -> 0.01 us  [body(): same = lax.ppermute(same, AXES, SECOND_HOP[0])]
  transfers between devices with their start and end apart: 17 -> 20, of which waited for: 5 -> 9; matrix products, arithmetic and copies ran while one was open for 5% -> 0% of each run, Pallas kernels for 11% -> 16%
where the time goes in v2:
time: 87.3 us; the launch traced here: 85.7 us
  starting transfers between devices  50.6 us (58%)
  Pallas kernels  17.9 us (21%)
  waiting for transfers between devices  12.3 us (14%)
  local copies, waits for them, and re-layouts  3.4 us (4%)
  between operations  0.94 us (1%)
    ppermute x9, starting transfers between devices, sum_over_devices(): lax.ppermute(term, AXES, shift_map(axis, d))  17 us
    ppermute x3, starting transfers between devices, body(): lax.ppermute(two_stats, AXES, shift_map(0, d))  8.33 us
    ppermute x9, waiting for transfers between devices, sum_over_devices(): lax.ppermute(term, AXES, shift_map(axis, d))  6.84 us
    pallas_call x1, Pallas kernels, own_logits(): pl.pallas_call(logits_kernel, in_specs=[HBM] * 3, out_specs=[HBM, VMEM, V...  5.92 us
    ppermute x1, starting transfers between devices, body(): far_keys = lax.ppermute(near_keys, AXES, CORE_SWAP)  5.41 us
    pallas_call x1, Pallas kernels, attention_parts(): pl.pallas_call(attention_kernel, in_specs=[SMEM] + [VMEM] * (6 + len(mask...  5.27 us
    ppermute x1, starting transfers between devices, body(): other = lax.ppermute(other, AXES, FIRST_HOP)  4.88 us
    ppermute x1, starting transfers between devices, body(): two_stats = jnp.stack([stats, lax.ppermute(stats, AXES, Y_PAIR)])  4.7 us
  transfers between devices with their start and end apart: 20, of which 9 were waited for; matrix products, arithmetic and copies ran while one was open for 0% of the time, Pallas kernels for 16%

profile of v2, /device:TPU:2, one launch (start us, length us, event | category | flops | bytes accessed | tf_op | source)
XLA Modules:
  0.0 85.7 jit_solution(5654981670165436347)
XLA Ops:
  0.7 1.1 %concatenate.3 = bf16[64,896]{1,0:T(8,128)(2,1)S(1)} concatenate(bf16[64,192]{1,0:T(8,128)(2,1)} %param.27, bf16[64,144]{1,0:T(8,128)(2,1)} %param.28, bf16[64,192]{1,0:T(8,128)(2,1)} %param.29, bf16[64,288]{1,0:T(8,128)(2,1)} %param.30, bf16[64,80]{1,0:T(8,128)(2,1)S(1)} %broadcast_in_dim.3), dimensions={1} | concatenate | bytes 229376 | tf_op jit(solution)/shard_map/concatenate | solution.py:479
  1.9 3.8 %collective-permute-start = (bf16[64,896]{1,0:T(8,128)(2,1)S(1)}, bf16[64,896]{1,0:T(8,128)(2,1)S(1)}, u32[]{:S(2)}, u32[]{:S(2)}) collective-permute-start(bf16[64,896]{1,0:T(8,128)(2,1)S(1)} %concatenate.3), channel_id=1, source_target_pairs={{0,0},{8,8},{16,1},{24,9},{32,2},{40,10},{48,3},{56,11},{4,64},{12... | collective-permute-start | bytes 344072 | tf_op jit(solution)/shard_map/ppermute | solution.py:480
  5.7 5.9 %own_logits.1 = (f32[64,64,128]{2,1,0:T(8,128)}, s16[33,64,128]{2,1,0:T(8,128)(2,1)}, s16[33,64,128]{2,1,0:T(8,128)(2,1)}) custom-call(bf16[64,128,128]{2,1,0:T(8,128)(2,1)} %pair_ref.3, bf16[64,128]{1,0:T(8,128)(2,1)} %bitcast.8, s32[64,128]{1,0:T(8,128)} %labels_ref.1), custom_call_target="tpu_custom_call" | custom-call | flops 200000000 | bytes 6000000 | tf_op jit(solution)/shard_map/own_logits/pallas_call | solution.py:191
  11.6 2.1 %collective-permute-start.2 = (s16[33,64,128]{2,1,0:T(8,128)(2,1)}, s16[33,64,128]{2,1,0:T(8,128)(2,1)S(1)}, u32[]{:S(2)}, u32[]{:S(2)}) collective-permute-start(s16[33,64,128]{2,1,0:T(8,128)(2,1)} %get-tuple-element.28), channel_id=1, source_target_pairs={{0,0},{8,10},{16,16},{24,9},{32,32},{40,8},{48,48},{56,11},{4,4},{... | collective-permute-start | bytes 1622024 | tf_op jit(solution)/shard_map/ppermute | solution.py:483
  13.7 4.9 %collective-permute-start.3 = (s16[33,64,128]{2,1,0:T(8,128)(2,1)}, s16[33,64,128]{2,1,0:T(8,128)(2,1)S(1)}, u32[]{:S(2)}, u32[]{:S(2)}) collective-permute-start(s16[33,64,128]{2,1,0:T(8,128)(2,1)} %get-tuple-element.29), channel_id=1, source_target_pairs={{0,0},{8,10},{16,16},{24,9},{32,32},{40,8},{48,48},{56,11},{4,4},{... | collective-permute-start | bytes 1622024 | tf_op jit(solution)/shard_map/ppermute | solution.py:484
  18.6 5.4 %collective-permute-start.1 = (bf16[64,896]{1,0:T(8,128)(2,1)S(1)}, bf16[64,896]{1,0:T(8,128)(2,1)S(1)}, u32[]{:S(2)}, u32[]{:S(2)}) collective-permute-start(bf16[64,896]{1,0:T(8,128)(2,1)S(1)} %collective-permute-done.near_ref), channel_id=1, source_target_pairs={{0,8},{8,0},{16,24},{24,16},{32,40},{40,32},{48,56},{56,48},{4,12}... | collective-permute-start | bytes 344072 | tf_op jit(solution)/shard_map/ppermute | solution.py:485
  24.0 1.0 %collective-permute-done.1.far_ref = bf16[64,896]{1,0:T(8,128)(2,1)S(1)} collective-permute-done((bf16[64,896]{1,0:T(8,128)(2,1)S(1)}, bf16[64,896]{1,0:T(8,128)(2,1)S(1)}, u32[]{:S(2)}, u32[]{:S(2)}) %collective-permute-start.1) | collective-permute-done | bytes 114720 | tf_op jit(solution)/shard_map/ppermute | solution.py:485
  25.1 0.8 copy-done.13
  25.8 0.7 copy-done.14
  26.5 0.7 copy-done.15
  27.3 5.3 %attention_parts.1 = (f32[64,16,128]{2,1,0:T(8,128)S(1)}, f32[64,16,128]{2,1,0:T(8,128)S(1)}, bf16[64,16,128]{2,1,0:T(8,128)(2,1)S(1)}, f32[24,128]{1,0:T(8,128)S(1)}) custom-call(f32[12]{0:T(128)S(1)} %copy-done.12, bf16[64,128,128]{2,1,0:T(8,128)(2,1)S(1)} %copy-done, bf16[64,896]{1,0:T(8,128)(2,1)S(1)} %collective-permute-done.near_ref, ...), custom_call_target="tpu_custom_call" | custom-call | flops 1000000000 | bytes 4000000 | tf_op jit(solution)/shard_map/attention_parts/pallas_call | solution.py:303
  32.5 3.8 %collective-permute-start.4 = (s16[33,64,128]{2,1,0:T(8,128)(2,1)S(1)}, s16[33,64,128]{2,1,0:T(8,128)(2,1)S(1)}, u32[]{:S(2)}, u32[]{:S(2)}) collective-permute-start(s16[33,64,128]{2,1,0:T(8,128)(2,1)S(1)} %collective-permute-done.2), channel_id=1, source_target_pairs={{0,0},{10,8},{16,1},{9,9},{32,2},{8,10},{48,3},{11,11},{4,64},{74,... | collective-permute-start | bytes 1622024 | tf_op jit(solution)/shard_map/ppermute | solution.py:497
  36.8 4.7 %collective-permute-start.6 = (f32[24,128]{1,0:T(8,128)S(1)}, f32[24,128]{1,0:T(8,128)S(1)}, u32[]{:S(2)}, u32[]{:S(2)}) collective-permute-start(f32[24,128]{1,0:T(8,128)S(1)} %get-tuple-element.33), channel_id=1, source_target_pairs={{0,4},{8,12},{16,20},{24,28},{32,36},{40,44},{48,52},{56,60},{4,0}... | collective-permute-start | bytes 36872 | tf_op jit(solution)/shard_map/ppermute | solution.py:499
  41.5 1.7 %collective-permute-done.6 = f32[24,128]{1,0:T(8,128)S(1)} collective-permute-done((f32[24,128]{1,0:T(8,128)S(1)}, f32[24,128]{1,0:T(8,128)S(1)}, u32[]{:S(2)}, u32[]{:S(2)}) %collective-permute-start.6) | collective-permute-done | bytes 12320 | tf_op jit(solution)/shard_map/ppermute | solution.py:499
  43.2 5.7 %collective-permute-start.8 = (f32[2,24,128]{2,1,0:T(8,128)S(1)}, f32[2,24,128]{2,1,0:T(8,128)S(1)}, u32[]{:S(2)}, u32[]{:S(2)}) collective-permute-start(f32[2,24,128]{2,1,0:T(8,128)S(1)} %pad_maximum_fusion.refs_0_), channel_id=1, source_target_pairs={{0,2},{8,10},{16,18},{24,26},{32,34},{40,42},{48,50},{56,58},{4,6}... | collective-permute-start | bytes 73736 | tf_op jit(solution)/shard_map/ppermute | solution.py:500
  48.9 2.6 %collective-permute-start.7 = (f32[2,24,128]{2,1,0:T(8,128)S(1)}, f32[2,24,128]{2,1,0:T(8,128)S(1)}, u32[]{:S(2)}, u32[]{:S(2)}) collective-permute-start(f32[2,24,128]{2,1,0:T(8,128)S(1)} %pad_maximum_fusion.refs_0_), channel_id=1, source_target_pairs={{0,1},{8,9},{16,17},{24,25},{32,33},{40,41},{48,49},{56,57},{4,5},... | collective-permute-start | bytes 73736 | tf_op jit(solution)/shard_map/ppermute | solution.py:500
  51.5 1.6 %collective-permute-done.9.refs_3_ = f32[2,24,128]{2,1,0:T(8,128)S(1)} collective-permute-done((f32[2,24,128]{2,1,0:T(8,128)S(1)}, f32[2,24,128]{2,1,0:T(8,128)S(1)}, u32[]{:S(2)}, u32[]{:S(2)}) %collective-permute-start.9) | collective-permute-done | bytes 24608 | tf_op jit(solution)/shard_map/ppermute | solution.py:500
  53.2 4.5 %bin_gradient.1 = (bf16[64,64,128]{2,1,0:T(8,128)(2,1)S(1)}, f32[64,128]{1,0:T(8,128)S(1)}) custom-call(s32[1024]{0:T(1024)S(1)} %copy-done.4, bf16[64,128,128]{2,1,0:T(8,128)(2,1)S(1)} %copy-done, f32[64,64,128]{2,1,0:T(8,128)S(1)} %copy-done.1, s32[64,128]{1,0:T(8,128)S(1)} %copy-done.2, s16[33,64,128]{2,1,0:T(8,128)(2,1)S(1)} %collective-permute-done.4.near_ref, ...), custom_call_target="tpu_custom_call" | custom-call | flops 200000000 | bytes 6000000 | tf_op jit(solution)/shard_map/bin_gradient/pallas_call | solution.py:379
  57.8 1.2 %collective-permute-done.10 = f32[64,128]{1,0:T(8,128)S(1)} collective-permute-done((f32[64,128]{1,0:T(8,128)S(1)}, f32[64,128]{1,0:T(8,128)S(1)}, u32[]{:S(2)}, u32[]{:S(2)}) %collective-permute-start.10) | collective-permute-done | bytes 32800 | tf_op jit(solution)/shard_map/ppermute | solution.py:449
  59.0 2.3 %collective-permute-start.13 = (f32[64,128]{1,0:T(8,128)S(1)}, f32[64,128]{1,0:T(8,128)S(1)}, u32[]{:S(2)}, u32[]{:S(2)}) collective-permute-start(f32[64,128]{1,0:T(8,128)S(1)} %add.30), channel_id=1, source_target_pairs={{0,3},{8,11},{16,19},{24,27},{32,35},{40,43},{48,51},{56,59},{4,7}... | collective-permute-start | bytes 98312 | tf_op jit(solution)/shard_map/ppermute | solution.py:451
  61.8 2.4 %collective-permute-start.11 = (f32[64,128]{1,0:T(8,128)S(1)}, f32[64,128]{1,0:T(8,128)S(1)}, u32[]{:S(2)}, u32[]{:S(2)}) collective-permute-start(f32[64,128]{1,0:T(8,128)S(1)} %add.30), channel_id=1, source_target_pairs={{0,2},{8,10},{16,18},{24,26},{32,34},{40,42},{48,50},{56,58},{4,6}... | collective-permute-start | bytes 98312 | tf_op jit(solution)/shard_map/ppermute | solution.py:451
  64.1 1.0 %collective-permute-done.12 = f32[64,128]{1,0:T(8,128)S(1)} collective-permute-done((f32[64,128]{1,0:T(8,128)S(1)}, f32[64,128]{1,0:T(8,128)S(1)}, u32[]{:S(2)}, u32[]{:S(2)}) %collective-permute-start.12) | collective-permute-done | bytes 32800 | tf_op jit(solution)/shard_map/ppermute | solution.py:451
  65.2 2.0 %collective-permute-done.11 = f32[64,128]{1,0:T(8,128)S(1)} collective-permute-done((f32[64,128]{1,0:T(8,128)S(1)}, f32[64,128]{1,0:T(8,128)S(1)}, u32[]{:S(2)}, u32[]{:S(2)}) %collective-permute-start.11) | collective-permute-done | bytes 32800 | tf_op jit(solution)/shard_map/ppermute | solution.py:451
  67.2 3.1 %collective-permute-start.16 = (f32[64,128]{1,0:T(8,128)S(1)}, f32[64,128]{1,0:T(8,128)S(1)}, u32[]{:S(2)}, u32[]{:S(2)}) collective-permute-start(f32[64,128]{1,0:T(8,128)S(1)} %add_add_fusion.1), channel_id=1, source_target_pairs={{0,68},{8,76},{16,84},{24,92},{32,100},{40,108},{48,116},{56,124},... | collective-permute-start | bytes 98312 | tf_op jit(solution)/shard_map/ppermute | solution.py:451
  70.3 1.5 %collective-permute-start.15 = (f32[64,128]{1,0:T(8,128)S(1)}, f32[64,128]{1,0:T(8,128)S(1)}, u32[]{:S(2)}, u32[]{:S(2)}) collective-permute-start(f32[64,128]{1,0:T(8,128)S(1)} %add_add_fusion.1), channel_id=1, source_target_pairs={{0,4},{8,12},{16,20},{24,28},{32,36},{40,44},{48,52},{56,60},{4,64... | collective-permute-start | bytes 98312 | tf_op jit(solution)/shard_map/ppermute | solution.py:451
  71.8 3.6 %collective-permute-start.14 = (f32[64,128]{1,0:T(8,128)S(1)}, f32[64,128]{1,0:T(8,128)S(1)}, u32[]{:S(2)}, u32[]{:S(2)}) collective-permute-start(f32[64,128]{1,0:T(8,128)S(1)} %add_add_fusion.1), channel_id=1, source_target_pairs={{0,64},{8,72},{16,80},{24,88},{32,96},{40,104},{48,112},{56,120},{... | collective-permute-start | bytes 98312 | tf_op jit(solution)/shard_map/ppermute | solution.py:451
  75.8 1.8 %collective-permute-done.14 = f32[64,128]{1,0:T(8,128)S(1)} collective-permute-done((f32[64,128]{1,0:T(8,128)S(1)}, f32[64,128]{1,0:T(8,128)S(1)}, u32[]{:S(2)}, u32[]{:S(2)}) %collective-permute-start.14) | collective-permute-done | bytes 32800 | tf_op jit(solution)/shard_map/ppermute | solution.py:451
  77.6 0.9 %collective-permute-start.19 = (f32[64,128]{1,0:T(8,128)S(1)}, f32[64,128]{1,0:T(8,128)S(1)}, u32[]{:S(2)}, u32[]{:S(2)}) collective-permute-start(f32[64,128]{1,0:T(8,128)S(1)} %add_add_fusion), channel_id=1, source_target_pairs={{0,48},{8,56},{16,0},{24,8},{32,16},{40,24},{48,32},{56,40},{4,52}... | collective-permute-start | bytes 98312 | tf_op jit(solution)/shard_map/ppermute | solution.py:451
  78.5 1.2 %collective-permute-start.18 = (f32[64,128]{1,0:T(8,128)S(1)}, f32[64,128]{1,0:T(8,128)S(1)}, u32[]{:S(2)}, u32[]{:S(2)}) collective-permute-start(f32[64,128]{1,0:T(8,128)S(1)} %add_add_fusion), channel_id=1, source_target_pairs={{0,16},{8,24},{16,32},{24,40},{32,48},{40,56},{48,0},{56,8},{4,20}... | collective-permute-start | bytes 98312 | tf_op jit(solution)/shard_map/ppermute | solution.py:451
  79.7 1.6 %collective-permute-start.17 = (f32[64,128]{1,0:T(8,128)S(1)}, f32[64,128]{1,0:T(8,128)S(1)}, u32[]{:S(2)}, u32[]{:S(2)}) collective-permute-start(f32[64,128]{1,0:T(8,128)S(1)} %add_add_fusion), channel_id=1, source_target_pairs={{0,32},{8,40},{16,48},{24,56},{32,0},{40,8},{48,16},{56,24},{4,36}... | collective-permute-start | bytes 98312 | tf_op jit(solution)/shard_map/ppermute | solution.py:451
  81.3 2.2 %pair_gradient.1 = bf16[64,128,128]{2,1,0:T(8,128)(2,1)} custom-call(f32[64,16,128]{2,1,0:T(8,128)S(1)} %get-tuple-element.26.exp_ref, f32[64,16,128]{2,1,0:T(8,128)S(1)} %get-tuple-element.27.grad_ref, f32[2,24,128]{2,1,0:T(8,128)S(1)} %pad_maximum_fusion.refs_0_, f32[2,24,128]{2,1,0:T(8,128)S(1)} %collective-permute-done.7.refs_1_, ...), custom_call_target="tpu_custom_call" | custom-call | flops 300000000 | bytes 5000000 | tf_op jit(solution)/shard_map/pair_gradient/pallas_call | solution.py:433
  83.6 1.5 %collective-permute-done.17 = f32[64,128]{1,0:T(8,128)S(1)} collective-permute-done((f32[64,128]{1,0:T(8,128)S(1)}, f32[64,128]{1,0:T(8,128)S(1)}, u32[]{:S(2)}, u32[]{:S(2)}) %collective-permute-start.17) | collective-permute-done | bytes 32800 | tf_op jit(solution)/shard_map/ppermute | solution.py:451
  (51 shorter events, 2.3 us)
Async XLA Ops:
  0.6 24.3 %copy-start = (bf16[64,128,128]{2,1,0:T(8,128)(2,1)S(1)}, bf16[64,128,128]{2,1,0:T(8,128)(2,1)}, u32[]{:S(2)}) copy-start(bf16[64,128,128]{2,1,0:T(8,128)(2,1)} %pair_ref.3) | copy-start | bytes 6291460
  0.6 24.3 %copy-start.4 = (s32[1024]{0:T(1024)S(1)}, s32[1024]{0:T(1024)}, u32[]{:S(2)}) copy-start(s32[1024]{0:T(1024)} %mask_smem.1) | copy-start | bytes 12292
  0.7 24.3 %copy-start.7 = (bf16[64,1536]{1,0:T(8,128)(2,1)S(1)}, bf16[64,1536]{1,0:T(8,128)(2,1)}, u32[]{:S(2)}) copy-start(bf16[64,1536]{1,0:T(8,128)(2,1)} %cot_ref.1) | copy-start | bytes 589828
  0.7 24.3 %copy-start.8 = (bf16[64,288]{1,0:T(8,128)(2,1)S(1)}, bf16[64,288]{1,0:T(8,128)(2,1)}, u32[]{:S(2)}) copy-start(bf16[64,288]{1,0:T(8,128)(2,1)} %refs_6_.1) | copy-start | bytes 110596
  0.7 24.3 %copy-start.11 = (bf16[64,192]{1,0:T(8,128)(2,1)S(1)}, bf16[64,192]{1,0:T(8,128)(2,1)}, u32[]{:S(2)}) copy-start(bf16[64,192]{1,0:T(8,128)(2,1)} %refs_5_.1) | copy-start | bytes 73732
  0.7 24.3 %copy-start.12 = (f32[12]{0:T(128)S(1)}, f32[12]{0:T(128)}, u32[]{:S(2)}) copy-start(f32[12]{0:T(128)} %point_smem.1) | copy-start | bytes 148
  0.7 24.3 %copy-start.10 = (bf16[64,144]{1,0:T(8,128)(2,1)S(1)}, bf16[64,144]{1,0:T(8,128)(2,1)}, u32[]{:S(2)}) copy-start(bf16[64,144]{1,0:T(8,128)(2,1)} %refs_4_.1) | copy-start | bytes 55300
  0.7 24.3 %copy-start.9 = (bf16[64,192]{1,0:T(8,128)(2,1)S(1)}, bf16[64,192]{1,0:T(8,128)(2,1)}, u32[]{:S(2)}) copy-start(bf16[64,192]{1,0:T(8,128)(2,1)} %refs_3_.1) | copy-start | bytes 73732
  1.9 9.8 %collective-permute-start = (bf16[64,896]{1,0:T(8,128)(2,1)S(1)}, bf16[64,896]{1,0:T(8,128)(2,1)S(1)}, u32[]{:S(2)}, u32[]{:S(2)}) collective-permute-start(bf16[64,896]{1,0:T(8,128)(2,1)S(1)} %concatenate.3), channel_id=1, source_target_pairs={{0,0},{8,8},{16,1},{24,9},{32,2},{40,10},{48,3},{56,11},{4,64},{12... | collective-permute-start | bytes 344072 | tf_op jit(solution)/shard_map/ppermute | solution.py:480
  11.6 41.5 %copy-start.1 = (f32[64,64,128]{2,1,0:T(8,128)S(1)}, f32[64,64,128]{2,1,0:T(8,128)}, u32[]{:S(2)}) copy-start(f32[64,64,128]{2,1,0:T(8,128)} %get-tuple-element.38.own_ref) | copy-start | bytes 6291460
  11.6 41.5 %copy-start.2 = (s32[64,128]{1,0:T(8,128)S(1)}, s32[64,128]{1,0:T(8,128)}, u32[]{:S(2)}) copy-start(s32[64,128]{1,0:T(8,128)} %labels_ref.1) | copy-start | bytes 98308
  11.6 41.5 %copy-start.6 = (f32[64]{0:T(128)S(1)}, f32[64]{0:T(128)}, u32[]{:S(2)}) copy-start(f32[64]{0:T(128)} %param.23) | copy-start | bytes 772
  11.6 20.9 %collective-permute-start.2 = (s16[33,64,128]{2,1,0:T(8,128)(2,1)}, s16[33,64,128]{2,1,0:T(8,128)(2,1)S(1)}, u32[]{:S(2)}, u32[]{:S(2)}) collective-permute-start(s16[33,64,128]{2,1,0:T(8,128)(2,1)} %get-tuple-element.28), channel_id=1, source_target_pairs={{0,0},{8,10},{16,16},{24,9},{32,32},{40,8},{48,48},{56,11},{4,4},{... | collective-permute-start | bytes 1622024 | tf_op jit(solution)/shard_map/ppermute | solution.py:483
  13.7 18.8 %collective-permute-start.3 = (s16[33,64,128]{2,1,0:T(8,128)(2,1)}, s16[33,64,128]{2,1,0:T(8,128)(2,1)S(1)}, u32[]{:S(2)}, u32[]{:S(2)}) collective-permute-start(s16[33,64,128]{2,1,0:T(8,128)(2,1)} %get-tuple-element.29), channel_id=1, source_target_pairs={{0,0},{8,10},{16,16},{24,9},{32,32},{40,8},{48,48},{56,11},{4,4},{... | collective-permute-start | bytes 1622024 | tf_op jit(solution)/shard_map/ppermute | solution.py:484
  18.6 6.4 %collective-permute-start.1 = (bf16[64,896]{1,0:T(8,128)(2,1)S(1)}, bf16[64,896]{1,0:T(8,128)(2,1)S(1)}, u32[]{:S(2)}, u32[]{:S(2)}) collective-permute-start(bf16[64,896]{1,0:T(8,128)(2,1)S(1)} %collective-permute-done.near_ref), channel_id=1, source_target_pairs={{0,8},{8,0},{16,24},{24,16},{32,40},{40,32},{48,56},{56,48},{4,12}... | collective-permute-start | bytes 344072 | tf_op jit(solution)/shard_map/ppermute | solution.py:485
  32.5 20.6 %collective-permute-start.4 = (s16[33,64,128]{2,1,0:T(8,128)(2,1)S(1)}, s16[33,64,128]{2,1,0:T(8,128)(2,1)S(1)}, u32[]{:S(2)}, u32[]{:S(2)}) collective-permute-start(s16[33,64,128]{2,1,0:T(8,128)(2,1)S(1)} %collective-permute-done.2), channel_id=1, source_target_pairs={{0,0},{10,8},{16,1},{9,9},{32,2},{8,10},{48,3},{11,11},{4,64},{74,... | collective-permute-start | bytes 1622024 | tf_op jit(solution)/shard_map/ppermute | solution.py:497
  36.3 16.8 %collective-permute-start.5 = (s16[33,64,128]{2,1,0:T(8,128)(2,1)S(1)}, s16[33,64,128]{2,1,0:T(8,128)(2,1)S(1)}, u32[]{:S(2)}, u32[]{:S(2)}) collective-permute-start(s16[33,64,128]{2,1,0:T(8,128)(2,1)S(1)} %collective-permute-done.3), channel_id=1, source_target_pairs={{0,8},{10,0},{16,9},{9,1},{32,10},{8,2},{48,11},{11,3},{4,72},{74,... | collective-permute-start | bytes 1622024 | tf_op jit(solution)/shard_map/ppermute | solution.py:498
  36.8 6.4 %collective-permute-start.6 = (f32[24,128]{1,0:T(8,128)S(1)}, f32[24,128]{1,0:T(8,128)S(1)}, u32[]{:S(2)}, u32[]{:S(2)}) collective-permute-start(f32[24,128]{1,0:T(8,128)S(1)} %get-tuple-element.33), channel_id=1, source_target_pairs={{0,4},{8,12},{16,20},{24,28},{32,36},{40,44},{48,52},{56,60},{4,0}... | collective-permute-start | bytes 36872 | tf_op jit(solution)/shard_map/ppermute | solution.py:499
  43.2 9.9 %collective-permute-start.9 = (f32[2,24,128]{2,1,0:T(8,128)S(1)}, f32[2,24,128]{2,1,0:T(8,128)S(1)}, u32[]{:S(2)}, u32[]{:S(2)}) collective-permute-start(f32[2,24,128]{2,1,0:T(8,128)S(1)} %pad_maximum_fusion.refs_0_), channel_id=1, source_target_pairs={{0,3},{8,11},{16,19},{24,27},{32,35},{40,43},{48,51},{56,59},{4,7}... | collective-permute-start | bytes 73736 | tf_op jit(solution)/shard_map/ppermute | solution.py:500
  43.2 9.9 %collective-permute-start.8 = (f32[2,24,128]{2,1,0:T(8,128)S(1)}, f32[2,24,128]{2,1,0:T(8,128)S(1)}, u32[]{:S(2)}, u32[]{:S(2)}) collective-permute-start(f32[2,24,128]{2,1,0:T(8,128)S(1)} %pad_maximum_fusion.refs_0_), channel_id=1, source_target_pairs={{0,2},{8,10},{16,18},{24,26},{32,34},{40,42},{48,50},{56,58},{4,6}... | collective-permute-start | bytes 73736 | tf_op jit(solution)/shard_map/ppermute | solution.py:500
  48.9 4.2 %collective-permute-start.7 = (f32[2,24,128]{2,1,0:T(8,128)S(1)}, f32[2,24,128]{2,1,0:T(8,128)S(1)}, u32[]{:S(2)}, u32[]{:S(2)}) collective-permute-start(f32[2,24,128]{2,1,0:T(8,128)S(1)} %pad_maximum_fusion.refs_0_), channel_id=1, source_target_pairs={{0,1},{8,9},{16,17},{24,25},{32,33},{40,41},{48,49},{56,57},{4,5},... | collective-permute-start | bytes 73736 | tf_op jit(solution)/shard_map/ppermute | solution.py:500
  53.2 28.2 %copy-start.3 = (bf16[128,64]{0,1:T(8,128)(2,1)S(1)}, bf16[128,64]{0,1:T(8,128)(2,1)}, u32[]{:S(2)}) copy-start(bf16[128,64]{0,1:T(8,128)(2,1)} %param.22) | copy-start | bytes 49156
  57.7 1.3 %collective-permute-start.10 = (f32[64,128]{1,0:T(8,128)S(1)}, f32[64,128]{1,0:T(8,128)S(1)}, u32[]{:S(2)}, u32[]{:S(2)}) collective-permute-start(f32[64,128]{1,0:T(8,128)S(1)} %get-tuple-element.43), channel_id=1, source_target_pairs={{0,8},{8,0},{16,24},{24,16},{32,40},{40,32},{48,56},{56,48},{4,12}... | collective-permute-start | bytes 98312 | tf_op jit(solution)/shard_map/ppermute | solution.py:449
  59.0 5.2 %collective-permute-start.13 = (f32[64,128]{1,0:T(8,128)S(1)}, f32[64,128]{1,0:T(8,128)S(1)}, u32[]{:S(2)}, u32[]{:S(2)}) collective-permute-start(f32[64,128]{1,0:T(8,128)S(1)} %add.30), channel_id=1, source_target_pairs={{0,3},{8,11},{16,19},{24,27},{32,35},{40,43},{48,51},{56,59},{4,7}... | collective-permute-start | bytes 98312 | tf_op jit(solution)/shard_map/ppermute | solution.py:451
  61.3 3.9 %collective-permute-start.12 = (f32[64,128]{1,0:T(8,128)S(1)}, f32[64,128]{1,0:T(8,128)S(1)}, u32[]{:S(2)}, u32[]{:S(2)}) collective-permute-start(f32[64,128]{1,0:T(8,128)S(1)} %add.30), channel_id=1, source_target_pairs={{0,1},{8,9},{16,17},{24,25},{32,33},{40,41},{48,49},{56,57},{4,5},... | collective-permute-start | bytes 98312 | tf_op jit(solution)/shard_map/ppermute | solution.py:451
  61.8 5.4 %collective-permute-start.11 = (f32[64,128]{1,0:T(8,128)S(1)}, f32[64,128]{1,0:T(8,128)S(1)}, u32[]{:S(2)}, u32[]{:S(2)}) collective-permute-start(f32[64,128]{1,0:T(8,128)S(1)} %add.30), channel_id=1, source_target_pairs={{0,2},{8,10},{16,18},{24,26},{32,34},{40,42},{48,50},{56,58},{4,6}... | collective-permute-start | bytes 98312 | tf_op jit(solution)/shard_map/ppermute | solution.py:451
  67.2 8.1 %collective-permute-start.16 = (f32[64,128]{1,0:T(8,128)S(1)}, f32[64,128]{1,0:T(8,128)S(1)}, u32[]{:S(2)}, u32[]{:S(2)}) collective-permute-start(f32[64,128]{1,0:T(8,128)S(1)} %add_add_fusion.1), channel_id=1, source_target_pairs={{0,68},{8,76},{16,84},{24,92},{32,100},{40,108},{48,116},{56,124},... | collective-permute-start | bytes 98312 | tf_op jit(solution)/shard_map/ppermute | solution.py:451
  70.3 5.5 %collective-permute-start.15 = (f32[64,128]{1,0:T(8,128)S(1)}, f32[64,128]{1,0:T(8,128)S(1)}, u32[]{:S(2)}, u32[]{:S(2)}) collective-permute-start(f32[64,128]{1,0:T(8,128)S(1)} %add_add_fusion.1), channel_id=1, source_target_pairs={{0,4},{8,12},{16,20},{24,28},{32,36},{40,44},{48,52},{56,60},{4,64... | collective-permute-start | bytes 98312 | tf_op jit(solution)/shard_map/ppermute | solution.py:451
  71.8 5.8 %collective-permute-start.14 = (f32[64,128]{1,0:T(8,128)S(1)}, f32[64,128]{1,0:T(8,128)S(1)}, u32[]{:S(2)}, u32[]{:S(2)}) collective-permute-start(f32[64,128]{1,0:T(8,128)S(1)} %add_add_fusion.1), channel_id=1, source_target_pairs={{0,64},{8,72},{16,80},{24,88},{32,96},{40,104},{48,112},{56,120},{... | collective-permute-start | bytes 98312 | tf_op jit(solution)/shard_map/ppermute | solution.py:451
  77.6 6.0 %collective-permute-start.19 = (f32[64,128]{1,0:T(8,128)S(1)}, f32[64,128]{1,0:T(8,128)S(1)}, u32[]{:S(2)}, u32[]{:S(2)}) collective-permute-start(f32[64,128]{1,0:T(8,128)S(1)} %add_add_fusion), channel_id=1, source_target_pairs={{0,48},{8,56},{16,0},{24,8},{32,16},{40,24},{48,32},{56,40},{4,52}... | collective-permute-start | bytes 98312 | tf_op jit(solution)/shard_map/ppermute | solution.py:451
  78.5 5.1 %collective-permute-start.18 = (f32[64,128]{1,0:T(8,128)S(1)}, f32[64,128]{1,0:T(8,128)S(1)}, u32[]{:S(2)}, u32[]{:S(2)}) collective-permute-start(f32[64,128]{1,0:T(8,128)S(1)} %add_add_fusion), channel_id=1, source_target_pairs={{0,16},{8,24},{16,32},{24,40},{32,48},{40,56},{48,0},{56,8},{4,20}... | collective-permute-start | bytes 98312 | tf_op jit(solution)/shard_map/ppermute | solution.py:451
  79.7 5.4 %collective-permute-start.17 = (f32[64,128]{1,0:T(8,128)S(1)}, f32[64,128]{1,0:T(8,128)S(1)}, u32[]{:S(2)}, u32[]{:S(2)}) collective-permute-start(f32[64,128]{1,0:T(8,128)S(1)} %add_add_fusion), channel_id=1, source_target_pairs={{0,32},{8,40},{16,48},{24,56},{32,0},{40,8},{48,16},{56,24},{4,36}... | collective-permute-start | bytes 98312 | tf_op jit(solution)/shard_map/ppermute | solution.py:451
  (4 other events, 26.5 us)

commit v3 on v2

--- a/solution.py
+++ b/solution.py
@@ -15,11 +15,14 @@
 PAD_HEADS = 16
 CHUNK = 8
 QUANT = 32760.0
+BINS = 64
+STATS = 24
 
 WIDTHS = (192, 144, 192, 288)
 PER_HEAD = (16, 12, 16, 24)
 CAT = 896
 WINDOWS = ((0, 256), (128, 384), (256, 896))
+WINDOW_PARTS = ((0,), (1,), (2, 3))
 
 NT = (((1,), (1,)), ((), ()))
 TN = (((0,), (0,)), ((), ()))
@@ -58,26 +61,25 @@
 CORE_SWAP = [(device_index(n, h), device_index(n, 1 - h)) for n in CHIPS for h in (0, 1)]
 
 
-Y_PAIR = [(device_index((x, y, z), h), device_index((x, y ^ 1, z), h)) for x, y, z in CHIPS for h in (0, 1)]
-
-
-def shift_map(axis, distance):
+def trade_map(axis, bits):
     pairs = []
     for n in CHIPS:
         m = list(n)
-        m[axis] = (m[axis] + distance) % 4
+        m[axis] ^= bits
         pairs += [(device_index(n, h), device_index(tuple(m), h)) for h in (0, 1)]
     return pairs
 
 
-def head_masks():
-    masks = np.zeros((3, PAD_HEADS, CAT), np.float32)
-    start = 0
-    for part, (width, size) in enumerate(zip(WIDTHS, PER_HEAD)):
-        for column in range(width):
-            masks[min(part, 2), column // size, start + column] = 1.0
-        start += width
-    return [masks[k][:, lo:hi] for k, (lo, hi) in enumerate(WINDOWS)]
+def head_columns(lo, hi, parts):
+    head = lax.broadcasted_iota(jnp.int32, (PAD_HEADS, hi - lo), 0)
+    column = lax.broadcasted_iota(jnp.int32, (PAD_HEADS, hi - lo), 1) + lo
+    held = jnp.zeros((PAD_HEADS, hi - lo), jnp.float32)
+    for part in parts:
+        size = PER_HEAD[part]
+        first = sum(WIDTHS[:part]) + head * size
+        inside = (column >= first) & (column < first + size) & (head < HEADS)
+        held = jnp.where(inside, 1.0, held)
+    return held
 
 
 def dot(a, b, dims=(((1,), (0,)), ((), ()))):
@@ -129,25 +131,30 @@
 PARAMS = pltpu.CompilerParams(vmem_limit_bytes=16 * 1024 * 1024)
 
 
-def logits_kernel(
-    pair_hbm, weight_hbm, labels_hbm, own_hbm, same_ref, other_ref, pair_ref, weight_ref, labels_ref, own_ref, slabs,
-    top, pair_sem, own_sem, small_sem,
-):
-    small = [
-        pltpu.make_async_copy(weight_hbm, weight_ref, small_sem.at[0]),
-        pltpu.make_async_copy(labels_hbm, labels_ref, small_sem.at[1]),
-    ]
-    coming = chunk_copies(pair_hbm, pair_ref, pair_sem)
-    going = chunk_copies(own_ref, own_hbm, own_sem)
-    small[0].start()
-    coming[0].start()
-    for copy in coming[1:] + small[1:]:
-        copy.start()
-    small[0].wait()
+SLABS = 33
+SLAB_PARTS = ((0, 8), (8, 16), (16, 24), (24, 33))
+
+
+def logits_kernel(pair_hbm, weight_hbm, labels_hbm, *refs):
+    keys_hbm, (own_hbm, same_hbm, other_hbm, cat_hbm) = refs[:4], refs[4:8]
+    pair_ref, weight_ref, labels_ref, own_ref, same_ref, other_ref, cat_ref, slabs, top = refs[8:17]
+    pair_sem, own_sem, slab_sem, small_sem = refs[17:21]
+    keys_refs = refs[21:]
+    copy = pltpu.make_async_copy
+    weight_in = copy(weight_hbm, weight_ref, small_sem.at[0])
+    small_in = [copy(labels_hbm, labels_ref, small_sem.at[1])]
+    small_in += [copy(a, b, small_sem.at[3 + k]) for k, (a, b) in enumerate(zip(keys_hbm, keys_refs))]
+    cat_out = copy(cat_ref, cat_hbm, small_sem.at[2])
+    pair_in = chunk_copies(pair_hbm, pair_ref, pair_sem)
+    own_out = chunk_copies(own_ref, own_hbm, own_sem)
+    weight_in.start()
+    for c in pair_in + small_in:
+        c.start()
+    weight_in.wait()
     weight_t = weight_ref[...]
-    size = pair_ref.shape[0] // len(coming)
-    for k in range(len(coming)):
-        coming[k].wait()
+    size = pair_ref.shape[0] // len(pair_in)
+    for k in range(len(pair_in)):
+        pair_in[k].wait()
         for first in range(k * size, (k + 1) * size, 4):
             flat = pair_ref[first : first + 4].reshape(4 * 128, 128)
             terms = dot(weight_t, flat, NT)
@@ -157,8 +164,11 @@
                 own_ref[row] = term
                 slabs[pl.ds(row, 64, stride=64), :] = term
                 top[pl.ds(row, 1), :] = jnp.max(jnp.abs(term), axis=0, keepdims=True)
-        going[k].start()
-    small[1].wait()
+        own_out[k].start()
+    for c in small_in:
+        c.wait()
+    lay_out(cat_ref, keys_refs)
+    cat_out.start()
 
     core = own_core()
     level = jnp.ceil(16.0 * jnp.log2(jnp.maximum(top[...], 1e-30)))
@@ -173,51 +183,85 @@
         same_ref[slab] = narrow(jnp.where(core == 0, first, second))
         other_ref[slab] = narrow(jnp.where(core == 0, second, first))
 
-    def pair_of_bins(b, carry):
-        upper = slabs[pl.ds(pl.multiple_of(b * 64, 64), 64), :] * scale
-        lower = slabs[pl.ds(pl.multiple_of((b + 32) * 64, 64), 64), :] * scale
-        put(b, upper, lower)
-        return carry
-
-    lax.fori_loop(0, 32, pair_of_bins, 0, unroll=8)
-    put(32, level, labels_ref[...].astype(jnp.float32))
-    for copy in going:
-        copy.wait()
-
-
-def own_logits(pair_tile, weight_rows, labels):
+    slab_out = []
+    for part, (lo, hi) in enumerate(SLAB_PARTS):
+        for b in range(lo, min(hi, 32)):
+            put(b, slabs[b * 64 : (b + 1) * 64, :] * scale, slabs[(b + 32) * 64 : (b + 33) * 64, :] * scale)
+        if hi == SLABS:
+            put(32, level, labels_ref[...].astype(jnp.float32))
+        for k, (ref, hbm) in enumerate(((same_ref, same_hbm), (other_ref, other_hbm))):
+            slab_out.append(copy(ref.at[pl.ds(lo, hi - lo)], hbm.at[pl.ds(lo, hi - lo)], slab_sem.at[part, k]))
+            slab_out[-1].start()
+    for c in own_out + slab_out + [cat_out]:
+        c.wait()
+
+
+def own_logits(pair_tile, weight_rows, labels, keys):
     rows = pair_tile.shape[0]
-    block = jax.ShapeDtypeStruct((33, 64, 128), jnp.int16)
+    block = jax.ShapeDtypeStruct((SLABS, 64, 128), jnp.int16)
+    cat = jax.ShapeDtypeStruct((rows, CAT), jnp.bfloat16)
+    own = jax.ShapeDtypeStruct((rows, 64, 128), jnp.float32)
+    arrays = [pair_tile, weight_rows, labels, own, block, block, cat]
     return pl.pallas_call(
         logits_kernel,
-        in_specs=[HBM] * 3,
-        out_specs=[HBM, VMEM, VMEM],
-        out_shape=[
-            jax.ShapeDtypeStruct((rows, 64, 128), jnp.float32),
-            block,
-            block,
-        ],
-        scratch_shapes=[
-            pltpu.VMEM(pair_tile.shape, jnp.bfloat16),
-            pltpu.VMEM(weight_rows.shape, jnp.bfloat16),
-            pltpu.VMEM(labels.shape, jnp.int32),
-            pltpu.VMEM((rows, 64, 128), jnp.float32),
+        in_specs=[HBM] * (3 + len(keys)),
+        out_specs=[HBM] * 4,
+        out_shape=[own, block, block, cat],
+        scratch_shapes=[pltpu.VMEM(a.shape, a.dtype) for a in arrays]
+        + [
             pltpu.VMEM((64 * 64, 128), jnp.float32),
             pltpu.VMEM((64, 128), jnp.float32),
             pltpu.SemaphoreType.DMA((8,)),
             pltpu.SemaphoreType.DMA((8,)),
-            pltpu.SemaphoreType.DMA((2,)),
-        ],
+            pltpu.SemaphoreType.DMA((len(SLAB_PARTS), 2)),
+            pltpu.SemaphoreType.DMA((3 + len(keys),)),
+        ]
+        + [pltpu.VMEM(k.shape, k.dtype) for k in keys],
         compiler_params=pltpu.CompilerParams(vmem_limit_bytes=60 * 1024 * 1024),
         cost_estimate=pl.CostEstimate(flops=200_000_000, bytes_accessed=6_000_000, transcendentals=8192),
         name="own_logits",
-    )(pair_tile, weight_rows, labels)
-
-
-def attention_kernel(point_smem, pair_ref, near_ref, far_ref, cot_ref, bias_ref, mask_ref, *refs):
-    scalar_mask_ref, point_mask_ref, value_mask_ref = refs[:3]
-    query_refs = refs[3:7]
-    exp_ref, grad_ref, cot_out_ref, stats_ref, keys, cot_rows, cat_ref = refs[7:]
+    )(pair_tile, weight_rows, labels, *keys)
+
+
+def pair_parts_kernel(pair_ref, cot_ref, bias_ref, bias_out_ref, value_out_ref, cot_out_ref, cot_rows):
+    length = CHUNK * PAD_HEADS
+    for h in range(HEADS):
+        cot_rows[h * 64 : (h + 1) * 64] = cot_ref[:, h * 128 : (h + 1) * 128]
+    bias_t = padded_heads(bias_ref)
+    row_of = lax.broadcasted_iota(jnp.int32, (length, 768), 0)
+    column_of = lax.broadcasted_iota(jnp.int32, (length, 768), 1)
+    same_head = row_of % PAD_HEADS == column_of // 64
+    place = column_of % 64 - row_of // PAD_HEADS
+    for step in range(pair_ref.shape[0] // CHUNK):
+        pick = (same_head & (place == step * CHUNK)).astype(jnp.bfloat16)
+        cot = dot(pick, cot_rows[...]).astype(jnp.bfloat16)
+        cot_out_ref[step * CHUNK : (step + 1) * CHUNK] = cot.reshape(CHUNK, PAD_HEADS, 128)
+        for t in range(CHUNK):
+            row = step * CHUNK + t
+            both = jnp.concatenate([bias_t, cot[t * PAD_HEADS : (t + 1) * PAD_HEADS]], axis=0)
+            result = dot(both, pair_ref[row], NT)
+            bias_out_ref[row] = result[:PAD_HEADS]
+            value_out_ref[row] = result[PAD_HEADS:]
+
+
+def pair_parts(pair_tile, cot_pair, bias_rows):
+    rows = pair_tile.shape[0]
+    part = jax.ShapeDtypeStruct((rows, PAD_HEADS, 128), jnp.float32)
+    return pl.pallas_call(
+        pair_parts_kernel,
+        in_specs=[VMEM] * 3,
+        out_specs=[VMEM] * 3,
+        out_shape=[part, part, jax.ShapeDtypeStruct((rows, PAD_HEADS, 128), jnp.bfloat16)],
+        scratch_shapes=[pltpu.VMEM((768, 128), jnp.bfloat16)],
+        compiler_params=PARAMS,
+        cost_estimate=pl.CostEstimate(flops=1_000_000_000, bytes_accessed=4_000_000, transcendentals=0),
+        name="pair_parts",
+    )(pair_tile, cot_pair, bias_rows)
+
+
+def attention_kernel(point_smem, near_ref, far_ref, pair_bias_ref, pair_value_ref, mask_ref, *refs):
+    query_refs = refs[:4]
+    exp_ref, grad_ref, stats_ref, keys, cat_ref = refs[4:]
     length = CHUNK * PAD_HEADS
 
     def iota(shape, dim):
@@ -228,23 +272,19 @@
     keys[:64] = jnp.where(core == 0, near, far).astype(jnp.bfloat16)
     keys[64:] = jnp.where(core == 0, far, near).astype(jnp.bfloat16)
     lay_out(cat_ref, query_refs)
-    for h in range(HEADS):
-        cot_rows[h * 64 : (h + 1) * 64] = cot_ref[:, h * 128 : (h + 1) * 128]
-    bias_t = padded_heads(bias_ref)
-
+
+    masks = [head_columns(lo, hi, parts) for (lo, hi), parts in zip(WINDOWS, WINDOW_PARTS)]
     right = [keys[:, lo:hi] for lo, hi in WINDOWS]
     key_points = right[1].astype(jnp.float32)
     key_sq = lax.dot_general(
-        point_mask_ref[...],
+        masks[1],
         key_points * key_points,
         NT,
         precision=lax.Precision.HIGHEST,
         preferred_element_type=jnp.float32,
     )
     key_sq = jnp.concatenate([key_sq] * CHUNK, axis=0)
-    head_masks = [
-        jnp.concatenate([mask[...]] * CHUNK, axis=0) for mask in (scalar_mask_ref, point_mask_ref, value_mask_ref)
-    ]
+    masks = [jnp.concatenate([mask] * CHUNK, axis=0) for mask in masks]
 
     head_of = iota((length, 128), 0) % PAD_HEADS
     raw = jnp.zeros((length, 128), jnp.float32)
@@ -255,31 +295,17 @@
     column_mask = mask_ref[pl.ds(lax.axis_index("col"), 1), :]
     key_bias = jnp.where(column_mask > 0, 0.0, -1000000000.0)
     lane = iota((length, 128), 1)
-
-    for step in range(pair_ref.shape[0] // CHUNK):
-        residue = step * CHUNK + iota((length, 64), 0) // PAD_HEADS
-        pick = (residue == iota((length, 64), 1)).astype(jnp.bfloat16)
+    place = iota((length, 64), 1) - iota((length, 64), 0) // PAD_HEADS
+
+    for step in range(exp_ref.shape[0] // CHUNK):
+        pick = (place == step * CHUNK).astype(jnp.bfloat16)
         spread = dot(pick, cat_ref[...])
-        left = [spread[:, lo:hi] * mask for (lo, hi), mask in zip(WINDOWS, head_masks)]
+        left = [spread[:, lo:hi] * mask for (lo, hi), mask in zip(WINDOWS, masks)]
         scalar_term, cross_term, value_term = [dot(a.astype(jnp.bfloat16), b, NT) for a, b in zip(left, right)]
         query_sq = jnp.sum(left[1] * left[1], axis=1, keepdims=True)
-
-        row_of = iota((length, 768), 0)
-        column_of = iota((length, 768), 1)
-        cot_pick = (step * CHUNK + row_of // PAD_HEADS == column_of % 64) & (row_of % PAD_HEADS == column_of // 64)
-        cot = dot(cot_pick.astype(jnp.bfloat16), cot_rows[...]).astype(jnp.bfloat16)
         rows = slice(step * CHUNK, (step + 1) * CHUNK)
-        cot_out_ref[rows] = cot.reshape(CHUNK, PAD_HEADS, 128)
-
-        pair_bias, pair_value = [], []
-        for t in range(CHUNK):
-            both = jnp.concatenate([bias_t, cot[t * PAD_HEADS : (t + 1) * PAD_HEADS]], axis=0)
-            result = dot(both, pair_ref[step * CHUNK + t], NT)
-            pair_bias.append(result[:PAD_HEADS])
-            pair_value.append(result[PAD_HEADS:])
-        pair_bias = jnp.concatenate(pair_bias, axis=0)
-        value_grad = value_term + jnp.concatenate(pair_value, axis=0)
-
+        pair_bias = pair_bias_ref[rows].reshape(length, 128)
+        value_grad = value_term + pair_value_ref[rows].reshape(length, 128)
         logits = (
             LOGIT_WEIGHT
             * (scalar_term * 0.25 + pair_bias - point_scale * (query_sq + key_sq - 2.0 * cross_term))
@@ -297,28 +323,18 @@
             stats_ref[q * 8 + step : q * 8 + step + 1, :] = packed[q : q + 1]
 
 
-def attention_parts(pair_tile, queries, near, far, cot_pair, bias_rows, point_weight, mask_rows):
-    rows = pair_tile.shape[0]
-    masks = [jnp.asarray(m) for m in head_masks()]
+def attention_parts(queries, near, far, pair_bias, pair_value, point_weight, mask_rows):
+    part = jax.ShapeDtypeStruct(pair_bias.shape, jnp.float32)
     return pl.pallas_call(
         attention_kernel,
-        in_specs=[SMEM] + [VMEM] * (6 + len(masks) + len(queries)),
-        out_specs=[VMEM] * 4,
-        out_shape=[
-            jax.ShapeDtypeStruct((rows, PAD_HEADS, 128), jnp.float32),
-            jax.ShapeDtypeStruct((rows, PAD_HEADS, 128), jnp.float32),
-            jax.ShapeDtypeStruct((rows, PAD_HEADS, 128), jnp.bfloat16),
-            jax.ShapeDtypeStruct((24, 128), jnp.float32),
-        ],
-        scratch_shapes=[
-            pltpu.VMEM((128, CAT), jnp.bfloat16),
-            pltpu.VMEM((768, 128), jnp.bfloat16),
-            pltpu.VMEM((64, CAT), jnp.bfloat16),
-        ],
+        in_specs=[SMEM] + [VMEM] * (5 + len(queries)),
+        out_specs=[VMEM] * 3,
+        out_shape=[part, part, jax.ShapeDtypeStruct((STATS, 128), jnp.float32)],
+        scratch_shapes=[pltpu.VMEM((128, CAT), jnp.bfloat16), pltpu.VMEM((64, CAT), jnp.bfloat16)],
         compiler_params=PARAMS,
-        cost_estimate=pl.CostEstimate(flops=1_000_000_000, bytes_accessed=4_000_000, transcendentals=200_000),
+        cost_estimate=pl.CostEstimate(flops=4_000_000_000, bytes_accessed=2_000_000, transcendentals=200_000),
         name="attention_parts",
-    )(point_weight, pair_tile, near, far, cot_pair, bias_rows, mask_rows, *masks, *queries)
+    )(point_weight, near, far, pair_bias, pair_value, mask_rows, *queries)
 
 
 def bins_kernel(
@@ -399,10 +415,10 @@
     length = CHUNK * PAD_HEADS
     weight_t = weight_ref[...]
     bias_t = padded_heads(bias_ref)
-    places = [(ref, y) for ref in stats_refs for y in (0, 1)]
-    tops = [ref[y, 0:8, :] for ref, y in places]
-    totals = [ref[y, 8:16, :] for ref, y in places]
-    weighted = [ref[y, 16:24, :] for ref, y in places]
+    places = [(ref, BINS + STATS * y) for ref in stats_refs for y in (0, 1)]
+    tops = [ref[at : at + 8, :] for ref, at in places]
+    totals = [ref[at + 8 : at + 16, :] for ref, at in places]
+    weighted = [ref[at + 16 : at + 24, :] for ref, at in places]
     top = functools.reduce(jnp.maximum, tops)
     factors = [jnp.exp(m - top) for m in tops]
     total = sum(f * s for f, s in zip(factors, totals))
@@ -445,12 +461,31 @@
     )(weights, value_grad, *stats, bins, cot, weight_rows, bias_rows)
 
 
-def sum_over_devices(term):
-    term = term + lax.ppermute(term, AXES, CORE_SWAP)
-    for axis in range(3):
-        one, two, three = [lax.ppermute(term, AXES, shift_map(axis, d)) for d in (1, 2, 3)]
-        term = (term + two) + (one + three)
-    return term
+def pack_kernel(stats_ref, own_ref, one_ref, two_ref, three_ref, out_ref):
+    out_ref[:BINS] = (own_ref[...] + two_ref[...]) + (one_ref[...] + three_ref[...])
+    out_ref[BINS:] = stats_ref[...]
+
+
+def pack_more_kernel(own_ref, one_ref, two_ref, three_ref, out_ref):
+    out_ref[:BINS] = (own_ref[:BINS] + two_ref[:BINS]) + (one_ref[:BINS] + three_ref[:BINS])
+    out_ref[BINS : BINS + STATS] = own_ref[BINS:]
+    out_ref[BINS + STATS :] = one_ref[BINS:]
+
+
+def packed(kernel, rows, name, *arrays):
+    return pl.pallas_call(
+        kernel,
+        in_specs=[VMEM] * len(arrays),
+        out_specs=VMEM,
+        out_shape=jax.ShapeDtypeStruct((rows, 128), jnp.float32),
+        compiler_params=PARAMS,
+        cost_estimate=pl.CostEstimate(flops=30_000, bytes_accessed=200_000, transcendentals=0),
+        name=name,
+    )(*arrays)
+
+
+def trade(array, axis):
+    return [array] + [lax.ppermute(array, AXES, trade_map(axis, d)) for d in (1, 2, 3)]
 
 
 def body(
@@ -475,36 +510,37 @@
     weight_rows = jnp.transpose(dist_weight)
     bias_rows = jnp.transpose(bias_weight)
 
-    pad = jnp.zeros((query_scalar.shape[0], CAT - sum(WIDTHS)), jnp.bfloat16)
-    own_keys = jnp.concatenate([key_scalar, key_points, value_scalar, value_points, pad], axis=1)
-    near_keys = lax.ppermute(own_keys, AXES, MIRROR)
-    own, same, other = own_logits(pair_rep, weight_rows, labels)
-    same, other, near_keys = lax.optimization_barrier((same, other, near_keys))
+    own, same, other, own_keys = own_logits(
+        pair_rep, weight_rows, labels, (key_scalar, key_points, value_scalar, value_points)
+    )
     same = lax.ppermute(same, AXES, FIRST_HOP)
     other = lax.ppermute(other, AXES, FIRST_HOP)
+    near_keys = lax.ppermute(own_keys, AXES, MIRROR)
+    same = lax.ppermute(same, AXES, SECOND_HOP[0])
+    other = lax.ppermute(other, AXES, SECOND_HOP[1])
+    pair_bias, pair_value, cot = pair_parts(pair_rep, cot_pair, bias_rows)
+    same, pair_bias = lax.optimization_barrier((same, pair_bias))
+    bins, term = bin_gradient(
+        pair_rep, own, same, other, labels, dist_bias.reshape(1, 64), mask_rows, residue_mask
+    )
+    term = term + lax.ppermute(term, AXES, CORE_SWAP)
+    near_keys, _ = lax.optimization_barrier((near_keys, term))
     far_keys = lax.ppermute(near_keys, AXES, CORE_SWAP)
-    weights, value_grad, cot, stats = attention_parts(
-        pair_rep,
+    weights, value_grad, stats = attention_parts(
         (query_scalar, query_points, cot_scalar, cot_points),
         near_keys,
         far_keys,
-        cot_pair,
-        bias_rows,
+        pair_bias,
+        pair_value,
         point_weight,
         mask_rows,
     )
-    same, other, stats = lax.optimization_barrier((same, other, stats))
-    same = lax.ppermute(same, AXES, SECOND_HOP[0])
-    other = lax.ppermute(other, AXES, SECOND_HOP[1])
-    two_stats = jnp.stack([stats, lax.ppermute(stats, AXES, Y_PAIR)])
-    stats = [two_stats] + [lax.ppermute(two_stats, AXES, shift_map(0, d)) for d in (1, 2, 3)]
-    same, other, stats = lax.optimization_barrier((same, other, stats))
-    bins, weight_term = bin_gradient(
-        pair_rep, own, same, other, labels, dist_bias.reshape(1, 64), mask_rows, residue_mask
-    )
-    weight_grad = jnp.transpose(sum_over_devices(weight_term))
-    pair_grad = pair_gradient(weights, value_grad, stats, bins, cot, weight_rows, bias_rows)
-    return (pair_grad, weight_grad)
+    message = packed(pack_kernel, BINS + STATS, "sum_z", stats, *trade(term, 2))
+    message = packed(pack_more_kernel, BINS + 2 * STATS, "sum_y", *trade(message, 1))
+    arrived = trade(message, 0)
+    pair_grad = pair_gradient(weights, value_grad, arrived, bins, cot, weight_rows, bias_rows)
+    own_sum, one, two, three = [a[:BINS] for a in arrived]
+    return (pair_grad, jnp.transpose((own_sum + two) + (one + three)))
 
 
 def solution(mesh):

time: 87.3 us -> 79.7 us (0.913)
  starting transfers between devices: 50.6 us -> 36 us
  waiting for transfers between devices: 12.3 us -> 23.4 us
  local copies, waits for them, and re-layouts: 3.4 us -> 0.08 us
    ppermute x14 -> x10, starting transfers between devices: 30.1 us -> 20.4 us  [the longest x9 17.3 us: trade(): lax.ppermute(array, AXES, trade_map(axis, d))]
    ppermute x1, waiting for transfers between devices: 0.01 us -> 5.81 us  [body(): same = lax.ppermute(same, AXES, FIRST_HOP)]
    ppermute x1, starting transfers between devices: 5.41 us -> 0.43 us  [body(): far_keys = lax.ppermute(near_keys, AXES, CORE_SWAP)]
    ppermute x1, waiting for transfers between devices: 0.01 us -> 4.97 us  [body(): other = lax.ppermute(other, AXES, SECOND_HOP[1])]
    ppermute x1, waiting for transfers between devices: 0.01 us -> 2.43 us  [body(): other = lax.ppermute(other, AXES, FIRST_HOP)]
    unnamed x32 -> x26, local copies, waits for them, and re-layouts: 2.27 us -> 0.08 us
    ppermute x1, starting transfers between devices: 2.05 us -> 3.96 us  [body(): same = lax.ppermute(same, AXES, FIRST_HOP)]
    ppermute x1, starting transfers between devices: 3.8 us -> 1.91 us  [body(): near_keys = lax.ppermute(own_keys, AXES, MIRROR)]
  transfers between devices with their start and end apart: 20 -> 16, of which waited for: 9 -> 9; matrix products, arithmetic and copies ran while one was open for 0% -> 0% of each run, Pallas kernels for 16% -> 12%
where the time goes in v3:
time: 79.7 us; the launch traced here: 78.2 us
  starting transfers between devices  36 us (45%)
  waiting for transfers between devices  23.4 us (29%)
  Pallas kernels  17.2 us (22%)
  between operations  0.87 us (1%)
    ppermute x9, starting transfers between devices, trade(): lax.ppermute(array, AXES, trade_map(axis, d))  17.3 us
    ppermute x9, waiting for transfers between devices, trade(): lax.ppermute(array, AXES, trade_map(axis, d))  9.34 us
    ppermute x1, waiting for transfers between devices, body(): same = lax.ppermute(same, AXES, FIRST_HOP)  5.81 us
    pallas_call x1, Pallas kernels, own_logits(): pl.pallas_call(logits_kernel, in_specs=[HBM] * (3 + len(keys)), out_specs...  5.4 us
    ppermute x1, waiting for transfers between devices, body(): other = lax.ppermute(other, AXES, SECOND_HOP[1])  4.97 us
    pallas_call x1, Pallas kernels, bin_gradient(): pl.pallas_call(bins_kernel, in_specs=[SMEM] + [VMEM] * 7, out_specs=[VMEM...  4.44 us
    ppermute x1, starting transfers between devices, body(): same = lax.ppermute(same, AXES, FIRST_HOP)  3.96 us
    ppermute x1, starting transfers between devices, body(): other = lax.ppermute(other, AXES, FIRST_HOP)  3.82 us
  transfers between devices with their start and end apart: 16, of which 9 were waited for; matrix products, arithmetic and copies ran while one was open for 0% of the time, Pallas kernels for 12%

profile of v3, /device:TPU:2, one launch (start us, length us, event | category | flops | bytes accessed | tf_op | source)
XLA Modules:
  0.0 78.2 jit_solution(5313685839983031378)
XLA Ops:
  0.7 5.4 %own_logits.1 = (f32[64,64,128]{2,1,0:T(8,128)}, s16[33,64,128]{2,1,0:T(8,128)(2,1)}, s16[33,64,128]{2,1,0:T(8,128)(2,1)}, bf16[64,896]{1,0:T(8,128)(2,1)}) custom-call(bf16[64,128,128]{2,1,0:T(8,128)(2,1)} %pair_ref.3, bf16[64,128]{1,0:T(8,128)(2,1)} %bitcast.6, s32[64,128]{1,0:T(8,128)} %labels_ref.1, bf16[64,192]{1,0:T(8,128)(2,1)} %refs_0_.2, ...), custom_call_target="tpu_custom_call" | custom-call | flops 200000000 | bytes 6000000 | tf_op jit(solution)/shard_map/own_logits/pallas_call | solution.py:205
  6.1 0.0 copy-start.1
  6.1 0.0 copy-start.2
  6.1 4.0 %collective-permute-start.1 = (s16[33,64,128]{2,1,0:T(8,128)(2,1)}, s16[33,64,128]{2,1,0:T(8,128)(2,1)S(1)}, u32[]{:S(2)}, u32[]{:S(2)}) collective-permute-start(s16[33,64,128]{2,1,0:T(8,128)(2,1)} %get-tuple-element.19), channel_id=1, source_target_pairs={{0,0},{8,10},{16,16},{24,9},{32,32},{40,8},{48,48},{56,11},{4,4},{... | collective-permute-start | bytes 1622024 | tf_op jit(solution)/shard_map/ppermute | solution.py:516
  10.1 3.8 %collective-permute-start.3 = (s16[33,64,128]{2,1,0:T(8,128)(2,1)}, s16[33,64,128]{2,1,0:T(8,128)(2,1)S(1)}, u32[]{:S(2)}, u32[]{:S(2)}) collective-permute-start(s16[33,64,128]{2,1,0:T(8,128)(2,1)} %get-tuple-element.22), channel_id=1, source_target_pairs={{0,0},{8,10},{16,16},{24,9},{32,32},{40,8},{48,48},{56,11},{4,4},{... | collective-permute-start | bytes 1622024 | tf_op jit(solution)/shard_map/ppermute | solution.py:517
  13.9 5.8 %collective-permute-done.1 = s16[33,64,128]{2,1,0:T(8,128)(2,1)S(1)} collective-permute-done((s16[33,64,128]{2,1,0:T(8,128)(2,1)}, s16[33,64,128]{2,1,0:T(8,128)(2,1)S(1)}, u32[]{:S(2)}, u32[]{:S(2)}) %collective-permute-start.1) | collective-permute-done | bytes 540704 | tf_op jit(solution)/shard_map/ppermute | solution.py:516
  19.7 3.4 %collective-permute-start.2 = (s16[33,64,128]{2,1,0:T(8,128)(2,1)S(1)}, s16[33,64,128]{2,1,0:T(8,128)(2,1)S(1)}, u32[]{:S(2)}, u32[]{:S(2)}) collective-permute-start(s16[33,64,128]{2,1,0:T(8,128)(2,1)S(1)} %collective-permute-done.1), channel_id=1, source_target_pairs={{0,0},{10,8},{16,1},{9,9},{32,2},{8,10},{48,3},{11,11},{4,64},{74,... | collective-permute-start | bytes 1622024 | tf_op jit(solution)/shard_map/ppermute | solution.py:519
  23.1 2.4 %collective-permute-done.3 = s16[33,64,128]{2,1,0:T(8,128)(2,1)S(1)} collective-permute-done((s16[33,64,128]{2,1,0:T(8,128)(2,1)}, s16[33,64,128]{2,1,0:T(8,128)(2,1)S(1)}, u32[]{:S(2)}, u32[]{:S(2)}) %collective-permute-start.3) | collective-permute-done | bytes 540704 | tf_op jit(solution)/shard_map/ppermute | solution.py:517
  25.5 2.2 %collective-permute-start.4 = (s16[33,64,128]{2,1,0:T(8,128)(2,1)S(1)}, s16[33,64,128]{2,1,0:T(8,128)(2,1)S(1)}, u32[]{:S(2)}, u32[]{:S(2)}) collective-permute-start(s16[33,64,128]{2,1,0:T(8,128)(2,1)S(1)} %collective-permute-done.3), channel_id=1, source_target_pairs={{0,8},{10,0},{16,9},{9,1},{32,10},{8,2},{48,11},{11,3},{4,72},{74,... | collective-permute-start | bytes 1622024 | tf_op jit(solution)/shard_map/ppermute | solution.py:520
  27.7 1.9 %collective-permute-start = (bf16[64,896]{1,0:T(8,128)(2,1)}, bf16[64,896]{1,0:T(8,128)(2,1)S(1)}, u32[]{:S(2)}, u32[]{:S(2)}) collective-permute-start(bf16[64,896]{1,0:T(8,128)(2,1)} %get-tuple-element.17), channel_id=1, source_target_pairs={{0,0},{8,8},{16,1},{24,9},{32,2},{40,10},{48,3},{56,11},{4,64},{12... | collective-permute-start | bytes 344072 | tf_op jit(solution)/shard_map/ppermute | solution.py:518
  29.6 2.4 %pair_parts.1 = (f32[64,16,128]{2,1,0:T(8,128)S(1)}, f32[64,16,128]{2,1,0:T(8,128)S(1)}, bf16[64,16,128]{2,1,0:T(8,128)(2,1)S(1)}) custom-call(bf16[64,128,128]{2,1,0:T(8,128)(2,1)S(1)} %copy-done, bf16[64,1536]{1,0:T(8,128)(2,1)S(1)} %copy-done.7, bf16[12,128]{1,0:T(8,128)(2,1)S(1)} %bitcast.10), custom_call_target="tpu_custom_call" | custom-call | flops 1000000000 | bytes 4000000 | tf_op jit(solution)/shard_map/pair_parts/pallas_call | solution.py:250
  32.0 5.0 %collective-permute-done.4.far_ref = s16[33,64,128]{2,1,0:T(8,128)(2,1)S(1)} collective-permute-done((s16[33,64,128]{2,1,0:T(8,128)(2,1)S(1)}, s16[33,64,128]{2,1,0:T(8,128)(2,1)S(1)}, u32[]{:S(2)}, u32[]{:S(2)}) %collective-permute-start.4) | collective-permute-done | bytes 540704 | tf_op jit(solution)/shard_map/ppermute | solution.py:520
  37.0 0.0 copy-start.9
  37.0 4.4 %bin_gradient.1 = (bf16[64,64,128]{2,1,0:T(8,128)(2,1)S(1)}, f32[64,128]{1,0:T(8,128)S(1)}) custom-call(s32[1024]{0:T(1024)S(1)} %copy-done.4, bf16[64,128,128]{2,1,0:T(8,128)(2,1)S(1)} %copy-done, f32[64,64,128]{2,1,0:T(8,128)S(1)} %copy-done.1, s32[64,128]{1,0:T(8,128)S(1)} %copy-done.2, s16[33,64,128]{2,1,0:T(8,128)(2,1)S(1)} %collective-permute-done.2.near_ref, ...), custom_call_target="tpu_custom_call" | custom-call | flops 200000000 | bytes 6000000 | tf_op jit(solution)/shard_map/bin_gradient/pallas_call | solution.py:395
  41.5 3.1 %collective-permute-start.5 = (f32[64,128]{1,0:T(8,128)S(1)}, f32[64,128]{1,0:T(8,128)S(1)}, u32[]{:S(2)}, u32[]{:S(2)}) collective-permute-start(f32[64,128]{1,0:T(8,128)S(1)} %get-tuple-element.23), channel_id=1, source_target_pairs={{0,8},{8,0},{16,24},{24,16},{32,40},{40,32},{48,56},{56,48},{4,12}... | collective-permute-start | bytes 98312 | tf_op jit(solution)/shard_map/ppermute | solution.py:526
  44.5 0.9 %collective-permute-done.5 = f32[64,128]{1,0:T(8,128)S(1)} collective-permute-done((f32[64,128]{1,0:T(8,128)S(1)}, f32[64,128]{1,0:T(8,128)S(1)}, u32[]{:S(2)}, u32[]{:S(2)}) %collective-permute-start.5) | collective-permute-done | bytes 32800 | tf_op jit(solution)/shard_map/ppermute | solution.py:526
  45.4 0.4 collective-permute-start.6
  45.8 3.5 %collective-permute-start.9 = (f32[64,128]{1,0:T(8,128)S(1)}, f32[64,128]{1,0:T(8,128)S(1)}, u32[]{:S(2)}, u32[]{:S(2)}) collective-permute-start(f32[64,128]{1,0:T(8,128)S(1)} %add.12.own_ref), channel_id=1, source_target_pairs={{0,48},{8,56},{16,32},{24,40},{32,16},{40,24},{48,0},{56,8},{4,52}... | collective-permute-start | bytes 98312 | tf_op jit(solution)/shard_map/ppermute | solution.py:488
  49.4 0.9 %collective-permute-start.7 = (f32[64,128]{1,0:T(8,128)S(1)}, f32[64,128]{1,0:T(8,128)S(1)}, u32[]{:S(2)}, u32[]{:S(2)}) collective-permute-start(f32[64,128]{1,0:T(8,128)S(1)} %add.12.own_ref), channel_id=1, source_target_pairs={{0,16},{8,24},{16,0},{24,8},{32,48},{40,56},{48,32},{56,40},{4,20}... | collective-permute-start | bytes 98312 | tf_op jit(solution)/shard_map/ppermute | solution.py:488
  50.3 2.7 %attention_parts.1 = (f32[64,16,128]{2,1,0:T(8,128)S(1)}, f32[64,16,128]{2,1,0:T(8,128)S(1)}, f32[24,128]{1,0:T(8,128)S(1)}) custom-call(f32[12]{0:T(128)S(1)} %copy-done.12, bf16[64,896]{1,0:T(8,128)(2,1)S(1)} %collective-permute-done.near_ref, bf16[64,896]{1,0:T(8,128)(2,1)S(1)} %collective-permute-done.6.far_ref, ...), custom_call_target="tpu_custom_call" | custom-call | flops 4000000000 | bytes 2000000 | tf_op jit(solution)/shard_map/attention_parts/pallas_call | solution.py:328
  53.0 1.8 %collective-permute-done.8.two_ref = f32[64,128]{1,0:T(8,128)S(1)} collective-permute-done((f32[64,128]{1,0:T(8,128)S(1)}, f32[64,128]{1,0:T(8,128)S(1)}, u32[]{:S(2)}, u32[]{:S(2)}) %collective-permute-start.8) | collective-permute-done | bytes 32800 | tf_op jit(solution)/shard_map/ppermute | solution.py:488
  54.8 3.1 %collective-permute-start.12 = (f32[88,128]{1,0:T(8,128)S(1)}, f32[88,128]{1,0:T(8,128)S(1)}, u32[]{:S(2)}, u32[]{:S(2)}) collective-permute-start(f32[88,128]{1,0:T(8,128)S(1)} %sum_z.1.own_ref), channel_id=1, source_target_pairs={{0,68},{8,76},{16,84},{24,92},{32,100},{40,108},{48,116},{56,124},... | collective-permute-start | bytes 135176 | tf_op jit(solution)/shard_map/ppermute | solution.py:488
  57.9 2.5 %collective-permute-start.11 = (f32[88,128]{1,0:T(8,128)S(1)}, f32[88,128]{1,0:T(8,128)S(1)}, u32[]{:S(2)}, u32[]{:S(2)}) collective-permute-start(f32[88,128]{1,0:T(8,128)S(1)} %sum_z.1.own_ref), channel_id=1, source_target_pairs={{0,64},{8,72},{16,80},{24,88},{32,96},{40,104},{48,112},{56,120},{... | collective-permute-start | bytes 135176 | tf_op jit(solution)/shard_map/ppermute | solution.py:488
  60.4 3.2 %collective-permute-done.11.two_ref = f32[88,128]{1,0:T(8,128)S(1)} collective-permute-done((f32[88,128]{1,0:T(8,128)S(1)}, f32[88,128]{1,0:T(8,128)S(1)}, u32[]{:S(2)}, u32[]{:S(2)}) %collective-permute-start.11) | collective-permute-done | bytes 45088 | tf_op jit(solution)/shard_map/ppermute | solution.py:488
  63.6 0.8 %collective-permute-done.10.one_ref = f32[88,128]{1,0:T(8,128)S(1)} collective-permute-done((f32[88,128]{1,0:T(8,128)S(1)}, f32[88,128]{1,0:T(8,128)S(1)}, u32[]{:S(2)}, u32[]{:S(2)}) %collective-permute-start.10) | collective-permute-done | bytes 45088 | tf_op jit(solution)/shard_map/ppermute | solution.py:488
  64.5 5.2 %collective-permute-start.15 = (f32[112,128]{1,0:T(8,128)S(1)}, f32[112,128]{1,0:T(8,128)S(1)}, u32[]{:S(2)}, u32[]{:S(2)}) collective-permute-start(f32[112,128]{1,0:T(8,128)S(1)} %sum_y.1.refs_0_), channel_id=1, source_target_pairs={{0,3},{8,11},{16,19},{24,27},{32,35},{40,43},{48,51},{56,59},{4,7}... | collective-permute-start | bytes 172040 | tf_op jit(solution)/shard_map/ppermute | solution.py:488
  69.7 0.6 collective-permute-start.14
  70.3 1.5 %collective-permute-start.13 = (f32[112,128]{1,0:T(8,128)S(1)}, f32[112,128]{1,0:T(8,128)S(1)}, u32[]{:S(2)}, u32[]{:S(2)}) collective-permute-start(f32[112,128]{1,0:T(8,128)S(1)} %sum_y.1.refs_0_), channel_id=1, source_target_pairs={{0,1},{8,9},{16,17},{24,25},{32,33},{40,41},{48,49},{56,57},{4,5},... | collective-permute-start | bytes 172040 | tf_op jit(solution)/shard_map/ppermute | solution.py:488
  71.8 0.6 collective-permute-done.15.refs_3_
  72.4 2.9 %collective-permute-done.14.refs_2_ = f32[112,128]{1,0:T(8,128)S(1)} collective-permute-done((f32[112,128]{1,0:T(8,128)S(1)}, f32[112,128]{1,0:T(8,128)S(1)}, u32[]{:S(2)}, u32[]{:S(2)}) %collective-permute-start.14) | collective-permute-done | bytes 57376 | tf_op jit(solution)/shard_map/ppermute | solution.py:488
  75.3 0.6 fusion.1
  76.0 2.2 %pair_gradient.1 = bf16[64,128,128]{2,1,0:T(8,128)(2,1)} custom-call(f32[64,16,128]{2,1,0:T(8,128)S(1)} %get-tuple-element.27.exp_ref, f32[64,16,128]{2,1,0:T(8,128)S(1)} %get-tuple-element.28.grad_ref, f32[112,128]{1,0:T(8,128)S(1)} %sum_y.1.refs_0_, f32[112,128]{1,0:T(8,128)S(1)} %collective-permute-done.13.refs_1_, ...), custom_call_target="tpu_custom_call" | custom-call | flops 300000000 | bytes 5000000 | tf_op jit(solution)/shard_map/pair_gradient/pallas_call | solution.py:449
  (35 shorter events, 0.1 us)
Async XLA Ops:
  0.6 29.0 %copy-start = (bf16[64,128,128]{2,1,0:T(8,128)(2,1)S(1)}, bf16[64,128,128]{2,1,0:T(8,128)(2,1)}, u32[]{:S(2)}) copy-start(bf16[64,128,128]{2,1,0:T(8,128)(2,1)} %pair_ref.3) | copy-start | bytes 6291460
  0.6 29.0 %copy-start.7 = (bf16[64,1536]{1,0:T(8,128)(2,1)S(1)}, bf16[64,1536]{1,0:T(8,128)(2,1)}, u32[]{:S(2)}) copy-start(bf16[64,1536]{1,0:T(8,128)(2,1)} %cot_ref.1) | copy-start | bytes 589828
  0.7 29.0 %copy-start.5 = (bf16[128,12]{0,1:T(8,128)(2,1)S(1)}, bf16[128,12]{0,1:T(8,128)(2,1)}, u32[]{:S(2)}) copy-start(bf16[128,12]{0,1:T(8,128)(2,1)} %param.21) | copy-start | bytes 9220
  6.1 30.9 %copy-start.1 = (f32[64,64,128]{2,1,0:T(8,128)S(1)}, f32[64,64,128]{2,1,0:T(8,128)}, u32[]{:S(2)}) copy-start(f32[64,64,128]{2,1,0:T(8,128)} %get-tuple-element.18.own_ref) | copy-start | bytes 6291460
  6.1 30.9 %copy-start.2 = (s32[64,128]{1,0:T(8,128)S(1)}, s32[64,128]{1,0:T(8,128)}, u32[]{:S(2)}) copy-start(s32[64,128]{1,0:T(8,128)} %labels_ref.1) | copy-start | bytes 98308
  6.1 30.9 %copy-start.4 = (s32[1024]{0:T(1024)S(1)}, s32[1024]{0:T(1024)}, u32[]{:S(2)}) copy-start(s32[1024]{0:T(1024)} %mask_smem.1) | copy-start | bytes 12292
  6.1 30.9 %copy-start.6 = (f32[64]{0:T(128)S(1)}, f32[64]{0:T(128)}, u32[]{:S(2)}) copy-start(f32[64]{0:T(128)} %param.20) | copy-start | bytes 772
  6.1 13.6 %collective-permute-start.1 = (s16[33,64,128]{2,1,0:T(8,128)(2,1)}, s16[33,64,128]{2,1,0:T(8,128)(2,1)S(1)}, u32[]{:S(2)}, u32[]{:S(2)}) collective-permute-start(s16[33,64,128]{2,1,0:T(8,128)(2,1)} %get-tuple-element.19), channel_id=1, source_target_pairs={{0,0},{8,10},{16,16},{24,9},{32,32},{40,8},{48,48},{56,11},{4,4},{... | collective-permute-start | bytes 1622024 | tf_op jit(solution)/shard_map/ppermute | solution.py:516
  10.1 15.4 %collective-permute-start.3 = (s16[33,64,128]{2,1,0:T(8,128)(2,1)}, s16[33,64,128]{2,1,0:T(8,128)(2,1)S(1)}, u32[]{:S(2)}, u32[]{:S(2)}) collective-permute-start(s16[33,64,128]{2,1,0:T(8,128)(2,1)} %get-tuple-element.22), channel_id=1, source_target_pairs={{0,0},{8,10},{16,16},{24,9},{32,32},{40,8},{48,48},{56,11},{4,4},{... | collective-permute-start | bytes 1622024 | tf_op jit(solution)/shard_map/ppermute | solution.py:517
  19.7 12.3 %collective-permute-start.2 = (s16[33,64,128]{2,1,0:T(8,128)(2,1)S(1)}, s16[33,64,128]{2,1,0:T(8,128)(2,1)S(1)}, u32[]{:S(2)}, u32[]{:S(2)}) collective-permute-start(s16[33,64,128]{2,1,0:T(8,128)(2,1)S(1)} %collective-permute-done.1), channel_id=1, source_target_pairs={{0,0},{10,8},{16,1},{9,9},{32,2},{8,10},{48,3},{11,11},{4,64},{74,... | collective-permute-start | bytes 1622024 | tf_op jit(solution)/shard_map/ppermute | solution.py:519
  25.5 11.4 %collective-permute-start.4 = (s16[33,64,128]{2,1,0:T(8,128)(2,1)S(1)}, s16[33,64,128]{2,1,0:T(8,128)(2,1)S(1)}, u32[]{:S(2)}, u32[]{:S(2)}) collective-permute-start(s16[33,64,128]{2,1,0:T(8,128)(2,1)S(1)} %collective-permute-done.3), channel_id=1, source_target_pairs={{0,8},{10,0},{16,9},{9,1},{32,10},{8,2},{48,11},{11,3},{4,72},{74,... | collective-permute-start | bytes 1622024 | tf_op jit(solution)/shard_map/ppermute | solution.py:520
  27.7 17.7 %collective-permute-start = (bf16[64,896]{1,0:T(8,128)(2,1)}, bf16[64,896]{1,0:T(8,128)(2,1)S(1)}, u32[]{:S(2)}, u32[]{:S(2)}) collective-permute-start(bf16[64,896]{1,0:T(8,128)(2,1)} %get-tuple-element.17), channel_id=1, source_target_pairs={{0,0},{8,8},{16,1},{24,9},{32,2},{40,10},{48,3},{56,11},{4,64},{12... | collective-permute-start | bytes 344072 | tf_op jit(solution)/shard_map/ppermute | solution.py:518
  37.0 13.3 %copy-start.8 = (bf16[64,288]{1,0:T(8,128)(2,1)S(1)}, bf16[64,288]{1,0:T(8,128)(2,1)}, u32[]{:S(2)}) copy-start(bf16[64,288]{1,0:T(8,128)(2,1)} %refs_3_.3) | copy-start | bytes 110596
  37.0 13.2 %copy-start.9 = (bf16[64,192]{1,0:T(8,128)(2,1)S(1)}, bf16[64,192]{1,0:T(8,128)(2,1)}, u32[]{:S(2)}) copy-start(bf16[64,192]{1,0:T(8,128)(2,1)} %refs_0_.3) | copy-start | bytes 73732
  37.0 13.2 %copy-start.10 = (bf16[64,144]{1,0:T(8,128)(2,1)S(1)}, bf16[64,144]{1,0:T(8,128)(2,1)}, u32[]{:S(2)}) copy-start(bf16[64,144]{1,0:T(8,128)(2,1)} %refs_1_.3) | copy-start | bytes 55300
  37.0 13.2 %copy-start.11 = (bf16[64,192]{1,0:T(8,128)(2,1)S(1)}, bf16[64,192]{1,0:T(8,128)(2,1)}, u32[]{:S(2)}) copy-start(bf16[64,192]{1,0:T(8,128)(2,1)} %refs_2_.3) | copy-start | bytes 73732
  37.0 13.2 %copy-start.12 = (f32[12]{0:T(128)S(1)}, f32[12]{0:T(128)}, u32[]{:S(2)}) copy-start(f32[12]{0:T(128)} %point_smem.1) | copy-start | bytes 148
  41.5 3.9 %collective-permute-start.5 = (f32[64,128]{1,0:T(8,128)S(1)}, f32[64,128]{1,0:T(8,128)S(1)}, u32[]{:S(2)}, u32[]{:S(2)}) collective-permute-start(f32[64,128]{1,0:T(8,128)S(1)} %get-tuple-element.23), channel_id=1, source_target_pairs={{0,8},{8,0},{16,24},{24,16},{32,40},{40,32},{48,56},{56,48},{4,12}... | collective-permute-start | bytes 98312 | tf_op jit(solution)/shard_map/ppermute | solution.py:526
  45.4 4.8 %collective-permute-start.6 = (bf16[64,896]{1,0:T(8,128)(2,1)S(1)}, bf16[64,896]{1,0:T(8,128)(2,1)S(1)}, u32[]{:S(2)}, u32[]{:S(2)}) collective-permute-start(bf16[64,896]{1,0:T(8,128)(2,1)S(1)} %collective-permute-done.near_ref), channel_id=1, source_target_pairs={{0,8},{8,0},{16,24},{24,16},{32,40},{40,32},{48,56},{56,48},{4,12}... | collective-permute-start | bytes 344072 | tf_op jit(solution)/shard_map/ppermute | solution.py:528
  45.8 7.2 %collective-permute-start.9 = (f32[64,128]{1,0:T(8,128)S(1)}, f32[64,128]{1,0:T(8,128)S(1)}, u32[]{:S(2)}, u32[]{:S(2)}) collective-permute-start(f32[64,128]{1,0:T(8,128)S(1)} %add.12.own_ref), channel_id=1, source_target_pairs={{0,48},{8,56},{16,32},{24,40},{32,16},{40,24},{48,0},{56,8},{4,52}... | collective-permute-start | bytes 98312 | tf_op jit(solution)/shard_map/ppermute | solution.py:488
  49.4 5.4 %collective-permute-start.8 = (f32[64,128]{1,0:T(8,128)S(1)}, f32[64,128]{1,0:T(8,128)S(1)}, u32[]{:S(2)}, u32[]{:S(2)}) collective-permute-start(f32[64,128]{1,0:T(8,128)S(1)} %add.12.own_ref), channel_id=1, source_target_pairs={{0,32},{8,40},{16,48},{24,56},{32,0},{40,8},{48,16},{56,24},{4,36}... | collective-permute-start | bytes 98312 | tf_op jit(solution)/shard_map/ppermute | solution.py:488
  49.4 5.4 %collective-permute-start.7 = (f32[64,128]{1,0:T(8,128)S(1)}, f32[64,128]{1,0:T(8,128)S(1)}, u32[]{:S(2)}, u32[]{:S(2)}) collective-permute-start(f32[64,128]{1,0:T(8,128)S(1)} %add.12.own_ref), channel_id=1, source_target_pairs={{0,16},{8,24},{16,0},{24,8},{32,48},{40,56},{48,32},{56,40},{4,20}... | collective-permute-start | bytes 98312 | tf_op jit(solution)/shard_map/ppermute | solution.py:488
  50.3 25.7 %copy-start.3 = (bf16[128,64]{0,1:T(8,128)(2,1)S(1)}, bf16[128,64]{0,1:T(8,128)(2,1)}, u32[]{:S(2)}) copy-start(bf16[128,64]{0,1:T(8,128)(2,1)} %param.19) | copy-start | bytes 49156
  54.8 5.6 %collective-permute-start.12 = (f32[88,128]{1,0:T(8,128)S(1)}, f32[88,128]{1,0:T(8,128)S(1)}, u32[]{:S(2)}, u32[]{:S(2)}) collective-permute-start(f32[88,128]{1,0:T(8,128)S(1)} %sum_z.1.own_ref), channel_id=1, source_target_pairs={{0,68},{8,76},{16,84},{24,92},{32,100},{40,108},{48,116},{56,124},... | collective-permute-start | bytes 135176 | tf_op jit(solution)/shard_map/ppermute | solution.py:488
  57.9 5.7 %collective-permute-start.11 = (f32[88,128]{1,0:T(8,128)S(1)}, f32[88,128]{1,0:T(8,128)S(1)}, u32[]{:S(2)}, u32[]{:S(2)}) collective-permute-start(f32[88,128]{1,0:T(8,128)S(1)} %sum_z.1.own_ref), channel_id=1, source_target_pairs={{0,64},{8,72},{16,80},{24,88},{32,96},{40,104},{48,112},{56,120},{... | collective-permute-start | bytes 135176 | tf_op jit(solution)/shard_map/ppermute | solution.py:488
  60.4 4.0 %collective-permute-start.10 = (f32[88,128]{1,0:T(8,128)S(1)}, f32[88,128]{1,0:T(8,128)S(1)}, u32[]{:S(2)}, u32[]{:S(2)}) collective-permute-start(f32[88,128]{1,0:T(8,128)S(1)} %sum_z.1.own_ref), channel_id=1, source_target_pairs={{0,4},{8,12},{16,20},{24,28},{32,36},{40,44},{48,52},{56,60},{4,0}... | collective-permute-start | bytes 135176 | tf_op jit(solution)/shard_map/ppermute | solution.py:488
  64.5 8.0 %collective-permute-start.15 = (f32[112,128]{1,0:T(8,128)S(1)}, f32[112,128]{1,0:T(8,128)S(1)}, u32[]{:S(2)}, u32[]{:S(2)}) collective-permute-start(f32[112,128]{1,0:T(8,128)S(1)} %sum_y.1.refs_0_), channel_id=1, source_target_pairs={{0,3},{8,11},{16,19},{24,27},{32,35},{40,43},{48,51},{56,59},{4,7}... | collective-permute-start | bytes 172040 | tf_op jit(solution)/shard_map/ppermute | solution.py:488
  69.7 5.7 %collective-permute-start.14 = (f32[112,128]{1,0:T(8,128)S(1)}, f32[112,128]{1,0:T(8,128)S(1)}, u32[]{:S(2)}, u32[]{:S(2)}) collective-permute-start(f32[112,128]{1,0:T(8,128)S(1)} %sum_y.1.refs_0_), channel_id=1, source_target_pairs={{0,2},{8,10},{16,18},{24,26},{32,34},{40,42},{48,50},{56,58},{4,6}... | collective-permute-start | bytes 172040 | tf_op jit(solution)/shard_map/ppermute | solution.py:488
  70.3 5.0 %collective-permute-start.13 = (f32[112,128]{1,0:T(8,128)S(1)}, f32[112,128]{1,0:T(8,128)S(1)}, u32[]{:S(2)}, u32[]{:S(2)}) collective-permute-start(f32[112,128]{1,0:T(8,128)S(1)} %sum_y.1.refs_0_), channel_id=1, source_target_pairs={{0,1},{8,9},{16,17},{24,25},{32,33},{40,41},{48,49},{56,57},{4,5},... | collective-permute-start | bytes 172040 | tf_op jit(solution)/shard_map/ppermute | solution.py:488

commit v4 on v3

--- a/solution.py
+++ b/solution.py
@@ -57,7 +57,6 @@
     ]
     for s in (0, 1)
 ]
-MIRROR = [(device_index(n, h), device_index(mirror_chip(n), h)) for n in CHIPS for h in (0, 1)]
 CORE_SWAP = [(device_index(n, h), device_index(n, 1 - h)) for n in CHIPS for h in (0, 1)]
 
 
@@ -411,7 +410,9 @@
 
 
 def output_kernel(exp_ref, grad_ref, *refs):
-    stats_refs, (bins_ref, cot_ref, weight_ref, bias_ref, out_hbm, out_ref, sent) = refs[:4], refs[4:]
+    stats_refs, (bins_ref, cot_ref, weight_ref, bias_ref, out_hbm, sum_ref, out_ref, sent) = refs[:4], refs[4:]
+    own_sum, one, two, three = [ref[:BINS] for ref in stats_refs]
+    sum_ref[...] = (own_sum + two) + (one + three)
     length = CHUNK * PAD_HEADS
     weight_t = weight_ref[...]
     bias_t = padded_heads(bias_ref)
@@ -449,8 +450,11 @@
     return pl.pallas_call(
         output_kernel,
         in_specs=[VMEM] * 10,
-        out_specs=HBM,
-        out_shape=jax.ShapeDtypeStruct((rows, 128, 128), jnp.bfloat16),
+        out_specs=[HBM, VMEM],
+        out_shape=[
+            jax.ShapeDtypeStruct((rows, 128, 128), jnp.bfloat16),
+            jax.ShapeDtypeStruct((BINS, 128), jnp.float32),
+        ],
         scratch_shapes=[
             pltpu.VMEM((rows, 128, 128), jnp.bfloat16),
             pltpu.SemaphoreType.DMA((rows // CHUNK,)),
@@ -515,10 +519,13 @@
     )
     same = lax.ppermute(same, AXES, FIRST_HOP)
     other = lax.ppermute(other, AXES, FIRST_HOP)
-    near_keys = lax.ppermute(own_keys, AXES, MIRROR)
+    near_keys = lax.ppermute(own_keys, AXES, FIRST_HOP)
+    other, near_keys = lax.optimization_barrier((other, near_keys))
+    bias_rows, _ = lax.optimization_barrier((bias_rows, other))
+    pair_bias, pair_value, cot = pair_parts(pair_rep, cot_pair, bias_rows)
     same = lax.ppermute(same, AXES, SECOND_HOP[0])
     other = lax.ppermute(other, AXES, SECOND_HOP[1])
-    pair_bias, pair_value, cot = pair_parts(pair_rep, cot_pair, bias_rows)
+    near_keys = lax.ppermute(near_keys, AXES, SECOND_HOP[0])
     same, pair_bias = lax.optimization_barrier((same, pair_bias))
     bins, term = bin_gradient(
         pair_rep, own, same, other, labels, dist_bias.reshape(1, 64), mask_rows, residue_mask
@@ -538,9 +545,8 @@
     message = packed(pack_kernel, BINS + STATS, "sum_z", stats, *trade(term, 2))
     message = packed(pack_more_kernel, BINS + 2 * STATS, "sum_y", *trade(message, 1))
     arrived = trade(message, 0)
-    pair_grad = pair_gradient(weights, value_grad, arrived, bins, cot, weight_rows, bias_rows)
-    own_sum, one, two, three = [a[:BINS] for a in arrived]
-    return (pair_grad, jnp.transpose((own_sum + two) + (one + three)))
+    pair_grad, weight_sum = pair_gradient(weights, value_grad, arrived, bins, cot, weight_rows, bias_rows)
+    return (pair_grad, jnp.transpose(weight_sum))
 
 
 def solution(mesh):

time: 79.7 us -> 76.1 us (0.955)
  waiting for transfers between devices: 23.4 us -> 17.9 us
  starting transfers between devices: 36 us -> 38.6 us
    ppermute x1 -> x2, starting transfers between devices: 1.91 us -> 5.89 us  [the longest x1 3.53 us: body(): near_keys = lax.ppermute(own_keys, AXES, FIRST_HOP)]
    ppermute x1 -> x2, waiting for transfers between devices: 0.01 us -> 3.66 us  [the longest x1 3.66 us: body(): near_keys = lax.ppermute(own_keys, AXES, FIRST_HOP)]
    ppermute x1, waiting for transfers between devices: 5.81 us -> 2.28 us  [body(): same = lax.ppermute(same, AXES, FIRST_HOP)]
    ppermute x1, waiting for transfers between devices: 4.97 us -> 2.1 us  [body(): other = lax.ppermute(other, AXES, SECOND_HOP[1])]
    ppermute x1, waiting for transfers between devices: 2.43 us -> 0.01 us  [body(): other = lax.ppermute(other, AXES, FIRST_HOP)]
    ppermute x1, starting transfers between devices: 3.06 us -> 1.12 us  [body(): term = term + lax.ppermute(term, AXES, CORE_SWAP)]
  transfers between devices with their start and end apart: 16 -> 17, of which waited for: 9 -> 10; matrix products, arithmetic and copies ran while one was open for 0% -> 0% of each run, Pallas kernels for 12% -> 13%
where the time goes in v4:
time: 76.1 us; the launch traced here: 75.3 us
  starting transfers between devices  38.6 us (51%)
  waiting for transfers between devices  17.9 us (24%)
  Pallas kernels  17.8 us (23%)
  between operations  0.88 us (1%)
    ppermute x9, starting transfers between devices, trade(): lax.ppermute(array, AXES, trade_map(axis, d))  17.2 us
    ppermute x9, waiting for transfers between devices, trade(): lax.ppermute(array, AXES, trade_map(axis, d))  9.02 us
    pallas_call x1, Pallas kernels, own_logits(): pl.pallas_call(logits_kernel, in_specs=[HBM] * (3 + len(keys)), out_specs...  5.4 us
    pallas_call x1, Pallas kernels, bin_gradient(): pl.pallas_call(bins_kernel, in_specs=[SMEM] + [VMEM] * 7, out_specs=[VMEM...  4.44 us
    ppermute x1, starting transfers between devices, body(): same = lax.ppermute(same, AXES, FIRST_HOP)  3.96 us
    ppermute x1, starting transfers between devices, body(): other = lax.ppermute(other, AXES, FIRST_HOP)  3.82 us
    ppermute x1, waiting for transfers between devices, body(): near_keys = lax.ppermute(own_keys, AXES, FIRST_HOP)  3.66 us
    ppermute x1, starting transfers between devices, body(): near_keys = lax.ppermute(own_keys, AXES, FIRST_HOP)  3.53 us
  transfers between devices with their start and end apart: 17, of which 10 were waited for; matrix products, arithmetic and copies ran while one was open for 0% of the time, Pallas kernels for 13%

profile of v4, /device:TPU:2, one launch (start us, length us, event | category | flops | bytes accessed | tf_op | source)
XLA Modules:
  0.0 75.3 jit_solution(3617402587310609406)
XLA Ops:
  0.7 5.4 %own_logits.1 = (f32[64,64,128]{2,1,0:T(8,128)}, s16[33,64,128]{2,1,0:T(8,128)(2,1)}, s16[33,64,128]{2,1,0:T(8,128)(2,1)}, bf16[64,896]{1,0:T(8,128)(2,1)}) custom-call(bf16[64,128,128]{2,1,0:T(8,128)(2,1)} %pair_ref.3, bf16[64,128]{1,0:T(8,128)(2,1)} %bitcast.5, s32[64,128]{1,0:T(8,128)} %labels_ref.1, bf16[64,192]{1,0:T(8,128)(2,1)} %refs_0_.2, ...), custom_call_target="tpu_custom_call" | custom-call | flops 200000000 | bytes 6000000 | tf_op jit(solution)/shard_map/own_logits/pallas_call | solution.py:204
  6.1 0.0 copy-start.1
  6.1 0.0 copy-start.2
  6.1 4.0 %collective-permute-start.3 = (s16[33,64,128]{2,1,0:T(8,128)(2,1)}, s16[33,64,128]{2,1,0:T(8,128)(2,1)S(1)}, u32[]{:S(2)}, u32[]{:S(2)}) collective-permute-start(s16[33,64,128]{2,1,0:T(8,128)(2,1)} %get-tuple-element.26), channel_id=1, source_target_pairs={{0,0},{8,10},{16,16},{24,9},{32,32},{40,8},{48,48},{56,11},{4,4},{... | collective-permute-start | bytes 1622024 | tf_op jit(solution)/shard_map/ppermute | solution.py:520
  10.1 3.8 %collective-permute-start = (s16[33,64,128]{2,1,0:T(8,128)(2,1)}, s16[33,64,128]{2,1,0:T(8,128)(2,1)S(1)}, u32[]{:S(2)}, u32[]{:S(2)}) collective-permute-start(s16[33,64,128]{2,1,0:T(8,128)(2,1)} %get-tuple-element.22), channel_id=1, source_target_pairs={{0,0},{8,10},{16,16},{24,9},{32,32},{40,8},{48,48},{56,11},{4,4},{... | collective-permute-start | bytes 1622024 | tf_op jit(solution)/shard_map/ppermute | solution.py:521
  13.9 3.5 %collective-permute-start.1 = (bf16[64,896]{1,0:T(8,128)(2,1)}, bf16[64,896]{1,0:T(8,128)(2,1)S(1)}, u32[]{:S(2)}, u32[]{:S(2)}) collective-permute-start(bf16[64,896]{1,0:T(8,128)(2,1)} %get-tuple-element.23), channel_id=1, source_target_pairs={{0,0},{8,10},{16,16},{24,9},{32,32},{40,8},{48,48},{56,11},{4,4},{... | collective-permute-start | bytes 344072 | tf_op jit(solution)/shard_map/ppermute | solution.py:522
  17.5 2.3 %collective-permute-done.3 = s16[33,64,128]{2,1,0:T(8,128)(2,1)S(1)} collective-permute-done((s16[33,64,128]{2,1,0:T(8,128)(2,1)}, s16[33,64,128]{2,1,0:T(8,128)(2,1)S(1)}, u32[]{:S(2)}, u32[]{:S(2)}) %collective-permute-start.3) | collective-permute-done | bytes 540704 | tf_op jit(solution)/shard_map/ppermute | solution.py:520
  19.7 3.4 %collective-permute-start.4 = (s16[33,64,128]{2,1,0:T(8,128)(2,1)S(1)}, s16[33,64,128]{2,1,0:T(8,128)(2,1)S(1)}, u32[]{:S(2)}, u32[]{:S(2)}) collective-permute-start(s16[33,64,128]{2,1,0:T(8,128)(2,1)S(1)} %collective-permute-done.3), channel_id=1, source_target_pairs={{0,0},{10,8},{16,1},{9,9},{32,2},{8,10},{48,3},{11,11},{4,64},{74,... | collective-permute-start | bytes 1622024 | tf_op jit(solution)/shard_map/ppermute | solution.py:526
  23.1 3.7 %collective-permute-done.1 = bf16[64,896]{1,0:T(8,128)(2,1)S(1)} collective-permute-done((bf16[64,896]{1,0:T(8,128)(2,1)}, bf16[64,896]{1,0:T(8,128)(2,1)S(1)}, u32[]{:S(2)}, u32[]{:S(2)}) %collective-permute-start.1) | collective-permute-done | bytes 114720 | tf_op jit(solution)/shard_map/ppermute | solution.py:522
  26.8 2.8 %collective-permute-start.5 = (s16[33,64,128]{2,1,0:T(8,128)(2,1)S(1)}, s16[33,64,128]{2,1,0:T(8,128)(2,1)S(1)}, u32[]{:S(2)}, u32[]{:S(2)}) collective-permute-start(s16[33,64,128]{2,1,0:T(8,128)(2,1)S(1)} %collective-permute-done), channel_id=1, source_target_pairs={{0,8},{10,0},{16,9},{9,1},{32,10},{8,2},{48,11},{11,3},{4,72},{74,... | collective-permute-start | bytes 1622024 | tf_op jit(solution)/shard_map/ppermute | solution.py:527
  29.6 2.4 %collective-permute-start.2 = (bf16[64,896]{1,0:T(8,128)(2,1)S(1)}, bf16[64,896]{1,0:T(8,128)(2,1)S(1)}, u32[]{:S(2)}, u32[]{:S(2)}) collective-permute-start(bf16[64,896]{1,0:T(8,128)(2,1)S(1)} %collective-permute-done.1), channel_id=1, source_target_pairs={{0,0},{10,8},{16,1},{9,9},{32,2},{8,10},{48,3},{11,11},{4,64},{74,... | collective-permute-start | bytes 344072 | tf_op jit(solution)/shard_map/ppermute | solution.py:528
  32.0 2.4 %pair_parts.1 = (f32[64,16,128]{2,1,0:T(8,128)S(1)}, f32[64,16,128]{2,1,0:T(8,128)S(1)}, bf16[64,16,128]{2,1,0:T(8,128)(2,1)S(1)}) custom-call(bf16[64,128,128]{2,1,0:T(8,128)(2,1)S(1)} %copy-done, bf16[64,1536]{1,0:T(8,128)(2,1)S(1)} %copy-done.7, bf16[12,128]{1,0:T(8,128)(2,1)S(1)} %bitcast.9), custom_call_target="tpu_custom_call" | custom-call | flops 1000000000 | bytes 4000000 | tf_op jit(solution)/shard_map/pair_parts/pallas_call | solution.py:249
  34.4 2.1 %collective-permute-done.5.far_ref = s16[33,64,128]{2,1,0:T(8,128)(2,1)S(1)} collective-permute-done((s16[33,64,128]{2,1,0:T(8,128)(2,1)S(1)}, s16[33,64,128]{2,1,0:T(8,128)(2,1)S(1)}, u32[]{:S(2)}, u32[]{:S(2)}) %collective-permute-start.5) | collective-permute-done | bytes 540704 | tf_op jit(solution)/shard_map/ppermute | solution.py:527
  36.5 4.4 %bin_gradient.1 = (bf16[64,64,128]{2,1,0:T(8,128)(2,1)S(1)}, f32[64,128]{1,0:T(8,128)S(1)}) custom-call(s32[1024]{0:T(1024)S(1)} %copy-done.4, bf16[64,128,128]{2,1,0:T(8,128)(2,1)S(1)} %copy-done, f32[64,64,128]{2,1,0:T(8,128)S(1)} %copy-done.1, s32[64,128]{1,0:T(8,128)S(1)} %copy-done.2, s16[33,64,128]{2,1,0:T(8,128)(2,1)S(1)} %collective-permute-done.4.near_ref, ...), custom_call_target="tpu_custom_call" | custom-call | flops 200000000 | bytes 6000000 | tf_op jit(solution)/shard_map/bin_gradient/pallas_call | solution.py:394
  41.0 1.1 %collective-permute-start.6 = (f32[64,128]{1,0:T(8,128)S(1)}, f32[64,128]{1,0:T(8,128)S(1)}, u32[]{:S(2)}, u32[]{:S(2)}) collective-permute-start(f32[64,128]{1,0:T(8,128)S(1)} %get-tuple-element.31), channel_id=1, source_target_pairs={{0,8},{8,0},{16,24},{24,16},{32,40},{40,32},{48,56},{56,48},{4,12}... | collective-permute-start | bytes 98312 | tf_op jit(solution)/shard_map/ppermute | solution.py:533
  42.1 0.9 %collective-permute-done.6 = f32[64,128]{1,0:T(8,128)S(1)} collective-permute-done((f32[64,128]{1,0:T(8,128)S(1)}, f32[64,128]{1,0:T(8,128)S(1)}, u32[]{:S(2)}, u32[]{:S(2)}) %collective-permute-start.6) | collective-permute-done | bytes 32800 | tf_op jit(solution)/shard_map/ppermute | solution.py:533
  43.0 0.4 collective-permute-start.7
  43.4 6.7 %collective-permute-start.10 = (f32[64,128]{1,0:T(8,128)S(1)}, f32[64,128]{1,0:T(8,128)S(1)}, u32[]{:S(2)}, u32[]{:S(2)}) collective-permute-start(f32[64,128]{1,0:T(8,128)S(1)} %add.3.own_ref), channel_id=1, source_target_pairs={{0,48},{8,56},{16,32},{24,40},{32,16},{40,24},{48,0},{56,8},{4,52}... | collective-permute-start | bytes 98312 | tf_op jit(solution)/shard_map/ppermute | solution.py:492
  50.0 0.9 %collective-permute-start.8 = (f32[64,128]{1,0:T(8,128)S(1)}, f32[64,128]{1,0:T(8,128)S(1)}, u32[]{:S(2)}, u32[]{:S(2)}) collective-permute-start(f32[64,128]{1,0:T(8,128)S(1)} %add.3.own_ref), channel_id=1, source_target_pairs={{0,16},{8,24},{16,0},{24,8},{32,48},{40,56},{48,32},{56,40},{4,20}... | collective-permute-start | bytes 98312 | tf_op jit(solution)/shard_map/ppermute | solution.py:492
  51.0 2.7 %attention_parts.1 = (f32[64,16,128]{2,1,0:T(8,128)S(1)}, f32[64,16,128]{2,1,0:T(8,128)S(1)}, f32[24,128]{1,0:T(8,128)S(1)}) custom-call(f32[12]{0:T(128)S(1)} %copy-done.12, bf16[64,896]{1,0:T(8,128)(2,1)S(1)} %collective-permute-done.2.near_ref, bf16[64,896]{1,0:T(8,128)(2,1)S(1)} %collective-permute-done.7.far_ref, ...), custom_call_target="tpu_custom_call" | custom-call | flops 4000000000 | bytes 2000000 | tf_op jit(solution)/shard_map/attention_parts/pallas_call | solution.py:327
  53.7 1.8 %collective-permute-done.9.two_ref = f32[64,128]{1,0:T(8,128)S(1)} collective-permute-done((f32[64,128]{1,0:T(8,128)S(1)}, f32[64,128]{1,0:T(8,128)S(1)}, u32[]{:S(2)}, u32[]{:S(2)}) %collective-permute-start.9) | collective-permute-done | bytes 32800 | tf_op jit(solution)/shard_map/ppermute | solution.py:492
  55.5 3.1 %collective-permute-start.13 = (f32[88,128]{1,0:T(8,128)S(1)}, f32[88,128]{1,0:T(8,128)S(1)}, u32[]{:S(2)}, u32[]{:S(2)}) collective-permute-start(f32[88,128]{1,0:T(8,128)S(1)} %sum_z.1.own_ref), channel_id=1, source_target_pairs={{0,68},{8,76},{16,84},{24,92},{32,100},{40,108},{48,116},{56,124},... | collective-permute-start | bytes 135176 | tf_op jit(solution)/shard_map/ppermute | solution.py:492
  58.6 2.4 %collective-permute-start.12 = (f32[88,128]{1,0:T(8,128)S(1)}, f32[88,128]{1,0:T(8,128)S(1)}, u32[]{:S(2)}, u32[]{:S(2)}) collective-permute-start(f32[88,128]{1,0:T(8,128)S(1)} %sum_z.1.own_ref), channel_id=1, source_target_pairs={{0,64},{8,72},{16,80},{24,88},{32,96},{40,104},{48,112},{56,120},{... | collective-permute-start | bytes 135176 | tf_op jit(solution)/shard_map/ppermute | solution.py:492
  61.0 3.3 %collective-permute-done.12.two_ref = f32[88,128]{1,0:T(8,128)S(1)} collective-permute-done((f32[88,128]{1,0:T(8,128)S(1)}, f32[88,128]{1,0:T(8,128)S(1)}, u32[]{:S(2)}, u32[]{:S(2)}) %collective-permute-start.12) | collective-permute-done | bytes 45088 | tf_op jit(solution)/shard_map/ppermute | solution.py:492
  64.3 0.7 collective-permute-done.11.one_ref
  65.1 0.1 collective-permute-start.16
  65.1 3.1 %collective-permute-start.15 = (f32[112,128]{1,0:T(8,128)S(1)}, f32[112,128]{1,0:T(8,128)S(1)}, u32[]{:S(2)}, u32[]{:S(2)}) collective-permute-start(f32[112,128]{1,0:T(8,128)S(1)} %sum_y.1.refs_0_), channel_id=1, source_target_pairs={{0,2},{8,10},{16,18},{24,26},{32,34},{40,42},{48,50},{56,58},{4,6}... | collective-permute-start | bytes 172040 | tf_op jit(solution)/shard_map/ppermute | solution.py:492
  68.3 1.0 %collective-permute-start.14 = (f32[112,128]{1,0:T(8,128)S(1)}, f32[112,128]{1,0:T(8,128)S(1)}, u32[]{:S(2)}, u32[]{:S(2)}) collective-permute-start(f32[112,128]{1,0:T(8,128)S(1)} %sum_y.1.refs_0_), channel_id=1, source_target_pairs={{0,1},{8,9},{16,17},{24,25},{32,33},{40,41},{48,49},{56,57},{4,5},... | collective-permute-start | bytes 172040 | tf_op jit(solution)/shard_map/ppermute | solution.py:492
  69.2 0.1 collective-permute-done.16.refs_3_
  69.3 1.6 %collective-permute-done.15.refs_2_ = f32[112,128]{1,0:T(8,128)S(1)} collective-permute-done((f32[112,128]{1,0:T(8,128)S(1)}, f32[112,128]{1,0:T(8,128)S(1)}, u32[]{:S(2)}, u32[]{:S(2)}) %collective-permute-start.15) | collective-permute-done | bytes 57376 | tf_op jit(solution)/shard_map/ppermute | solution.py:492
  70.9 1.5 %collective-permute-done.14.refs_1_ = f32[112,128]{1,0:T(8,128)S(1)} collective-permute-done((f32[112,128]{1,0:T(8,128)S(1)}, f32[112,128]{1,0:T(8,128)S(1)}, u32[]{:S(2)}, u32[]{:S(2)}) %collective-permute-start.14) | collective-permute-done | bytes 57376 | tf_op jit(solution)/shard_map/ppermute | solution.py:492
  72.4 2.8 %pair_gradient.1 = (bf16[64,128,128]{2,1,0:T(8,128)(2,1)}, f32[64,128]{1,0:T(8,128)}) custom-call(f32[64,16,128]{2,1,0:T(8,128)S(1)} %get-tuple-element.35.exp_ref, f32[64,16,128]{2,1,0:T(8,128)S(1)} %get-tuple-element.36.grad_ref, f32[112,128]{1,0:T(8,128)S(1)} %sum_y.1.refs_0_, f32[112,128]{1,0:T(8,128)S(1)} %collective-permute-done.14.refs_1_, ...), custom_call_target="tpu_custom_call" | custom-call | flops 300000000 | bytes 5000000 | tf_op jit(solution)/shard_map/pair_gradient/pallas_call | solution.py:450
  (36 shorter events, 0.1 us)
Async XLA Ops:
  0.6 31.3 %copy-start = (bf16[64,128,128]{2,1,0:T(8,128)(2,1)S(1)}, bf16[64,128,128]{2,1,0:T(8,128)(2,1)}, u32[]{:S(2)}) copy-start(bf16[64,128,128]{2,1,0:T(8,128)(2,1)} %pair_ref.3) | copy-start | bytes 6291460
  0.6 31.3 %copy-start.5 = (bf16[128,12]{0,1:T(8,128)(2,1)S(1)}, bf16[128,12]{0,1:T(8,128)(2,1)}, u32[]{:S(2)}) copy-start(bf16[128,12]{0,1:T(8,128)(2,1)} %param.21) | copy-start | bytes 9220
  0.7 31.3 %copy-start.7 = (bf16[64,1536]{1,0:T(8,128)(2,1)S(1)}, bf16[64,1536]{1,0:T(8,128)(2,1)}, u32[]{:S(2)}) copy-start(bf16[64,1536]{1,0:T(8,128)(2,1)} %cot_ref.1) | copy-start | bytes 589828
  6.1 30.4 %copy-start.1 = (f32[64,64,128]{2,1,0:T(8,128)S(1)}, f32[64,64,128]{2,1,0:T(8,128)}, u32[]{:S(2)}) copy-start(f32[64,64,128]{2,1,0:T(8,128)} %get-tuple-element.25.own_ref) | copy-start | bytes 6291460
  6.1 30.4 %copy-start.2 = (s32[64,128]{1,0:T(8,128)S(1)}, s32[64,128]{1,0:T(8,128)}, u32[]{:S(2)}) copy-start(s32[64,128]{1,0:T(8,128)} %labels_ref.1) | copy-start | bytes 98308
  6.1 30.4 %copy-start.4 = (s32[1024]{0:T(1024)S(1)}, s32[1024]{0:T(1024)}, u32[]{:S(2)}) copy-start(s32[1024]{0:T(1024)} %mask_smem.1) | copy-start | bytes 12292
  6.1 30.4 %copy-start.6 = (f32[64]{0:T(128)S(1)}, f32[64]{0:T(128)}, u32[]{:S(2)}) copy-start(f32[64]{0:T(128)} %param.20) | copy-start | bytes 772
  6.1 13.6 %collective-permute-start.3 = (s16[33,64,128]{2,1,0:T(8,128)(2,1)}, s16[33,64,128]{2,1,0:T(8,128)(2,1)S(1)}, u32[]{:S(2)}, u32[]{:S(2)}) collective-permute-start(s16[33,64,128]{2,1,0:T(8,128)(2,1)} %get-tuple-element.26), channel_id=1, source_target_pairs={{0,0},{8,10},{16,16},{24,9},{32,32},{40,8},{48,48},{56,11},{4,4},{... | collective-permute-start | bytes 1622024 | tf_op jit(solution)/shard_map/ppermute | solution.py:520
  10.1 16.7 %collective-permute-start = (s16[33,64,128]{2,1,0:T(8,128)(2,1)}, s16[33,64,128]{2,1,0:T(8,128)(2,1)S(1)}, u32[]{:S(2)}, u32[]{:S(2)}) collective-permute-start(s16[33,64,128]{2,1,0:T(8,128)(2,1)} %get-tuple-element.22), channel_id=1, source_target_pairs={{0,0},{8,10},{16,16},{24,9},{32,32},{40,8},{48,48},{56,11},{4,4},{... | collective-permute-start | bytes 1622024 | tf_op jit(solution)/shard_map/ppermute | solution.py:521
  13.9 12.8 %collective-permute-start.1 = (bf16[64,896]{1,0:T(8,128)(2,1)}, bf16[64,896]{1,0:T(8,128)(2,1)S(1)}, u32[]{:S(2)}, u32[]{:S(2)}) collective-permute-start(bf16[64,896]{1,0:T(8,128)(2,1)} %get-tuple-element.23), channel_id=1, source_target_pairs={{0,0},{8,10},{16,16},{24,9},{32,32},{40,8},{48,48},{56,11},{4,4},{... | collective-permute-start | bytes 344072 | tf_op jit(solution)/shard_map/ppermute | solution.py:522
  19.7 14.6 %collective-permute-start.4 = (s16[33,64,128]{2,1,0:T(8,128)(2,1)S(1)}, s16[33,64,128]{2,1,0:T(8,128)(2,1)S(1)}, u32[]{:S(2)}, u32[]{:S(2)}) collective-permute-start(s16[33,64,128]{2,1,0:T(8,128)(2,1)S(1)} %collective-permute-done.3), channel_id=1, source_target_pairs={{0,0},{10,8},{16,1},{9,9},{32,2},{8,10},{48,3},{11,11},{4,64},{74,... | collective-permute-start | bytes 1622024 | tf_op jit(solution)/shard_map/ppermute | solution.py:526
  26.8 9.7 %collective-permute-start.5 = (s16[33,64,128]{2,1,0:T(8,128)(2,1)S(1)}, s16[33,64,128]{2,1,0:T(8,128)(2,1)S(1)}, u32[]{:S(2)}, u32[]{:S(2)}) collective-permute-start(s16[33,64,128]{2,1,0:T(8,128)(2,1)S(1)} %collective-permute-done), channel_id=1, source_target_pairs={{0,8},{10,0},{16,9},{9,1},{32,10},{8,2},{48,11},{11,3},{4,72},{74,... | collective-permute-start | bytes 1622024 | tf_op jit(solution)/shard_map/ppermute | solution.py:527
  29.6 13.4 %collective-permute-start.2 = (bf16[64,896]{1,0:T(8,128)(2,1)S(1)}, bf16[64,896]{1,0:T(8,128)(2,1)S(1)}, u32[]{:S(2)}, u32[]{:S(2)}) collective-permute-start(bf16[64,896]{1,0:T(8,128)(2,1)S(1)} %collective-permute-done.1), channel_id=1, source_target_pairs={{0,0},{10,8},{16,1},{9,9},{32,2},{8,10},{48,3},{11,11},{4,64},{74,... | collective-permute-start | bytes 344072 | tf_op jit(solution)/shard_map/ppermute | solution.py:528
  36.5 14.4 %copy-start.8 = (bf16[64,288]{1,0:T(8,128)(2,1)S(1)}, bf16[64,288]{1,0:T(8,128)(2,1)}, u32[]{:S(2)}) copy-start(bf16[64,288]{1,0:T(8,128)(2,1)} %refs_3_.3) | copy-start | bytes 110596
  36.5 14.4 %copy-start.9 = (bf16[64,192]{1,0:T(8,128)(2,1)S(1)}, bf16[64,192]{1,0:T(8,128)(2,1)}, u32[]{:S(2)}) copy-start(bf16[64,192]{1,0:T(8,128)(2,1)} %refs_0_.3) | copy-start | bytes 73732
  36.5 14.4 %copy-start.10 = (bf16[64,144]{1,0:T(8,128)(2,1)S(1)}, bf16[64,144]{1,0:T(8,128)(2,1)}, u32[]{:S(2)}) copy-start(bf16[64,144]{1,0:T(8,128)(2,1)} %refs_1_.3) | copy-start | bytes 55300
  36.5 14.4 %copy-start.11 = (bf16[64,192]{1,0:T(8,128)(2,1)S(1)}, bf16[64,192]{1,0:T(8,128)(2,1)}, u32[]{:S(2)}) copy-start(bf16[64,192]{1,0:T(8,128)(2,1)} %refs_2_.3) | copy-start | bytes 73732
  36.5 14.4 %copy-start.12 = (f32[12]{0:T(128)S(1)}, f32[12]{0:T(128)}, u32[]{:S(2)}) copy-start(f32[12]{0:T(128)} %point_smem.1) | copy-start | bytes 148
  41.0 2.0 %collective-permute-start.6 = (f32[64,128]{1,0:T(8,128)S(1)}, f32[64,128]{1,0:T(8,128)S(1)}, u32[]{:S(2)}, u32[]{:S(2)}) collective-permute-start(f32[64,128]{1,0:T(8,128)S(1)} %get-tuple-element.31), channel_id=1, source_target_pairs={{0,8},{8,0},{16,24},{24,16},{32,40},{40,32},{48,56},{56,48},{4,12}... | collective-permute-start | bytes 98312 | tf_op jit(solution)/shard_map/ppermute | solution.py:533
  43.0 7.9 %collective-permute-start.7 = (bf16[64,896]{1,0:T(8,128)(2,1)S(1)}, bf16[64,896]{1,0:T(8,128)(2,1)S(1)}, u32[]{:S(2)}, u32[]{:S(2)}) collective-permute-start(bf16[64,896]{1,0:T(8,128)(2,1)S(1)} %collective-permute-done.2.near_ref), channel_id=1, source_target_pairs={{0,8},{8,0},{16,24},{24,16},{32,40},{40,32},{48,56},{56,48},{4,12}... | collective-permute-start | bytes 344072 | tf_op jit(solution)/shard_map/ppermute | solution.py:535
  43.4 10.3 %collective-permute-start.10 = (f32[64,128]{1,0:T(8,128)S(1)}, f32[64,128]{1,0:T(8,128)S(1)}, u32[]{:S(2)}, u32[]{:S(2)}) collective-permute-start(f32[64,128]{1,0:T(8,128)S(1)} %add.3.own_ref), channel_id=1, source_target_pairs={{0,48},{8,56},{16,32},{24,40},{32,16},{40,24},{48,0},{56,8},{4,52}... | collective-permute-start | bytes 98312 | tf_op jit(solution)/shard_map/ppermute | solution.py:492
  50.0 5.4 %collective-permute-start.9 = (f32[64,128]{1,0:T(8,128)S(1)}, f32[64,128]{1,0:T(8,128)S(1)}, u32[]{:S(2)}, u32[]{:S(2)}) collective-permute-start(f32[64,128]{1,0:T(8,128)S(1)} %add.3.own_ref), channel_id=1, source_target_pairs={{0,32},{8,40},{16,48},{24,56},{32,0},{40,8},{48,16},{56,24},{4,36}... | collective-permute-start | bytes 98312 | tf_op jit(solution)/shard_map/ppermute | solution.py:492
  50.0 5.4 %collective-permute-start.8 = (f32[64,128]{1,0:T(8,128)S(1)}, f32[64,128]{1,0:T(8,128)S(1)}, u32[]{:S(2)}, u32[]{:S(2)}) collective-permute-start(f32[64,128]{1,0:T(8,128)S(1)} %add.3.own_ref), channel_id=1, source_target_pairs={{0,16},{8,24},{16,0},{24,8},{32,48},{40,56},{48,32},{56,40},{4,20}... | collective-permute-start | bytes 98312 | tf_op jit(solution)/shard_map/ppermute | solution.py:492
  50.9 21.5 %copy-start.3 = (bf16[128,64]{0,1:T(8,128)(2,1)S(1)}, bf16[128,64]{0,1:T(8,128)(2,1)}, u32[]{:S(2)}) copy-start(bf16[128,64]{0,1:T(8,128)(2,1)} %param.19) | copy-start | bytes 49156
  55.5 5.5 %collective-permute-start.13 = (f32[88,128]{1,0:T(8,128)S(1)}, f32[88,128]{1,0:T(8,128)S(1)}, u32[]{:S(2)}, u32[]{:S(2)}) collective-permute-start(f32[88,128]{1,0:T(8,128)S(1)} %sum_z.1.own_ref), channel_id=1, source_target_pairs={{0,68},{8,76},{16,84},{24,92},{32,100},{40,108},{48,116},{56,124},... | collective-permute-start | bytes 135176 | tf_op jit(solution)/shard_map/ppermute | solution.py:492
  58.6 5.8 %collective-permute-start.12 = (f32[88,128]{1,0:T(8,128)S(1)}, f32[88,128]{1,0:T(8,128)S(1)}, u32[]{:S(2)}, u32[]{:S(2)}) collective-permute-start(f32[88,128]{1,0:T(8,128)S(1)} %sum_z.1.own_ref), channel_id=1, source_target_pairs={{0,64},{8,72},{16,80},{24,88},{32,96},{40,104},{48,112},{56,120},{... | collective-permute-start | bytes 135176 | tf_op jit(solution)/shard_map/ppermute | solution.py:492
  61.0 4.0 %collective-permute-start.11 = (f32[88,128]{1,0:T(8,128)S(1)}, f32[88,128]{1,0:T(8,128)S(1)}, u32[]{:S(2)}, u32[]{:S(2)}) collective-permute-start(f32[88,128]{1,0:T(8,128)S(1)} %sum_z.1.own_ref), channel_id=1, source_target_pairs={{0,4},{8,12},{16,20},{24,28},{32,36},{40,44},{48,52},{56,60},{4,0}... | collective-permute-start | bytes 135176 | tf_op jit(solution)/shard_map/ppermute | solution.py:492
  65.1 4.3 %collective-permute-start.16 = (f32[112,128]{1,0:T(8,128)S(1)}, f32[112,128]{1,0:T(8,128)S(1)}, u32[]{:S(2)}, u32[]{:S(2)}) collective-permute-start(f32[112,128]{1,0:T(8,128)S(1)} %sum_y.1.refs_0_), channel_id=1, source_target_pairs={{0,3},{8,11},{16,19},{24,27},{32,35},{40,43},{48,51},{56,59},{4,7}... | collective-permute-start | bytes 172040 | tf_op jit(solution)/shard_map/ppermute | solution.py:492
  65.1 5.8 %collective-permute-start.15 = (f32[112,128]{1,0:T(8,128)S(1)}, f32[112,128]{1,0:T(8,128)S(1)}, u32[]{:S(2)}, u32[]{:S(2)}) collective-permute-start(f32[112,128]{1,0:T(8,128)S(1)} %sum_y.1.refs_0_), channel_id=1, source_target_pairs={{0,2},{8,10},{16,18},{24,26},{32,34},{40,42},{48,50},{56,58},{4,6}... | collective-permute-start | bytes 172040 | tf_op jit(solution)/shard_map/ppermute | solution.py:492
  68.3 4.2 %collective-permute-start.14 = (f32[112,128]{1,0:T(8,128)S(1)}, f32[112,128]{1,0:T(8,128)S(1)}, u32[]{:S(2)}, u32[]{:S(2)}) collective-permute-start(f32[112,128]{1,0:T(8,128)S(1)} %sum_y.1.refs_0_), channel_id=1, source_target_pairs={{0,1},{8,9},{16,17},{24,25},{32,33},{40,41},{48,49},{56,57},{4,5},... | collective-permute-start | bytes 172040 | tf_op jit(solution)/shard_map/ppermute | solution.py:492

commit v5 on v3

--- a/solution.py
+++ b/solution.py
@@ -57,7 +57,6 @@
     ]
     for s in (0, 1)
 ]
-MIRROR = [(device_index(n, h), device_index(mirror_chip(n), h)) for n in CHIPS for h in (0, 1)]
 CORE_SWAP = [(device_index(n, h), device_index(n, 1 - h)) for n in CHIPS for h in (0, 1)]
 
 
@@ -132,19 +131,20 @@
 
 
 SLABS = 33
+KEY_SLABS = CAT // 128
 SLAB_PARTS = ((0, 8), (8, 16), (16, 24), (24, 33))
 
 
 def logits_kernel(pair_hbm, weight_hbm, labels_hbm, *refs):
-    keys_hbm, (own_hbm, same_hbm, other_hbm, cat_hbm) = refs[:4], refs[4:8]
-    pair_ref, weight_ref, labels_ref, own_ref, same_ref, other_ref, cat_ref, slabs, top = refs[8:17]
-    pair_sem, own_sem, slab_sem, small_sem = refs[17:21]
-    keys_refs = refs[21:]
+    keys_hbm, (own_hbm, same_hbm, other_hbm) = refs[:4], refs[4:7]
+    pair_ref, weight_ref, labels_ref, own_ref, same_ref, other_ref, cat_ref, slabs, top = refs[7:16]
+    pair_sem, own_sem, slab_sem, small_sem = refs[16:20]
+    keys_refs = refs[20:]
     copy = pltpu.make_async_copy
     weight_in = copy(weight_hbm, weight_ref, small_sem.at[0])
     small_in = [copy(labels_hbm, labels_ref, small_sem.at[1])]
     small_in += [copy(a, b, small_sem.at[3 + k]) for k, (a, b) in enumerate(zip(keys_hbm, keys_refs))]
-    cat_out = copy(cat_ref, cat_hbm, small_sem.at[2])
+    keys_out = copy(same_ref.at[pl.ds(SLABS, KEY_SLABS)], same_hbm.at[pl.ds(SLABS, KEY_SLABS)], small_sem.at[2])
     pair_in = chunk_copies(pair_hbm, pair_ref, pair_sem)
     own_out = chunk_copies(own_ref, own_hbm, own_sem)
     weight_in.start()
@@ -168,14 +168,28 @@
     for c in small_in:
         c.wait()
     lay_out(cat_ref, keys_refs)
-    cat_out.start()
+
+    def narrow(values):
+        return jnp.clip(jnp.round(values), -32767.0, 32767.0).astype(jnp.int32).astype(jnp.int16)
+
+    cat = cat_ref[...].astype(jnp.float32)
+    column = lax.broadcasted_iota(jnp.int32, cat.shape, 1)
+    coded = jnp.zeros_like(cat)
+    for part, width in enumerate(WIDTHS):
+        start = sum(WIDTHS[:part])
+        held = (column >= start) & (column < start + width)
+        largest = jnp.max(jnp.where(held, jnp.abs(cat), 0.0), axis=1, keepdims=True)
+        part_level = jnp.ceil(16.0 * jnp.log2(jnp.maximum(largest, 1e-30)))
+        coded = jnp.where(held, cat * (jnp.exp2(part_level * (-1.0 / 16.0)) * QUANT), coded)
+        coded = jnp.where(column == sum(WIDTHS) + part, part_level, coded)
+    coded = narrow(coded)
+    for k in range(KEY_SLABS):
+        same_ref[SLABS + k] = coded[:, k * 128 : (k + 1) * 128]
+    keys_out.start()
 
     core = own_core()
     level = jnp.ceil(16.0 * jnp.log2(jnp.maximum(top[...], 1e-30)))
     scale = jnp.exp2(level * (-1.0 / 16.0)) * QUANT
-
-    def narrow(values):
-        return jnp.clip(jnp.round(values), -32767.0, 32767.0).astype(jnp.int32).astype(jnp.int16)
 
     def put(slab, upper, lower):
         turned = jnp.transpose(jnp.concatenate([upper, lower], axis=0))
@@ -192,21 +206,22 @@
         for k, (ref, hbm) in enumerate(((same_ref, same_hbm), (other_ref, other_hbm))):
             slab_out.append(copy(ref.at[pl.ds(lo, hi - lo)], hbm.at[pl.ds(lo, hi - lo)], slab_sem.at[part, k]))
             slab_out[-1].start()
-    for c in own_out + slab_out + [cat_out]:
+    for c in own_out + slab_out + [keys_out]:
         c.wait()
 
 
 def own_logits(pair_tile, weight_rows, labels, keys):
     rows = pair_tile.shape[0]
-    block = jax.ShapeDtypeStruct((SLABS, 64, 128), jnp.int16)
+    same = jax.ShapeDtypeStruct((SLABS + KEY_SLABS, 64, 128), jnp.int16)
+    other = jax.ShapeDtypeStruct((SLABS, 64, 128), jnp.int16)
     cat = jax.ShapeDtypeStruct((rows, CAT), jnp.bfloat16)
     own = jax.ShapeDtypeStruct((rows, 64, 128), jnp.float32)
-    arrays = [pair_tile, weight_rows, labels, own, block, block, cat]
+    arrays = [pair_tile, weight_rows, labels, own, same, other, cat]
     return pl.pallas_call(
         logits_kernel,
         in_specs=[HBM] * (3 + len(keys)),
-        out_specs=[HBM] * 4,
-        out_shape=[own, block, block, cat],
+        out_specs=[HBM] * 3,
+        out_shape=[own, same, other],
         scratch_shapes=[pltpu.VMEM(a.shape, a.dtype) for a in arrays]
         + [
             pltpu.VMEM((64 * 64, 128), jnp.float32),
@@ -254,7 +269,7 @@
         out_shape=[part, part, jax.ShapeDtypeStruct((rows, PAD_HEADS, 128), jnp.bfloat16)],
         scratch_shapes=[pltpu.VMEM((768, 128), jnp.bfloat16)],
         compiler_params=PARAMS,
-        cost_estimate=pl.CostEstimate(flops=1_000_000_000, bytes_accessed=4_000_000, transcendentals=0),
+        cost_estimate=pl.CostEstimate(flops=300_000_000, bytes_accessed=4_000_000, transcendentals=0),
         name="pair_parts",
     )(pair_tile, cot_pair, bias_rows)
 
@@ -268,7 +283,21 @@
         return lax.broadcasted_iota(jnp.int32, shape, dim)
 
     core = own_core()
-    near, far = near_ref[...].astype(jnp.float32), far_ref[...].astype(jnp.float32)
+
+    def decoded(ref, first):
+        coded = jnp.concatenate(
+            [ref[first + k].astype(jnp.int32).astype(jnp.float32) for k in range(KEY_SLABS)], axis=1
+        )
+        column = iota(coded.shape, 1)
+        scale = jnp.zeros_like(coded)
+        for part, width in enumerate(WIDTHS):
+            start = sum(WIDTHS[:part])
+            at = sum(WIDTHS) + part
+            part_scale = jnp.exp2(coded[:, at : at + 1] * (1.0 / 16.0)) * (1.0 / QUANT)
+            scale = jnp.where((column >= start) & (column < start + width), part_scale, scale)
+        return coded * scale
+
+    near, far = decoded(near_ref, SLABS), decoded(far_ref, 0)
     keys[:64] = jnp.where(core == 0, near, far).astype(jnp.bfloat16)
     keys[64:] = jnp.where(core == 0, far, near).astype(jnp.bfloat16)
     lay_out(cat_ref, query_refs)
@@ -332,7 +361,7 @@
         out_shape=[part, part, jax.ShapeDtypeStruct((STATS, 128), jnp.float32)],
         scratch_shapes=[pltpu.VMEM((128, CAT), jnp.bfloat16), pltpu.VMEM((64, CAT), jnp.bfloat16)],
         compiler_params=PARAMS,
-        cost_estimate=pl.CostEstimate(flops=4_000_000_000, bytes_accessed=2_000_000, transcendentals=200_000),
+        cost_estimate=pl.CostEstimate(flops=500_000_000, bytes_accessed=2_000_000, transcendentals=200_000),
         name="attention_parts",
     )(point_weight, near, far, pair_bias, pair_value, mask_rows, *queries)
 
@@ -461,15 +490,16 @@
     )(weights, value_grad, *stats, bins, cot, weight_rows, bias_rows)
 
 
-def pack_kernel(stats_ref, own_ref, one_ref, two_ref, three_ref, out_ref):
-    out_ref[:BINS] = (own_ref[...] + two_ref[...]) + (one_ref[...] + three_ref[...])
+def pack_kernel(term_ref, swapped_ref, stats_ref, out_ref):
+    out_ref[:BINS] = term_ref[...] + swapped_ref[...]
     out_ref[BINS:] = stats_ref[...]
 
 
 def pack_more_kernel(own_ref, one_ref, two_ref, three_ref, out_ref):
     out_ref[:BINS] = (own_ref[:BINS] + two_ref[:BINS]) + (one_ref[:BINS] + three_ref[:BINS])
-    out_ref[BINS : BINS + STATS] = own_ref[BINS:]
-    out_ref[BINS + STATS :] = one_ref[BINS:]
+    if out_ref.shape[0] > BINS:
+        out_ref[BINS : BINS + STATS] = own_ref[BINS:]
+        out_ref[BINS + STATS :] = one_ref[BINS:]
 
 
 def packed(kernel, rows, name, *arrays):
@@ -510,36 +540,34 @@
     weight_rows = jnp.transpose(dist_weight)
     bias_rows = jnp.transpose(bias_weight)
 
-    own, same, other, own_keys = own_logits(
+    own, same, other = own_logits(
         pair_rep, weight_rows, labels, (key_scalar, key_points, value_scalar, value_points)
     )
     same = lax.ppermute(same, AXES, FIRST_HOP)
     other = lax.ppermute(other, AXES, FIRST_HOP)
-    near_keys = lax.ppermute(own_keys, AXES, MIRROR)
+    pair_bias, pair_value, cot = pair_parts(pair_rep, cot_pair, bias_rows)
+    same, pair_bias = lax.optimization_barrier((same, pair_bias))
     same = lax.ppermute(same, AXES, SECOND_HOP[0])
     other = lax.ppermute(other, AXES, SECOND_HOP[1])
-    pair_bias, pair_value, cot = pair_parts(pair_rep, cot_pair, bias_rows)
-    same, pair_bias = lax.optimization_barrier((same, pair_bias))
-    bins, term = bin_gradient(
-        pair_rep, own, same, other, labels, dist_bias.reshape(1, 64), mask_rows, residue_mask
-    )
-    term = term + lax.ppermute(term, AXES, CORE_SWAP)
-    near_keys, _ = lax.optimization_barrier((near_keys, term))
-    far_keys = lax.ppermute(near_keys, AXES, CORE_SWAP)
+    far_keys = lax.ppermute(same[SLABS:], AXES, CORE_SWAP)
     weights, value_grad, stats = attention_parts(
         (query_scalar, query_points, cot_scalar, cot_points),
-        near_keys,
+        same,
         far_keys,
         pair_bias,
         pair_value,
         point_weight,
         mask_rows,
     )
-    message = packed(pack_kernel, BINS + STATS, "sum_z", stats, *trade(term, 2))
+    same, stats = lax.optimization_barrier((same, stats))
+    bins, term = bin_gradient(
+        pair_rep, own, same, other, labels, dist_bias.reshape(1, 64), mask_rows, residue_mask
+    )
+    message = packed(pack_kernel, BINS + STATS, "sum_cores", term, lax.ppermute(term, AXES, CORE_SWAP), stats)
     message = packed(pack_more_kernel, BINS + 2 * STATS, "sum_y", *trade(message, 1))
     arrived = trade(message, 0)
+    own_sum, one, two, three = trade(packed(pack_more_kernel, BINS, "sum_x", *arrived), 2)
     pair_grad = pair_gradient(weights, value_grad, arrived, bins, cot, weight_rows, bias_rows)
-    own_sum, one, two, three = [a[:BINS] for a in arrived]
     return (pair_grad, jnp.transpose((own_sum + two) + (one + three)))
 
 

time: 79.7 us -> 73.1 us (0.917); the launches traced: 78.2 us -> 72.5 us
  starting transfers between devices: 36 us -> 30.6 us
    ppermute x1, waiting for transfers between devices: 0.01 us -> 5.42 us  [body(): same = lax.ppermute(same, AXES, SECOND_HOP[0])]
    ppermute x1, waiting for transfers between devices: 4.97 us -> 0.01 us  [body(): other = lax.ppermute(other, AXES, SECOND_HOP[1])]
    ppermute x3 -> x2, starting transfers between devices: 5.39 us -> 1.5 us  [the longest x1 1.42 us: body(): lax.ppermute(term, AXES, CORE_SWAP)]
    ppermute x9, starting transfers between devices: 17.3 us -> 15.9 us  [trade(): lax.ppermute(array, AXES, trade_map(axis, d))]
    ppermute x3 -> x2, waiting for transfers between devices: 0.87 us -> 2.17 us  [the longest x1 1.31 us: body(): far_keys = lax.ppermute(same[SLABS:], AXES, CORE_SWAP)]
    ppermute x1, waiting for transfers between devices: 5.81 us -> 4.61 us  [body(): same = lax.ppermute(same, AXES, FIRST_HOP)]
    ppermute x9, waiting for transfers between devices: 9.34 us -> 8.27 us  [trade(): lax.ppermute(array, AXES, trade_map(axis, d))]
  transfers between devices with their start and end apart: 16 -> 15, of which waited for: 9 -> 9; matrix products, arithmetic and copies ran while one was open for 0% -> 0% of each run, Pallas kernels for 12% -> 10%
where the time goes in v5:
time: 73.1 us; the launch traced here: 72.5 us
  starting transfers between devices  30.6 us (42%)
  waiting for transfers between devices  22.9 us (31%)
  Pallas kernels  17.5 us (24%)
  between operations  0.9 us (1%)
    ppermute x9, starting transfers between devices, trade(): lax.ppermute(array, AXES, trade_map(axis, d))  15.9 us
    ppermute x9, waiting for transfers between devices, trade(): lax.ppermute(array, AXES, trade_map(axis, d))  8.27 us
    pallas_call x1, Pallas kernels, own_logits(): pl.pallas_call(logits_kernel, in_specs=[HBM] * (3 + len(keys)), out_specs...  5.53 us
    ppermute x1, waiting for transfers between devices, body(): same = lax.ppermute(same, AXES, SECOND_HOP[0])  5.42 us
    ppermute x1, waiting for transfers between devices, body(): same = lax.ppermute(same, AXES, FIRST_HOP)  4.61 us
    pallas_call x1, Pallas kernels, bin_gradient(): pl.pallas_call(bins_kernel, in_specs=[SMEM] + [VMEM] * 7, out_specs=[VMEM...  4.51 us
    ppermute x1, starting transfers between devices, body(): other = lax.ppermute(other, AXES, FIRST_HOP)  3.83 us
    ppermute x1, starting transfers between devices, body(): same = lax.ppermute(same, AXES, FIRST_HOP)  3.82 us
  transfers between devices with their start and end apart: 15, of which 9 were waited for; matrix products, arithmetic and copies ran while one was open for 0% of the time, Pallas kernels for 10%

profile of v5, /device:TPU:2, one launch (start us, length us, event | category | flops | bytes accessed | tf_op | source)
XLA Modules:
  0.0 72.5 jit_solution(15137853392941615477)
XLA Ops:
  0.7 5.5 %own_logits.1 = (f32[64,64,128]{2,1,0:T(8,128)}, s16[40,64,128]{2,1,0:T(8,128)(2,1)}, s16[33,64,128]{2,1,0:T(8,128)(2,1)}) custom-call(bf16[64,128,128]{2,1,0:T(8,128)(2,1)} %pair_ref.3, bf16[64,128]{1,0:T(8,128)(2,1)} %bitcast.6, s32[64,128]{1,0:T(8,128)} %labels_ref.1, bf16[64,192]{1,0:T(8,128)(2,1)} %refs_0_.2, bf16[64,144]{1,0:T(8,128)(2,1)} %refs_1_.2, ...), custom_call_target="tpu_custom_call" | custom-call | flops 200000000 | bytes 6000000 | tf_op jit(solution)/shard_map/own_logits/pallas_call | solution.py:220
  6.3 3.8 %collective-permute-start = (s16[40,64,128]{2,1,0:T(8,128)(2,1)}, s16[40,64,128]{2,1,0:T(8,128)(2,1)S(1)}, u32[]{:S(2)}, u32[]{:S(2)}) collective-permute-start(s16[40,64,128]{2,1,0:T(8,128)(2,1)} %get-tuple-element.17), channel_id=1, source_target_pairs={{0,0},{8,10},{16,16},{24,9},{32,32},{40,8},{48,48},{56,11},{4,4},{... | collective-permute-start | bytes 1966088 | tf_op jit(solution)/shard_map/ppermute | solution.py:546
  10.1 3.8 %collective-permute-start.3 = (s16[33,64,128]{2,1,0:T(8,128)(2,1)}, s16[33,64,128]{2,1,0:T(8,128)(2,1)S(1)}, u32[]{:S(2)}, u32[]{:S(2)}) collective-permute-start(s16[33,64,128]{2,1,0:T(8,128)(2,1)} %get-tuple-element.27), channel_id=1, source_target_pairs={{0,0},{8,10},{16,16},{24,9},{32,32},{40,8},{48,48},{56,11},{4,4},{... | collective-permute-start | bytes 1622024 | tf_op jit(solution)/shard_map/ppermute | solution.py:547
  14.0 0.0 copy-start.1
  14.0 0.0 copy-start.3
  14.0 0.0 copy-start.12
  14.0 2.4 %pair_parts.1 = (f32[64,16,128]{2,1,0:T(8,128)S(1)}, f32[64,16,128]{2,1,0:T(8,128)S(1)}, bf16[64,16,128]{2,1,0:T(8,128)(2,1)S(1)}) custom-call(bf16[64,128,128]{2,1,0:T(8,128)(2,1)S(1)} %copy-done, bf16[64,1536]{1,0:T(8,128)(2,1)S(1)} %copy-done.2, bf16[12,128]{1,0:T(8,128)(2,1)S(1)} %bitcast.10), custom_call_target="tpu_custom_call" | custom-call | flops 300000000 | bytes 4000000 | tf_op jit(solution)/shard_map/pair_parts/pallas_call | solution.py:265
  16.4 4.6 %collective-permute-done = s16[40,64,128]{2,1,0:T(8,128)(2,1)S(1)} collective-permute-done((s16[40,64,128]{2,1,0:T(8,128)(2,1)}, s16[40,64,128]{2,1,0:T(8,128)(2,1)S(1)}, u32[]{:S(2)}, u32[]{:S(2)}) %collective-permute-start) | collective-permute-done | bytes 655392 | tf_op jit(solution)/shard_map/ppermute | solution.py:546
  21.0 3.4 %collective-permute-start.1 = (s16[40,64,128]{2,1,0:T(8,128)(2,1)S(1)}, s16[40,64,128]{2,1,0:T(8,128)(2,1)S(1)}, u32[]{:S(2)}, u32[]{:S(2)}) collective-permute-start(s16[40,64,128]{2,1,0:T(8,128)(2,1)S(1)} %collective-permute-done), channel_id=1, source_target_pairs={{0,0},{10,8},{16,1},{9,9},{32,2},{8,10},{48,3},{11,11},{4,64},{74,... | collective-permute-start | bytes 1966088 | tf_op jit(solution)/shard_map/ppermute | solution.py:550
  24.3 2.4 %collective-permute-done.3 = s16[33,64,128]{2,1,0:T(8,128)(2,1)S(1)} collective-permute-done((s16[33,64,128]{2,1,0:T(8,128)(2,1)}, s16[33,64,128]{2,1,0:T(8,128)(2,1)S(1)}, u32[]{:S(2)}, u32[]{:S(2)}) %collective-permute-start.3) | collective-permute-done | bytes 540704 | tf_op jit(solution)/shard_map/ppermute | solution.py:547
  26.8 2.2 %collective-permute-start.4 = (s16[33,64,128]{2,1,0:T(8,128)(2,1)S(1)}, s16[33,64,128]{2,1,0:T(8,128)(2,1)S(1)}, u32[]{:S(2)}, u32[]{:S(2)}) collective-permute-start(s16[33,64,128]{2,1,0:T(8,128)(2,1)S(1)} %collective-permute-done.3), channel_id=1, source_target_pairs={{0,8},{10,0},{16,9},{9,1},{32,10},{8,2},{48,11},{11,3},{4,72},{74,... | collective-permute-start | bytes 1622024 | tf_op jit(solution)/shard_map/ppermute | solution.py:551
  28.9 5.4 %collective-permute-done.1.near_ref = s16[40,64,128]{2,1,0:T(8,128)(2,1)S(1)} collective-permute-done((s16[40,64,128]{2,1,0:T(8,128)(2,1)S(1)}, s16[40,64,128]{2,1,0:T(8,128)(2,1)S(1)}, u32[]{:S(2)}, u32[]{:S(2)}) %collective-permute-start.1) | collective-permute-done | bytes 655392 | tf_op jit(solution)/shard_map/ppermute | solution.py:550
  34.4 0.1 collective-permute-start.2
  34.4 1.3 %collective-permute-done.2.far_ref = s16[7,64,128]{2,1,0:T(8,128)(2,1)S(1)} collective-permute-done((s16[7,64,128]{2,1,0:T(8,128)(2,1)S(1)}, s16[7,64,128]{2,1,0:T(8,128)(2,1)S(1)}, u32[]{:S(2)}, u32[]{:S(2)}) %collective-permute-start.2) | collective-permute-done | bytes 114720 | tf_op jit(solution)/shard_map/ppermute | solution.py:552
  35.8 2.8 %attention_parts.1 = (f32[64,16,128]{2,1,0:T(8,128)S(1)}, f32[64,16,128]{2,1,0:T(8,128)S(1)}, f32[24,128]{1,0:T(8,128)S(1)}) custom-call(f32[12]{0:T(128)S(1)} %copy-done.11, s16[40,64,128]{2,1,0:T(8,128)(2,1)S(1)} %collective-permute-done.1.near_ref, s16[7,64,128]{2,1,0:T(8,128)(2,1)S(1)} %collective-permute-done.2.far_ref, ...), custom_call_target="tpu_custom_call" | custom-call | flops 500000000 | bytes 2000000 | tf_op jit(solution)/shard_map/attention_parts/pallas_call | solution.py:357
  38.6 0.0 copy-done.3
  38.6 4.5 %bin_gradient.1 = (bf16[64,64,128]{2,1,0:T(8,128)(2,1)S(1)}, f32[64,128]{1,0:T(8,128)S(1)}) custom-call(s32[1024]{0:T(1024)S(1)} %copy-done.6, bf16[64,128,128]{2,1,0:T(8,128)(2,1)S(1)} %copy-done, f32[64,64,128]{2,1,0:T(8,128)S(1)} %copy-done.1, s32[64,128]{1,0:T(8,128)S(1)} %copy-done.3, s16[40,64,128]{2,1,0:T(8,128)(2,1)S(1)} %collective-permute-done.1.near_ref, ...), custom_call_target="tpu_custom_call" | custom-call | flops 200000000 | bytes 6000000 | tf_op jit(solution)/shard_map/bin_gradient/pallas_call | solution.py:424
  43.2 1.4 %collective-permute-start.5 = (f32[64,128]{1,0:T(8,128)S(1)}, f32[64,128]{1,0:T(8,128)S(1)}, u32[]{:S(2)}, u32[]{:S(2)}) collective-permute-start(f32[64,128]{1,0:T(8,128)S(1)} %get-tuple-element.28.term_ref), channel_id=1, source_target_pairs={{0,8},{8,0},{16,24},{24,16},{32,40},{40,32},{48,56},{56,48},{4,12}... | collective-permute-start | bytes 98312 | tf_op jit(solution)/shard_map/ppermute | solution.py:566
  44.6 0.9 %collective-permute-done.5.swapped_ref = f32[64,128]{1,0:T(8,128)S(1)} collective-permute-done((f32[64,128]{1,0:T(8,128)S(1)}, f32[64,128]{1,0:T(8,128)S(1)}, u32[]{:S(2)}, u32[]{:S(2)}) %collective-permute-start.5) | collective-permute-done | bytes 32800 | tf_op jit(solution)/shard_map/ppermute | solution.py:566
  45.4 3.0 %collective-permute-start.8 = (f32[88,128]{1,0:T(8,128)S(1)}, f32[88,128]{1,0:T(8,128)S(1)}, u32[]{:S(2)}, u32[]{:S(2)}) collective-permute-start(f32[88,128]{1,0:T(8,128)S(1)} %sum_cores.1.own_ref), channel_id=1, source_target_pairs={{0,68},{8,76},{16,84},{24,92},{32,100},{40,108},{48,116},{56,124},... | collective-permute-start | bytes 135176 | tf_op jit(solution)/shard_map/ppermute | solution.py:518
  48.5 1.5 %collective-permute-start.7 = (f32[88,128]{1,0:T(8,128)S(1)}, f32[88,128]{1,0:T(8,128)S(1)}, u32[]{:S(2)}, u32[]{:S(2)}) collective-permute-start(f32[88,128]{1,0:T(8,128)S(1)} %sum_cores.1.own_ref), channel_id=1, source_target_pairs={{0,64},{8,72},{16,80},{24,88},{32,96},{40,104},{48,112},{56,120},{... | collective-permute-start | bytes 135176 | tf_op jit(solution)/shard_map/ppermute | solution.py:518
  50.0 0.9 %collective-permute-done.8.three_ref = f32[88,128]{1,0:T(8,128)S(1)} collective-permute-done((f32[88,128]{1,0:T(8,128)S(1)}, f32[88,128]{1,0:T(8,128)S(1)}, u32[]{:S(2)}, u32[]{:S(2)}) %collective-permute-start.8) | collective-permute-done | bytes 45088 | tf_op jit(solution)/shard_map/ppermute | solution.py:518
  50.9 3.2 %collective-permute-done.7.two_ref = f32[88,128]{1,0:T(8,128)S(1)} collective-permute-done((f32[88,128]{1,0:T(8,128)S(1)}, f32[88,128]{1,0:T(8,128)S(1)}, u32[]{:S(2)}, u32[]{:S(2)}) %collective-permute-start.7) | collective-permute-done | bytes 45088 | tf_op jit(solution)/shard_map/ppermute | solution.py:518
  54.1 4.4 %collective-permute-start.11 = (f32[112,128]{1,0:T(8,128)S(1)}, f32[112,128]{1,0:T(8,128)S(1)}, u32[]{:S(2)}, u32[]{:S(2)}) collective-permute-start(f32[112,128]{1,0:T(8,128)S(1)} %sum_y.1.refs_0_.own_ref), channel_id=1, source_target_pairs={{0,3},{8,11},{16,19},{24,27},{32,35},{40,43},{48,51},{56,59},{4,7}... | collective-permute-start | bytes 172040 | tf_op jit(solution)/shard_map/ppermute | solution.py:518
  58.5 0.2 collective-permute-start.10
  58.8 1.9 %collective-permute-start.9 = (f32[112,128]{1,0:T(8,128)S(1)}, f32[112,128]{1,0:T(8,128)S(1)}, u32[]{:S(2)}, u32[]{:S(2)}) collective-permute-start(f32[112,128]{1,0:T(8,128)S(1)} %sum_y.1.refs_0_.own_ref), channel_id=1, source_target_pairs={{0,1},{8,9},{16,17},{24,25},{32,33},{40,41},{48,49},{56,57},{4,5},... | collective-permute-start | bytes 172040 | tf_op jit(solution)/shard_map/ppermute | solution.py:518
  60.7 3.5 %collective-permute-done.10.refs_2_.two_ref = f32[112,128]{1,0:T(8,128)S(1)} collective-permute-done((f32[112,128]{1,0:T(8,128)S(1)}, f32[112,128]{1,0:T(8,128)S(1)}, u32[]{:S(2)}, u32[]{:S(2)}) %collective-permute-start.10) | collective-permute-done | bytes 57376 | tf_op jit(solution)/shard_map/ppermute | solution.py:518
  64.2 2.2 %collective-permute-start.14 = (f32[64,128]{1,0:T(8,128)S(1)}, f32[64,128]{1,0:T(8,128)S(1)}, u32[]{:S(2)}, u32[]{:S(2)}) collective-permute-start(f32[64,128]{1,0:T(8,128)S(1)} %sum_x.1), channel_id=1, source_target_pairs={{0,48},{8,56},{16,32},{24,40},{32,16},{40,24},{48,0},{56,8},{4,52}... | collective-permute-start | bytes 98312 | tf_op jit(solution)/shard_map/ppermute | solution.py:518
  66.5 2.5 %collective-permute-start.12 = (f32[64,128]{1,0:T(8,128)S(1)}, f32[64,128]{1,0:T(8,128)S(1)}, u32[]{:S(2)}, u32[]{:S(2)}) collective-permute-start(f32[64,128]{1,0:T(8,128)S(1)} %sum_x.1), channel_id=1, source_target_pairs={{0,32},{8,40},{16,48},{24,56},{32,0},{40,8},{48,16},{56,24},{4,36}... | collective-permute-start | bytes 98312 | tf_op jit(solution)/shard_map/ppermute | solution.py:518
  69.0 2.2 %pair_gradient.1 = bf16[64,128,128]{2,1,0:T(8,128)(2,1)} custom-call(f32[64,16,128]{2,1,0:T(8,128)S(1)} %get-tuple-element.22.exp_ref, f32[64,16,128]{2,1,0:T(8,128)S(1)} %get-tuple-element.23.grad_ref, f32[112,128]{1,0:T(8,128)S(1)} %sum_y.1.refs_0_.own_ref, f32[112,128]{1,0:T(8,128)S(1)} %collective-permute-done.9.refs_1_.one_ref, ...), custom_call_target="tpu_custom_call" | custom-call | flops 300000000 | bytes 5000000 | tf_op jit(solution)/shard_map/pair_gradient/pallas_call | solution.py:478
  71.3 0.6 collective-permute-done.12
  71.9 0.6 add_bitcast_fusion
  (34 shorter events, 0.1 us)
Async XLA Ops:
  0.6 13.3 %copy-start = (bf16[64,128,128]{2,1,0:T(8,128)(2,1)S(1)}, bf16[64,128,128]{2,1,0:T(8,128)(2,1)}, u32[]{:S(2)}) copy-start(bf16[64,128,128]{2,1,0:T(8,128)(2,1)} %pair_ref.3) | copy-start | bytes 6291460
  0.6 13.3 %copy-start.2 = (bf16[64,1536]{1,0:T(8,128)(2,1)S(1)}, bf16[64,1536]{1,0:T(8,128)(2,1)}, u32[]{:S(2)}) copy-start(bf16[64,1536]{1,0:T(8,128)(2,1)} %cot_ref.1) | copy-start | bytes 589828
  0.7 13.3 %copy-start.10 = (bf16[128,12]{0,1:T(8,128)(2,1)S(1)}, bf16[128,12]{0,1:T(8,128)(2,1)}, u32[]{:S(2)}) copy-start(bf16[128,12]{0,1:T(8,128)(2,1)} %param.21) | copy-start | bytes 9220
  0.7 35.1 %copy-start.5 = (bf16[64,288]{1,0:T(8,128)(2,1)S(1)}, bf16[64,288]{1,0:T(8,128)(2,1)}, u32[]{:S(2)}) copy-start(bf16[64,288]{1,0:T(8,128)(2,1)} %refs_3_.3) | copy-start | bytes 110596
  0.7 35.1 %copy-start.6 = (s32[1024]{0:T(1024)S(1)}, s32[1024]{0:T(1024)}, u32[]{:S(2)}) copy-start(s32[1024]{0:T(1024)} %mask_smem.1) | copy-start | bytes 12292
  0.7 35.1 %copy-start.7 = (bf16[64,192]{1,0:T(8,128)(2,1)S(1)}, bf16[64,192]{1,0:T(8,128)(2,1)}, u32[]{:S(2)}) copy-start(bf16[64,192]{1,0:T(8,128)(2,1)} %refs_0_.3) | copy-start | bytes 73732
  0.7 35.1 %copy-start.8 = (bf16[64,144]{1,0:T(8,128)(2,1)S(1)}, bf16[64,144]{1,0:T(8,128)(2,1)}, u32[]{:S(2)}) copy-start(bf16[64,144]{1,0:T(8,128)(2,1)} %refs_1_.3) | copy-start | bytes 55300
  0.7 35.1 %copy-start.9 = (bf16[64,192]{1,0:T(8,128)(2,1)S(1)}, bf16[64,192]{1,0:T(8,128)(2,1)}, u32[]{:S(2)}) copy-start(bf16[64,192]{1,0:T(8,128)(2,1)} %refs_2_.3) | copy-start | bytes 73732
  0.7 35.1 %copy-start.11 = (f32[12]{0:T(128)S(1)}, f32[12]{0:T(128)}, u32[]{:S(2)}) copy-start(f32[12]{0:T(128)} %point_smem.1) | copy-start | bytes 148
  6.3 14.7 %collective-permute-start = (s16[40,64,128]{2,1,0:T(8,128)(2,1)}, s16[40,64,128]{2,1,0:T(8,128)(2,1)S(1)}, u32[]{:S(2)}, u32[]{:S(2)}) collective-permute-start(s16[40,64,128]{2,1,0:T(8,128)(2,1)} %get-tuple-element.17), channel_id=1, source_target_pairs={{0,0},{8,10},{16,16},{24,9},{32,32},{40,8},{48,48},{56,11},{4,4},{... | collective-permute-start | bytes 1966088 | tf_op jit(solution)/shard_map/ppermute | solution.py:546
  10.1 16.7 %collective-permute-start.3 = (s16[33,64,128]{2,1,0:T(8,128)(2,1)}, s16[33,64,128]{2,1,0:T(8,128)(2,1)S(1)}, u32[]{:S(2)}, u32[]{:S(2)}) collective-permute-start(s16[33,64,128]{2,1,0:T(8,128)(2,1)} %get-tuple-element.27), channel_id=1, source_target_pairs={{0,0},{8,10},{16,16},{24,9},{32,32},{40,8},{48,48},{56,11},{4,4},{... | collective-permute-start | bytes 1622024 | tf_op jit(solution)/shard_map/ppermute | solution.py:547
  14.0 24.6 %copy-start.1 = (f32[64,64,128]{2,1,0:T(8,128)S(1)}, f32[64,64,128]{2,1,0:T(8,128)}, u32[]{:S(2)}) copy-start(f32[64,64,128]{2,1,0:T(8,128)} %get-tuple-element.24.own_ref) | copy-start | bytes 6291460
  14.0 24.6 %copy-start.3 = (s32[64,128]{1,0:T(8,128)S(1)}, s32[64,128]{1,0:T(8,128)}, u32[]{:S(2)}) copy-start(s32[64,128]{1,0:T(8,128)} %labels_ref.1) | copy-start | bytes 98308
  14.0 24.6 %copy-start.12 = (f32[64]{0:T(128)S(1)}, f32[64]{0:T(128)}, u32[]{:S(2)}) copy-start(f32[64]{0:T(128)} %param.20) | copy-start | bytes 772
  21.0 13.4 %collective-permute-start.1 = (s16[40,64,128]{2,1,0:T(8,128)(2,1)S(1)}, s16[40,64,128]{2,1,0:T(8,128)(2,1)S(1)}, u32[]{:S(2)}, u32[]{:S(2)}) collective-permute-start(s16[40,64,128]{2,1,0:T(8,128)(2,1)S(1)} %collective-permute-done), channel_id=1, source_target_pairs={{0,0},{10,8},{16,1},{9,9},{32,2},{8,10},{48,3},{11,11},{4,64},{74,... | collective-permute-start | bytes 1966088 | tf_op jit(solution)/shard_map/ppermute | solution.py:550
  26.8 11.8 %collective-permute-start.4 = (s16[33,64,128]{2,1,0:T(8,128)(2,1)S(1)}, s16[33,64,128]{2,1,0:T(8,128)(2,1)S(1)}, u32[]{:S(2)}, u32[]{:S(2)}) collective-permute-start(s16[33,64,128]{2,1,0:T(8,128)(2,1)S(1)} %collective-permute-done.3), channel_id=1, source_target_pairs={{0,8},{10,0},{16,9},{9,1},{32,10},{8,2},{48,11},{11,3},{4,72},{74,... | collective-permute-start | bytes 1622024 | tf_op jit(solution)/shard_map/ppermute | solution.py:551
  34.4 1.4 %collective-permute-start.2 = (s16[7,64,128]{2,1,0:T(8,128)(2,1)S(1)}, s16[7,64,128]{2,1,0:T(8,128)(2,1)S(1)}, u32[]{:S(2)}, u32[]{:S(2)}) collective-permute-start(s16[7,64,128]{2,1,0:T(8,128)(2,1)S(1)} %slice.4), channel_id=1, source_target_pairs={{0,8},{8,0},{16,24},{24,16},{32,40},{40,32},{48,56},{56,48},{4,12}... | collective-permute-start | bytes 344072 | tf_op jit(solution)/shard_map/ppermute | solution.py:552
  38.6 30.4 %copy-start.4 = (bf16[128,64]{0,1:T(8,128)(2,1)S(1)}, bf16[128,64]{0,1:T(8,128)(2,1)}, u32[]{:S(2)}) copy-start(bf16[128,64]{0,1:T(8,128)(2,1)} %param.19) | copy-start | bytes 49156
  43.2 2.3 %collective-permute-start.5 = (f32[64,128]{1,0:T(8,128)S(1)}, f32[64,128]{1,0:T(8,128)S(1)}, u32[]{:S(2)}, u32[]{:S(2)}) collective-permute-start(f32[64,128]{1,0:T(8,128)S(1)} %get-tuple-element.28.term_ref), channel_id=1, source_target_pairs={{0,8},{8,0},{16,24},{24,16},{32,40},{40,32},{48,56},{56,48},{4,12}... | collective-permute-start | bytes 98312 | tf_op jit(solution)/shard_map/ppermute | solution.py:566
  45.4 5.4 %collective-permute-start.8 = (f32[88,128]{1,0:T(8,128)S(1)}, f32[88,128]{1,0:T(8,128)S(1)}, u32[]{:S(2)}, u32[]{:S(2)}) collective-permute-start(f32[88,128]{1,0:T(8,128)S(1)} %sum_cores.1.own_ref), channel_id=1, source_target_pairs={{0,68},{8,76},{16,84},{24,92},{32,100},{40,108},{48,116},{56,124},... | collective-permute-start | bytes 135176 | tf_op jit(solution)/shard_map/ppermute | solution.py:518
  48.5 5.6 %collective-permute-start.7 = (f32[88,128]{1,0:T(8,128)S(1)}, f32[88,128]{1,0:T(8,128)S(1)}, u32[]{:S(2)}, u32[]{:S(2)}) collective-permute-start(f32[88,128]{1,0:T(8,128)S(1)} %sum_cores.1.own_ref), channel_id=1, source_target_pairs={{0,64},{8,72},{16,80},{24,88},{32,96},{40,104},{48,112},{56,120},{... | collective-permute-start | bytes 135176 | tf_op jit(solution)/shard_map/ppermute | solution.py:518
  50.0 4.1 %collective-permute-start.6 = (f32[88,128]{1,0:T(8,128)S(1)}, f32[88,128]{1,0:T(8,128)S(1)}, u32[]{:S(2)}, u32[]{:S(2)}) collective-permute-start(f32[88,128]{1,0:T(8,128)S(1)} %sum_cores.1.own_ref), channel_id=1, source_target_pairs={{0,4},{8,12},{16,20},{24,28},{32,36},{40,44},{48,52},{56,60},{4,0}... | collective-permute-start | bytes 135176 | tf_op jit(solution)/shard_map/ppermute | solution.py:518
  54.1 6.6 %collective-permute-start.11 = (f32[112,128]{1,0:T(8,128)S(1)}, f32[112,128]{1,0:T(8,128)S(1)}, u32[]{:S(2)}, u32[]{:S(2)}) collective-permute-start(f32[112,128]{1,0:T(8,128)S(1)} %sum_y.1.refs_0_.own_ref), channel_id=1, source_target_pairs={{0,3},{8,11},{16,19},{24,27},{32,35},{40,43},{48,51},{56,59},{4,7}... | collective-permute-start | bytes 172040 | tf_op jit(solution)/shard_map/ppermute | solution.py:518
  58.5 5.7 %collective-permute-start.10 = (f32[112,128]{1,0:T(8,128)S(1)}, f32[112,128]{1,0:T(8,128)S(1)}, u32[]{:S(2)}, u32[]{:S(2)}) collective-permute-start(f32[112,128]{1,0:T(8,128)S(1)} %sum_y.1.refs_0_.own_ref), channel_id=1, source_target_pairs={{0,2},{8,10},{16,18},{24,26},{32,34},{40,42},{48,50},{56,58},{4,6}... | collective-permute-start | bytes 172040 | tf_op jit(solution)/shard_map/ppermute | solution.py:518
  58.8 5.5 %collective-permute-start.9 = (f32[112,128]{1,0:T(8,128)S(1)}, f32[112,128]{1,0:T(8,128)S(1)}, u32[]{:S(2)}, u32[]{:S(2)}) collective-permute-start(f32[112,128]{1,0:T(8,128)S(1)} %sum_y.1.refs_0_.own_ref), channel_id=1, source_target_pairs={{0,1},{8,9},{16,17},{24,25},{32,33},{40,41},{48,49},{56,57},{4,5},... | collective-permute-start | bytes 172040 | tf_op jit(solution)/shard_map/ppermute | solution.py:518
  64.2 7.0 %collective-permute-start.14 = (f32[64,128]{1,0:T(8,128)S(1)}, f32[64,128]{1,0:T(8,128)S(1)}, u32[]{:S(2)}, u32[]{:S(2)}) collective-permute-start(f32[64,128]{1,0:T(8,128)S(1)} %sum_x.1), channel_id=1, source_target_pairs={{0,48},{8,56},{16,32},{24,40},{32,16},{40,24},{48,0},{56,8},{4,52}... | collective-permute-start | bytes 98312 | tf_op jit(solution)/shard_map/ppermute | solution.py:518
  66.5 4.8 %collective-permute-start.13 = (f32[64,128]{1,0:T(8,128)S(1)}, f32[64,128]{1,0:T(8,128)S(1)}, u32[]{:S(2)}, u32[]{:S(2)}) collective-permute-start(f32[64,128]{1,0:T(8,128)S(1)} %sum_x.1), channel_id=1, source_target_pairs={{0,16},{8,24},{16,0},{24,8},{32,48},{40,56},{48,32},{56,40},{4,20}... | collective-permute-start | bytes 98312 | tf_op jit(solution)/shard_map/ppermute | solution.py:518
  66.5 5.4 %collective-permute-start.12 = (f32[64,128]{1,0:T(8,128)S(1)}, f32[64,128]{1,0:T(8,128)S(1)}, u32[]{:S(2)}, u32[]{:S(2)}) collective-permute-start(f32[64,128]{1,0:T(8,128)S(1)} %sum_x.1), channel_id=1, source_target_pairs={{0,32},{8,40},{16,48},{24,56},{32,0},{40,8},{48,16},{56,24},{4,36}... | collective-permute-start | bytes 98312 | tf_op jit(solution)/shard_map/ppermute | solution.py:518

commit v6 on v5

--- a/solution.py
+++ b/solution.py
@@ -65,7 +65,7 @@
     for n in CHIPS:
         m = list(n)
         m[axis] ^= bits
-        pairs += [(device_index(n, h), device_index(tuple(m), h)) for h in (0, 1)]
+        pairs += [(device_index(n, h), device_index(tuple(m), 1 - h)) for h in (0, 1)]
     return pairs
 
 
@@ -226,8 +226,8 @@
         + [
             pltpu.VMEM((64 * 64, 128), jnp.float32),
             pltpu.VMEM((64, 128), jnp.float32),
-            pltpu.SemaphoreType.DMA((8,)),
-            pltpu.SemaphoreType.DMA((8,)),
+            pltpu.SemaphoreType.DMA((4,)),
+            pltpu.SemaphoreType.DMA((4,)),
             pltpu.SemaphoreType.DMA((len(SLAB_PARTS), 2)),
             pltpu.SemaphoreType.DMA((3 + len(keys),)),
         ]
@@ -367,8 +367,8 @@
 
 
 def bins_kernel(
-    mask_smem, pair_ref, own_ref, labels_ref, near_ref, far_ref, bias_ref, mask_ref, bins_ref, weight_ref, mirror,
-    mirror_labels,
+    mask_smem, pair_ref, own_ref, labels_ref, near_ref, far_ref, bias_ref, mask_ref, stats_ref, bins_ref, weight_ref,
+    mirror, mirror_labels,
 ):
     core = own_core()
     low_lanes = lax.broadcasted_iota(jnp.int32, (64, 128), 1) < 64
@@ -392,7 +392,7 @@
         mirror[pl.ds(pl.multiple_of((b + 32) * 64, 64), 64), :] = lower * scale
         return carry
 
-    lax.fori_loop(0, 32, pair_of_bins, 0, unroll=8)
+    lax.fori_loop(0, 32, pair_of_bins, 0, unroll=32)
     bias = jnp.sum(eye(64, jnp.float32) * bias_ref[...], axis=1, keepdims=True)
     bias = jnp.broadcast_to(bias, (64, 128))
     column_mask = mask_ref[pl.ds(lax.axis_index("col"), 1), :].astype(jnp.float32)
@@ -416,18 +416,19 @@
             grads.append(grad)
         flat = pair_ref[step * CHUNK : (step + 1) * CHUNK].reshape(CHUNK * 128, 128)
         total += dot(jnp.concatenate(grads, axis=1), flat)
-    weight_ref[...] = total
-
-
-def bin_gradient(pair_tile, own, near, far, labels, dist_bias, mask_rows, residue_mask):
+    weight_ref[:BINS] = total
+    weight_ref[BINS:] = stats_ref[...]
+
+
+def bin_gradient(pair_tile, own, near, far, labels, dist_bias, mask_rows, residue_mask, stats):
     rows = pair_tile.shape[0]
     return pl.pallas_call(
         bins_kernel,
-        in_specs=[SMEM] + [VMEM] * 7,
+        in_specs=[SMEM] + [VMEM] * 8,
         out_specs=[VMEM, VMEM],
         out_shape=[
             jax.ShapeDtypeStruct((rows, 64, 128), jnp.bfloat16),
-            jax.ShapeDtypeStruct((64, 128), jnp.float32),
+            jax.ShapeDtypeStruct((BINS + STATS, 128), jnp.float32),
         ],
         scratch_shapes=[
             pltpu.VMEM((64 * 64, 128), jnp.float32),
@@ -436,15 +437,17 @@
         compiler_params=PARAMS,
         cost_estimate=pl.CostEstimate(flops=200_000_000, bytes_accessed=6_000_000, transcendentals=600_000),
         name="bin_gradient",
-    )(residue_mask, pair_tile, own, labels, near, far, dist_bias, mask_rows)
+    )(residue_mask, pair_tile, own, labels, near, far, dist_bias, mask_rows, stats)
 
 
 def output_kernel(exp_ref, grad_ref, *refs):
-    stats_refs, (bins_ref, cot_ref, weight_ref, bias_ref, out_hbm, out_ref, sent) = refs[:4], refs[4:]
+    core_ref, y_ref = refs[:2]
+    x_refs, (bins_ref, cot_ref, weight_ref, bias_ref, out_hbm, out_ref, sent) = refs[2:5], refs[5:]
     length = CHUNK * PAD_HEADS
     weight_t = weight_ref[...]
     bias_t = padded_heads(bias_ref)
-    places = [(ref, BINS + STATS * y) for ref in stats_refs for y in (0, 1)]
+    places = [(core_ref, FIRST.start), (y_ref, SECOND.start)]
+    places += [(ref, at.start) for ref in x_refs for at in (FIRST, SECOND)]
     tops = [ref[at : at + 8, :] for ref, at in places]
     totals = [ref[at + 8 : at + 16, :] for ref, at in places]
     weighted = [ref[at + 16 : at + 24, :] for ref, at in places]
@@ -477,7 +480,7 @@
     rows = bins.shape[0]
     return pl.pallas_call(
         output_kernel,
-        in_specs=[VMEM] * 10,
+        in_specs=[VMEM] * 11,
         out_specs=HBM,
         out_shape=jax.ShapeDtypeStruct((rows, 128, 128), jnp.bfloat16),
         scratch_shapes=[
@@ -490,16 +493,21 @@
     )(weights, value_grad, *stats, bins, cot, weight_rows, bias_rows)
 
 
-def pack_kernel(term_ref, swapped_ref, stats_ref, out_ref):
-    out_ref[:BINS] = term_ref[...] + swapped_ref[...]
-    out_ref[BINS:] = stats_ref[...]
+FIRST = slice(BINS, BINS + STATS)
+SECOND = slice(BINS + STATS, BINS + 2 * STATS)
+
+
+def pack_kernel(own_ref, swapped_ref, out_ref):
+    out_ref[:BINS] = own_ref[:BINS] + swapped_ref[:BINS]
+    out_ref[FIRST] = own_ref[FIRST]
+    out_ref[SECOND] = swapped_ref[FIRST]
 
 
 def pack_more_kernel(own_ref, one_ref, two_ref, three_ref, out_ref):
     out_ref[:BINS] = (own_ref[:BINS] + two_ref[:BINS]) + (one_ref[:BINS] + three_ref[:BINS])
     if out_ref.shape[0] > BINS:
-        out_ref[BINS : BINS + STATS] = own_ref[BINS:]
-        out_ref[BINS + STATS :] = one_ref[BINS:]
+        out_ref[FIRST] = own_ref[SECOND]
+        out_ref[SECOND] = one_ref[FIRST]
 
 
 def packed(kernel, rows, name, *arrays):
@@ -559,15 +567,15 @@
         point_weight,
         mask_rows,
     )
-    same, stats = lax.optimization_barrier((same, stats))
-    bins, term = bin_gradient(
-        pair_rep, own, same, other, labels, dist_bias.reshape(1, 64), mask_rows, residue_mask
+    bins, message = bin_gradient(
+        pair_rep, own, same, other, labels, dist_bias.reshape(1, 64), mask_rows, residue_mask, stats
     )
-    message = packed(pack_kernel, BINS + STATS, "sum_cores", term, lax.ppermute(term, AXES, CORE_SWAP), stats)
-    message = packed(pack_more_kernel, BINS + 2 * STATS, "sum_y", *trade(message, 1))
-    arrived = trade(message, 0)
-    own_sum, one, two, three = trade(packed(pack_more_kernel, BINS, "sum_x", *arrived), 2)
-    pair_grad = pair_gradient(weights, value_grad, arrived, bins, cot, weight_rows, bias_rows)
+    by_core = packed(pack_kernel, BINS + 2 * STATS, "sum_cores", message, lax.ppermute(message, AXES, CORE_SWAP))
+    by_y = trade(by_core, 1)
+    by_x = trade(packed(pack_more_kernel, BINS + 2 * STATS, "sum_y", *by_y), 0)
+    own_sum, one, two, three = trade(packed(pack_more_kernel, BINS, "sum_x", *by_x), 2)
+    stats = (by_core, by_y[1], *by_x[1:])
+    pair_grad = pair_gradient(weights, value_grad, stats, bins, cot, weight_rows, bias_rows)
     return (pair_grad, jnp.transpose((own_sum + two) + (one + three)))
 
 

time: 73.1 us -> 72 us (0.985)
  Pallas kernels: 17.5 us -> 16.6 us
  transfers between devices with their start and end apart: 15 -> 15, of which waited for: 9 -> 10; matrix products, arithmetic and copies ran while one was open for 0% -> 0% of each run, Pallas kernels for 10% -> 10%
where the time goes in v6:
time: 72 us; the launch traced here: 71 us
  starting transfers between devices  29.9 us (42%)
  waiting for transfers between devices  22.9 us (32%)
  Pallas kernels  16.6 us (23%)
  between operations  0.9 us (1%)
    ppermute x9, starting transfers between devices, trade(): lax.ppermute(array, AXES, trade_map(axis, d))  15.2 us
    ppermute x9, waiting for transfers between devices, trade(): lax.ppermute(array, AXES, trade_map(axis, d))  8.22 us
    ppermute x1, waiting for transfers between devices, body(): same = lax.ppermute(same, AXES, SECOND_HOP[0])  5.43 us
    pallas_call x1, Pallas kernels, own_logits(): pl.pallas_call(logits_kernel, in_specs=[HBM] * (3 + len(keys)), out_specs...  5.13 us
    ppermute x1, waiting for transfers between devices, body(): same = lax.ppermute(same, AXES, FIRST_HOP)  4.61 us
    pallas_call x1, Pallas kernels, bin_gradient(): pl.pallas_call(bins_kernel, in_specs=[SMEM] + [VMEM] * 8, out_specs=[VMEM...  4.07 us
    ppermute x1, starting transfers between devices, body(): other = lax.ppermute(other, AXES, FIRST_HOP)  3.83 us
    ppermute x1, starting transfers between devices, body(): same = lax.ppermute(same, AXES, FIRST_HOP)  3.83 us
  transfers between devices with their start and end apart: 15, of which 10 were waited for; matrix products, arithmetic and copies ran while one was open for 0% of the time, Pallas kernels for 10%

profile of v6, /device:TPU:2, one launch (start us, length us, event | category | flops | bytes accessed | tf_op | source)
XLA Modules:
  0.0 71.0 jit_solution(7794545028209895024)
XLA Ops:
  0.7 5.1 %own_logits.1 = (f32[64,64,128]{2,1,0:T(8,128)}, s16[40,64,128]{2,1,0:T(8,128)(2,1)}, s16[33,64,128]{2,1,0:T(8,128)(2,1)}) custom-call(bf16[64,128,128]{2,1,0:T(8,128)(2,1)} %pair_ref.3, bf16[64,128]{1,0:T(8,128)(2,1)} %bitcast.6, s32[64,128]{1,0:T(8,128)} %labels_ref.1, bf16[64,192]{1,0:T(8,128)(2,1)} %refs_0_.2, bf16[64,144]{1,0:T(8,128)(2,1)} %refs_1_.2, ...), custom_call_target="tpu_custom_call" | custom-call | flops 200000000 | bytes 6000000 | tf_op jit(solution)/shard_map/own_logits/pallas_call | solution.py:220
  5.9 3.8 %collective-permute-start = (s16[40,64,128]{2,1,0:T(8,128)(2,1)}, s16[40,64,128]{2,1,0:T(8,128)(2,1)S(1)}, u32[]{:S(2)}, u32[]{:S(2)}) collective-permute-start(s16[40,64,128]{2,1,0:T(8,128)(2,1)} %get-tuple-element.15), channel_id=1, source_target_pairs={{0,0},{8,10},{16,16},{24,9},{32,32},{40,8},{48,48},{56,11},{4,4},{... | collective-permute-start | bytes 1966088 | tf_op jit(solution)/shard_map/ppermute | solution.py:554
  9.7 3.8 %collective-permute-start.3 = (s16[33,64,128]{2,1,0:T(8,128)(2,1)}, s16[33,64,128]{2,1,0:T(8,128)(2,1)S(1)}, u32[]{:S(2)}, u32[]{:S(2)}) collective-permute-start(s16[33,64,128]{2,1,0:T(8,128)(2,1)} %get-tuple-element.23), channel_id=1, source_target_pairs={{0,0},{8,10},{16,16},{24,9},{32,32},{40,8},{48,48},{56,11},{4,4},{... | collective-permute-start | bytes 1622024 | tf_op jit(solution)/shard_map/ppermute | solution.py:555
  13.6 0.0 copy-start.1
  13.6 0.0 copy-start.3
  13.6 0.0 copy-start.12
  13.6 2.4 %pair_parts.1 = (f32[64,16,128]{2,1,0:T(8,128)S(1)}, f32[64,16,128]{2,1,0:T(8,128)S(1)}, bf16[64,16,128]{2,1,0:T(8,128)(2,1)S(1)}) custom-call(bf16[64,128,128]{2,1,0:T(8,128)(2,1)S(1)} %copy-done, bf16[64,1536]{1,0:T(8,128)(2,1)S(1)} %copy-done.2, bf16[12,128]{1,0:T(8,128)(2,1)S(1)} %bitcast.10), custom_call_target="tpu_custom_call" | custom-call | flops 300000000 | bytes 4000000 | tf_op jit(solution)/shard_map/pair_parts/pallas_call | solution.py:265
  16.0 4.6 %collective-permute-done = s16[40,64,128]{2,1,0:T(8,128)(2,1)S(1)} collective-permute-done((s16[40,64,128]{2,1,0:T(8,128)(2,1)}, s16[40,64,128]{2,1,0:T(8,128)(2,1)S(1)}, u32[]{:S(2)}, u32[]{:S(2)}) %collective-permute-start) | collective-permute-done | bytes 655392 | tf_op jit(solution)/shard_map/ppermute | solution.py:554
  20.6 3.4 %collective-permute-start.1 = (s16[40,64,128]{2,1,0:T(8,128)(2,1)S(1)}, s16[40,64,128]{2,1,0:T(8,128)(2,1)S(1)}, u32[]{:S(2)}, u32[]{:S(2)}) collective-permute-start(s16[40,64,128]{2,1,0:T(8,128)(2,1)S(1)} %collective-permute-done), channel_id=1, source_target_pairs={{0,0},{10,8},{16,1},{9,9},{32,2},{8,10},{48,3},{11,11},{4,64},{74,... | collective-permute-start | bytes 1966088 | tf_op jit(solution)/shard_map/ppermute | solution.py:558
  23.9 2.4 %collective-permute-done.3 = s16[33,64,128]{2,1,0:T(8,128)(2,1)S(1)} collective-permute-done((s16[33,64,128]{2,1,0:T(8,128)(2,1)}, s16[33,64,128]{2,1,0:T(8,128)(2,1)S(1)}, u32[]{:S(2)}, u32[]{:S(2)}) %collective-permute-start.3) | collective-permute-done | bytes 540704 | tf_op jit(solution)/shard_map/ppermute | solution.py:555
  26.4 2.1 %collective-permute-start.4 = (s16[33,64,128]{2,1,0:T(8,128)(2,1)S(1)}, s16[33,64,128]{2,1,0:T(8,128)(2,1)S(1)}, u32[]{:S(2)}, u32[]{:S(2)}) collective-permute-start(s16[33,64,128]{2,1,0:T(8,128)(2,1)S(1)} %collective-permute-done.3), channel_id=1, source_target_pairs={{0,8},{10,0},{16,9},{9,1},{32,10},{8,2},{48,11},{11,3},{4,72},{74,... | collective-permute-start | bytes 1622024 | tf_op jit(solution)/shard_map/ppermute | solution.py:559
  28.5 5.4 %collective-permute-done.1.near_ref = s16[40,64,128]{2,1,0:T(8,128)(2,1)S(1)} collective-permute-done((s16[40,64,128]{2,1,0:T(8,128)(2,1)S(1)}, s16[40,64,128]{2,1,0:T(8,128)(2,1)S(1)}, u32[]{:S(2)}, u32[]{:S(2)}) %collective-permute-start.1) | collective-permute-done | bytes 655392 | tf_op jit(solution)/shard_map/ppermute | solution.py:558
  34.0 0.1 collective-permute-start.2
  34.0 1.3 %collective-permute-done.2.far_ref = s16[7,64,128]{2,1,0:T(8,128)(2,1)S(1)} collective-permute-done((s16[7,64,128]{2,1,0:T(8,128)(2,1)S(1)}, s16[7,64,128]{2,1,0:T(8,128)(2,1)S(1)}, u32[]{:S(2)}, u32[]{:S(2)}) %collective-permute-start.2) | collective-permute-done | bytes 114720 | tf_op jit(solution)/shard_map/ppermute | solution.py:560
  35.4 2.8 %attention_parts.1 = (f32[64,16,128]{2,1,0:T(8,128)S(1)}, f32[64,16,128]{2,1,0:T(8,128)S(1)}, f32[24,128]{1,0:T(8,128)S(1)}) custom-call(f32[12]{0:T(128)S(1)} %copy-done.11, s16[40,64,128]{2,1,0:T(8,128)(2,1)S(1)} %collective-permute-done.1.near_ref, s16[7,64,128]{2,1,0:T(8,128)(2,1)S(1)} %collective-permute-done.2.far_ref, ...), custom_call_target="tpu_custom_call" | custom-call | flops 500000000 | bytes 2000000 | tf_op jit(solution)/shard_map/attention_parts/pallas_call | solution.py:357
  38.2 0.0 copy-done.3
  38.2 4.1 %bin_gradient.1 = (bf16[64,64,128]{2,1,0:T(8,128)(2,1)S(1)}, f32[88,128]{1,0:T(8,128)S(1)}) custom-call(s32[1024]{0:T(1024)S(1)} %copy-done.6, bf16[64,128,128]{2,1,0:T(8,128)(2,1)S(1)} %copy-done, f32[64,64,128]{2,1,0:T(8,128)S(1)} %copy-done.1, s32[64,128]{1,0:T(8,128)S(1)} %copy-done.3, s16[40,64,128]{2,1,0:T(8,128)(2,1)S(1)} %collective-permute-done.1.near_ref, ...), custom_call_target="tpu_custom_call" | custom-call | flops 200000000 | bytes 6000000 | tf_op jit(solution)/shard_map/bin_gradient/pallas_call | solution.py:425
  42.3 1.4 %collective-permute-start.5 = (f32[88,128]{1,0:T(8,128)S(1)}, f32[88,128]{1,0:T(8,128)S(1)}, u32[]{:S(2)}, u32[]{:S(2)}) collective-permute-start(f32[88,128]{1,0:T(8,128)S(1)} %get-tuple-element.25.own_ref), channel_id=1, source_target_pairs={{0,8},{8,0},{16,24},{24,16},{32,40},{40,32},{48,56},{56,48},{4,12}... | collective-permute-start | bytes 135176 | tf_op jit(solution)/shard_map/ppermute | solution.py:573
  43.7 0.9 %collective-permute-done.5.swapped_ref = f32[88,128]{1,0:T(8,128)S(1)} collective-permute-done((f32[88,128]{1,0:T(8,128)S(1)}, f32[88,128]{1,0:T(8,128)S(1)}, u32[]{:S(2)}, u32[]{:S(2)}) %collective-permute-start.5) | collective-permute-done | bytes 45088 | tf_op jit(solution)/shard_map/ppermute | solution.py:573
  44.6 3.1 %collective-permute-start.8 = (f32[112,128]{1,0:T(8,128)S(1)}, f32[112,128]{1,0:T(8,128)S(1)}, u32[]{:S(2)}, u32[]{:S(2)}) collective-permute-start(f32[112,128]{1,0:T(8,128)S(1)} %sum_cores.1.own_ref.refs_0_), channel_id=1, source_target_pairs={{0,76},{8,68},{16,92},{24,84},{32,108},{40,100},{48,124},{56,116},... | collective-permute-start | bytes 172040 | tf_op jit(solution)/shard_map/ppermute | solution.py:526
  47.7 1.2 %collective-permute-start.7 = (f32[112,128]{1,0:T(8,128)S(1)}, f32[112,128]{1,0:T(8,128)S(1)}, u32[]{:S(2)}, u32[]{:S(2)}) collective-permute-start(f32[112,128]{1,0:T(8,128)S(1)} %sum_cores.1.own_ref.refs_0_), channel_id=1, source_target_pairs={{0,72},{8,64},{16,88},{24,80},{32,104},{40,96},{48,120},{56,112},{... | collective-permute-start | bytes 172040 | tf_op jit(solution)/shard_map/ppermute | solution.py:526
  48.9 1.7 %collective-permute-done.8.three_ref = f32[112,128]{1,0:T(8,128)S(1)} collective-permute-done((f32[112,128]{1,0:T(8,128)S(1)}, f32[112,128]{1,0:T(8,128)S(1)}, u32[]{:S(2)}, u32[]{:S(2)}) %collective-permute-start.8) | collective-permute-done | bytes 57376 | tf_op jit(solution)/shard_map/ppermute | solution.py:526
  50.6 2.5 %collective-permute-done.7.two_ref = f32[112,128]{1,0:T(8,128)S(1)} collective-permute-done((f32[112,128]{1,0:T(8,128)S(1)}, f32[112,128]{1,0:T(8,128)S(1)}, u32[]{:S(2)}, u32[]{:S(2)}) %collective-permute-start.7) | collective-permute-done | bytes 57376 | tf_op jit(solution)/shard_map/ppermute | solution.py:526
  53.2 4.1 %collective-permute-start.11 = (f32[112,128]{1,0:T(8,128)S(1)}, f32[112,128]{1,0:T(8,128)S(1)}, u32[]{:S(2)}, u32[]{:S(2)}) collective-permute-start(f32[112,128]{1,0:T(8,128)S(1)} %sum_y.1.own_ref), channel_id=1, source_target_pairs={{0,11},{8,3},{16,27},{24,19},{32,43},{40,35},{48,59},{56,51},{4,15... | collective-permute-start | bytes 172040 | tf_op jit(solution)/shard_map/ppermute | solution.py:526
  57.3 2.2 %collective-permute-start.9 = (f32[112,128]{1,0:T(8,128)S(1)}, f32[112,128]{1,0:T(8,128)S(1)}, u32[]{:S(2)}, u32[]{:S(2)}) collective-permute-start(f32[112,128]{1,0:T(8,128)S(1)} %sum_y.1.own_ref), channel_id=1, source_target_pairs={{0,9},{8,1},{16,25},{24,17},{32,41},{40,33},{48,57},{56,49},{4,13}... | collective-permute-start | bytes 172040 | tf_op jit(solution)/shard_map/ppermute | solution.py:526
  59.5 3.0 %collective-permute-done.10.refs_3_.two_ref = f32[112,128]{1,0:T(8,128)S(1)} collective-permute-done((f32[112,128]{1,0:T(8,128)S(1)}, f32[112,128]{1,0:T(8,128)S(1)}, u32[]{:S(2)}, u32[]{:S(2)}) %collective-permute-start.10) | collective-permute-done | bytes 57376 | tf_op jit(solution)/shard_map/ppermute | solution.py:526
  62.5 0.4 collective-permute-done.9.refs_2_.one_ref
  62.9 2.4 %collective-permute-start.14 = (f32[64,128]{1,0:T(8,128)S(1)}, f32[64,128]{1,0:T(8,128)S(1)}, u32[]{:S(2)}, u32[]{:S(2)}) collective-permute-start(f32[64,128]{1,0:T(8,128)S(1)} %sum_x.1), channel_id=1, source_target_pairs={{0,56},{8,48},{16,40},{24,32},{32,24},{40,16},{48,8},{56,0},{4,60}... | collective-permute-start | bytes 98312 | tf_op jit(solution)/shard_map/ppermute | solution.py:526
  65.3 2.2 %collective-permute-start.12 = (f32[64,128]{1,0:T(8,128)S(1)}, f32[64,128]{1,0:T(8,128)S(1)}, u32[]{:S(2)}, u32[]{:S(2)}) collective-permute-start(f32[64,128]{1,0:T(8,128)S(1)} %sum_x.1), channel_id=1, source_target_pairs={{0,40},{8,32},{16,56},{24,48},{32,8},{40,0},{48,24},{56,16},{4,44}... | collective-permute-start | bytes 98312 | tf_op jit(solution)/shard_map/ppermute | solution.py:526
  67.5 2.2 %pair_gradient.1 = bf16[64,128,128]{2,1,0:T(8,128)(2,1)} custom-call(f32[64,16,128]{2,1,0:T(8,128)S(1)} %get-tuple-element.20.exp_ref, f32[64,16,128]{2,1,0:T(8,128)S(1)} %get-tuple-element.21.grad_ref, f32[112,128]{1,0:T(8,128)S(1)} %sum_cores.1.own_ref.refs_0_, f32[112,128]{1,0:T(8,128)S(1)} %collective-permute-done.6.one_ref.refs_1_, ...), custom_call_target="tpu_custom_call" | custom-call | flops 300000000 | bytes 5000000 | tf_op jit(solution)/shard_map/pair_gradient/pallas_call | solution.py:481
  69.8 0.6 collective-permute-done.12
  70.4 0.6 add_bitcast_fusion
  (34 shorter events, 0.1 us)
Async XLA Ops:
  0.6 12.9 %copy-start = (bf16[64,128,128]{2,1,0:T(8,128)(2,1)S(1)}, bf16[64,128,128]{2,1,0:T(8,128)(2,1)}, u32[]{:S(2)}) copy-start(bf16[64,128,128]{2,1,0:T(8,128)(2,1)} %pair_ref.3) | copy-start | bytes 6291460
  0.6 12.9 %copy-start.2 = (bf16[64,1536]{1,0:T(8,128)(2,1)S(1)}, bf16[64,1536]{1,0:T(8,128)(2,1)}, u32[]{:S(2)}) copy-start(bf16[64,1536]{1,0:T(8,128)(2,1)} %cot_ref.1) | copy-start | bytes 589828
  0.7 12.9 %copy-start.10 = (bf16[128,12]{0,1:T(8,128)(2,1)S(1)}, bf16[128,12]{0,1:T(8,128)(2,1)}, u32[]{:S(2)}) copy-start(bf16[128,12]{0,1:T(8,128)(2,1)} %param.21) | copy-start | bytes 9220
  0.7 34.7 %copy-start.5 = (bf16[64,288]{1,0:T(8,128)(2,1)S(1)}, bf16[64,288]{1,0:T(8,128)(2,1)}, u32[]{:S(2)}) copy-start(bf16[64,288]{1,0:T(8,128)(2,1)} %refs_3_.3) | copy-start | bytes 110596
  0.7 34.7 %copy-start.6 = (s32[1024]{0:T(1024)S(1)}, s32[1024]{0:T(1024)}, u32[]{:S(2)}) copy-start(s32[1024]{0:T(1024)} %mask_smem.1) | copy-start | bytes 12292
  0.7 34.7 %copy-start.7 = (bf16[64,192]{1,0:T(8,128)(2,1)S(1)}, bf16[64,192]{1,0:T(8,128)(2,1)}, u32[]{:S(2)}) copy-start(bf16[64,192]{1,0:T(8,128)(2,1)} %refs_0_.3) | copy-start | bytes 73732
  0.7 34.7 %copy-start.8 = (bf16[64,144]{1,0:T(8,128)(2,1)S(1)}, bf16[64,144]{1,0:T(8,128)(2,1)}, u32[]{:S(2)}) copy-start(bf16[64,144]{1,0:T(8,128)(2,1)} %refs_1_.3) | copy-start | bytes 55300
  0.7 34.7 %copy-start.9 = (bf16[64,192]{1,0:T(8,128)(2,1)S(1)}, bf16[64,192]{1,0:T(8,128)(2,1)}, u32[]{:S(2)}) copy-start(bf16[64,192]{1,0:T(8,128)(2,1)} %refs_2_.3) | copy-start | bytes 73732
  0.7 34.7 %copy-start.11 = (f32[12]{0:T(128)S(1)}, f32[12]{0:T(128)}, u32[]{:S(2)}) copy-start(f32[12]{0:T(128)} %point_smem.1) | copy-start | bytes 148
  5.9 14.7 %collective-permute-start = (s16[40,64,128]{2,1,0:T(8,128)(2,1)}, s16[40,64,128]{2,1,0:T(8,128)(2,1)S(1)}, u32[]{:S(2)}, u32[]{:S(2)}) collective-permute-start(s16[40,64,128]{2,1,0:T(8,128)(2,1)} %get-tuple-element.15), channel_id=1, source_target_pairs={{0,0},{8,10},{16,16},{24,9},{32,32},{40,8},{48,48},{56,11},{4,4},{... | collective-permute-start | bytes 1966088 | tf_op jit(solution)/shard_map/ppermute | solution.py:554
  9.7 16.7 %collective-permute-start.3 = (s16[33,64,128]{2,1,0:T(8,128)(2,1)}, s16[33,64,128]{2,1,0:T(8,128)(2,1)S(1)}, u32[]{:S(2)}, u32[]{:S(2)}) collective-permute-start(s16[33,64,128]{2,1,0:T(8,128)(2,1)} %get-tuple-element.23), channel_id=1, source_target_pairs={{0,0},{8,10},{16,16},{24,9},{32,32},{40,8},{48,48},{56,11},{4,4},{... | collective-permute-start | bytes 1622024 | tf_op jit(solution)/shard_map/ppermute | solution.py:555
  13.6 24.6 %copy-start.1 = (f32[64,64,128]{2,1,0:T(8,128)S(1)}, f32[64,64,128]{2,1,0:T(8,128)}, u32[]{:S(2)}) copy-start(f32[64,64,128]{2,1,0:T(8,128)} %get-tuple-element.22.own_ref) | copy-start | bytes 6291460
  13.6 24.6 %copy-start.3 = (s32[64,128]{1,0:T(8,128)S(1)}, s32[64,128]{1,0:T(8,128)}, u32[]{:S(2)}) copy-start(s32[64,128]{1,0:T(8,128)} %labels_ref.1) | copy-start | bytes 98308
  13.6 24.6 %copy-start.12 = (f32[64]{0:T(128)S(1)}, f32[64]{0:T(128)}, u32[]{:S(2)}) copy-start(f32[64]{0:T(128)} %param.20) | copy-start | bytes 772
  20.6 13.4 %collective-permute-start.1 = (s16[40,64,128]{2,1,0:T(8,128)(2,1)S(1)}, s16[40,64,128]{2,1,0:T(8,128)(2,1)S(1)}, u32[]{:S(2)}, u32[]{:S(2)}) collective-permute-start(s16[40,64,128]{2,1,0:T(8,128)(2,1)S(1)} %collective-permute-done), channel_id=1, source_target_pairs={{0,0},{10,8},{16,1},{9,9},{32,2},{8,10},{48,3},{11,11},{4,64},{74,... | collective-permute-start | bytes 1966088 | tf_op jit(solution)/shard_map/ppermute | solution.py:558
  26.4 11.8 %collective-permute-start.4 = (s16[33,64,128]{2,1,0:T(8,128)(2,1)S(1)}, s16[33,64,128]{2,1,0:T(8,128)(2,1)S(1)}, u32[]{:S(2)}, u32[]{:S(2)}) collective-permute-start(s16[33,64,128]{2,1,0:T(8,128)(2,1)S(1)} %collective-permute-done.3), channel_id=1, source_target_pairs={{0,8},{10,0},{16,9},{9,1},{32,10},{8,2},{48,11},{11,3},{4,72},{74,... | collective-permute-start | bytes 1622024 | tf_op jit(solution)/shard_map/ppermute | solution.py:559
  34.0 1.4 %collective-permute-start.2 = (s16[7,64,128]{2,1,0:T(8,128)(2,1)S(1)}, s16[7,64,128]{2,1,0:T(8,128)(2,1)S(1)}, u32[]{:S(2)}, u32[]{:S(2)}) collective-permute-start(s16[7,64,128]{2,1,0:T(8,128)(2,1)S(1)} %slice.4), channel_id=1, source_target_pairs={{0,8},{8,0},{16,24},{24,16},{32,40},{40,32},{48,56},{56,48},{4,12}... | collective-permute-start | bytes 344072 | tf_op jit(solution)/shard_map/ppermute | solution.py:560
  38.2 29.3 %copy-start.4 = (bf16[128,64]{0,1:T(8,128)(2,1)S(1)}, bf16[128,64]{0,1:T(8,128)(2,1)}, u32[]{:S(2)}) copy-start(bf16[128,64]{0,1:T(8,128)(2,1)} %param.19) | copy-start | bytes 49156
  42.3 2.3 %collective-permute-start.5 = (f32[88,128]{1,0:T(8,128)S(1)}, f32[88,128]{1,0:T(8,128)S(1)}, u32[]{:S(2)}, u32[]{:S(2)}) collective-permute-start(f32[88,128]{1,0:T(8,128)S(1)} %get-tuple-element.25.own_ref), channel_id=1, source_target_pairs={{0,8},{8,0},{16,24},{24,16},{32,40},{40,32},{48,56},{56,48},{4,12}... | collective-permute-start | bytes 135176 | tf_op jit(solution)/shard_map/ppermute | solution.py:573
  44.6 6.0 %collective-permute-start.8 = (f32[112,128]{1,0:T(8,128)S(1)}, f32[112,128]{1,0:T(8,128)S(1)}, u32[]{:S(2)}, u32[]{:S(2)}) collective-permute-start(f32[112,128]{1,0:T(8,128)S(1)} %sum_cores.1.own_ref.refs_0_), channel_id=1, source_target_pairs={{0,76},{8,68},{16,92},{24,84},{32,108},{40,100},{48,124},{56,116},... | collective-permute-start | bytes 172040 | tf_op jit(solution)/shard_map/ppermute | solution.py:526
  47.7 5.5 %collective-permute-start.7 = (f32[112,128]{1,0:T(8,128)S(1)}, f32[112,128]{1,0:T(8,128)S(1)}, u32[]{:S(2)}, u32[]{:S(2)}) collective-permute-start(f32[112,128]{1,0:T(8,128)S(1)} %sum_cores.1.own_ref.refs_0_), channel_id=1, source_target_pairs={{0,72},{8,64},{16,88},{24,80},{32,104},{40,96},{48,120},{56,112},{... | collective-permute-start | bytes 172040 | tf_op jit(solution)/shard_map/ppermute | solution.py:526
  48.9 4.3 %collective-permute-start.6 = (f32[112,128]{1,0:T(8,128)S(1)}, f32[112,128]{1,0:T(8,128)S(1)}, u32[]{:S(2)}, u32[]{:S(2)}) collective-permute-start(f32[112,128]{1,0:T(8,128)S(1)} %sum_cores.1.own_ref.refs_0_), channel_id=1, source_target_pairs={{0,12},{8,4},{16,28},{24,20},{32,44},{40,36},{48,60},{56,52},{4,8}... | collective-permute-start | bytes 172040 | tf_op jit(solution)/shard_map/ppermute | solution.py:526
  53.2 6.3 %collective-permute-start.11 = (f32[112,128]{1,0:T(8,128)S(1)}, f32[112,128]{1,0:T(8,128)S(1)}, u32[]{:S(2)}, u32[]{:S(2)}) collective-permute-start(f32[112,128]{1,0:T(8,128)S(1)} %sum_y.1.own_ref), channel_id=1, source_target_pairs={{0,11},{8,3},{16,27},{24,19},{32,43},{40,35},{48,59},{56,51},{4,15... | collective-permute-start | bytes 172040 | tf_op jit(solution)/shard_map/ppermute | solution.py:526
  57.3 5.2 %collective-permute-start.10 = (f32[112,128]{1,0:T(8,128)S(1)}, f32[112,128]{1,0:T(8,128)S(1)}, u32[]{:S(2)}, u32[]{:S(2)}) collective-permute-start(f32[112,128]{1,0:T(8,128)S(1)} %sum_y.1.own_ref), channel_id=1, source_target_pairs={{0,10},{8,2},{16,26},{24,18},{32,42},{40,34},{48,58},{56,50},{4,14... | collective-permute-start | bytes 172040 | tf_op jit(solution)/shard_map/ppermute | solution.py:526
  57.3 5.6 %collective-permute-start.9 = (f32[112,128]{1,0:T(8,128)S(1)}, f32[112,128]{1,0:T(8,128)S(1)}, u32[]{:S(2)}, u32[]{:S(2)}) collective-permute-start(f32[112,128]{1,0:T(8,128)S(1)} %sum_y.1.own_ref), channel_id=1, source_target_pairs={{0,9},{8,1},{16,25},{24,17},{32,41},{40,33},{48,57},{56,49},{4,13}... | collective-permute-start | bytes 172040 | tf_op jit(solution)/shard_map/ppermute | solution.py:526
  62.9 6.9 %collective-permute-start.14 = (f32[64,128]{1,0:T(8,128)S(1)}, f32[64,128]{1,0:T(8,128)S(1)}, u32[]{:S(2)}, u32[]{:S(2)}) collective-permute-start(f32[64,128]{1,0:T(8,128)S(1)} %sum_x.1), channel_id=1, source_target_pairs={{0,56},{8,48},{16,40},{24,32},{32,24},{40,16},{48,8},{56,0},{4,60}... | collective-permute-start | bytes 98312 | tf_op jit(solution)/shard_map/ppermute | solution.py:526
  65.3 4.5 %collective-permute-start.13 = (f32[64,128]{1,0:T(8,128)S(1)}, f32[64,128]{1,0:T(8,128)S(1)}, u32[]{:S(2)}, u32[]{:S(2)}) collective-permute-start(f32[64,128]{1,0:T(8,128)S(1)} %sum_x.1), channel_id=1, source_target_pairs={{0,24},{8,16},{16,8},{24,0},{32,56},{40,48},{48,40},{56,32},{4,28}... | collective-permute-start | bytes 98312 | tf_op jit(solution)/shard_map/ppermute | solution.py:526
  65.3 5.1 %collective-permute-start.12 = (f32[64,128]{1,0:T(8,128)S(1)}, f32[64,128]{1,0:T(8,128)S(1)}, u32[]{:S(2)}, u32[]{:S(2)}) collective-permute-start(f32[64,128]{1,0:T(8,128)S(1)} %sum_x.1), channel_id=1, source_target_pairs={{0,40},{8,32},{16,56},{24,48},{32,8},{40,0},{48,24},{56,16},{4,44}... | collective-permute-start | bytes 98312 | tf_op jit(solution)/shard_map/ppermute | solution.py:526

commit v7 on v6

--- a/solution.py
+++ b/solution.py
@@ -14,6 +14,7 @@
 HEADS = 12
 PAD_HEADS = 16
 CHUNK = 8
+BIN_CHUNK = 16
 QUANT = 32760.0
 BINS = 64
 STATS = 24
@@ -374,10 +375,9 @@
     low_lanes = lax.broadcasted_iota(jnp.int32, (64, 128), 1) < 64
 
     def halves(slab):
-        near = near_ref[slab].astype(jnp.int32).astype(jnp.float32)
-        far = far_ref[slab].astype(jnp.int32).astype(jnp.float32)
-        first = jnp.where(core == 0, near, far)
-        second = jnp.where(core == 0, far, near)
+        near, far = near_ref[slab], far_ref[slab]
+        first = lax.select(core == 0, near, far).astype(jnp.int32).astype(jnp.float32)
+        second = lax.select(core == 0, far, near).astype(jnp.int32).astype(jnp.float32)
         upper = jnp.where(low_lanes, first, pltpu.roll(second, 64, 1))
         lower = jnp.where(low_lanes, pltpu.roll(first, 64, 1), second)
         return upper, lower
@@ -400,10 +400,10 @@
     first_row = lax.axis_index("row") * 64
 
     total = jnp.zeros((64, 128), jnp.float32)
-    for step in range(pair_ref.shape[0] // CHUNK):
+    for step in range(pair_ref.shape[0] // BIN_CHUNK):
         grads = []
-        for t in range(CHUNK):
-            row = step * CHUNK + t
+        for t in range(BIN_CHUNK):
+            row = step * BIN_CHUNK + t
             logits = own_ref[row] + mirror[pl.ds(row, 64, stride=64), :] + bias
             weights = jnp.exp(logits - jnp.max(logits, axis=0, keepdims=True))
             valid = column_mask * mask_smem[first_row + row].astype(jnp.float32)
@@ -414,7 +414,7 @@
             grad = (weights * share - hits).astype(jnp.bfloat16)
             bins_ref[row] = grad
             grads.append(grad)
-        flat = pair_ref[step * CHUNK : (step + 1) * CHUNK].reshape(CHUNK * 128, 128)
+        flat = pair_ref[step * BIN_CHUNK : (step + 1) * BIN_CHUNK].reshape(BIN_CHUNK * 128, 128)
         total += dot(jnp.concatenate(grads, axis=1), flat)
     weight_ref[:BINS] = total
     weight_ref[BINS:] = stats_ref[...]

time: 72 us -> 71.9 us (level)
  no operation moved by 1% of the time
where the time goes in v7:
time: 71.9 us; the launch traced here: 70.8 us
  starting transfers between devices  29.9 us (42%)
  waiting for transfers between devices  22.6 us (31%)
  Pallas kernels  16.7 us (23%)
  between operations  0.9 us (1%)
    ppermute x9, starting transfers between devices, trade(): lax.ppermute(array, AXES, trade_map(axis, d))  15.2 us
    ppermute x9, waiting for transfers between devices, trade(): lax.ppermute(array, AXES, trade_map(axis, d))  7.98 us
    ppermute x1, waiting for transfers between devices, body(): same = lax.ppermute(same, AXES, SECOND_HOP[0])  5.42 us
    pallas_call x1, Pallas kernels, own_logits(): pl.pallas_call(logits_kernel, in_specs=[HBM] * (3 + len(keys)), out_specs...  5.13 us
    ppermute x1, waiting for transfers between devices, body(): same = lax.ppermute(same, AXES, FIRST_HOP)  4.61 us
    pallas_call x1, Pallas kernels, bin_gradient(): pl.pallas_call(bins_kernel, in_specs=[SMEM] + [VMEM] * 8, out_specs=[VMEM...  4.09 us
    ppermute x1, starting transfers between devices, body(): other = lax.ppermute(other, AXES, FIRST_HOP)  3.83 us
    ppermute x1, starting transfers between devices, body(): same = lax.ppermute(same, AXES, FIRST_HOP)  3.82 us
  transfers between devices with their start and end apart: 15, of which 10 were waited for; matrix products, arithmetic and copies ran while one was open for 0% of the time, Pallas kernels for 10%

profile of v7, /device:TPU:2, one launch (start us, length us, event | category | flops | bytes accessed | tf_op | source)
XLA Modules:
  0.0 70.8 jit_solution(239927239090208285)
XLA Ops:
  0.7 5.1 %own_logits.1 = (f32[64,64,128]{2,1,0:T(8,128)}, s16[40,64,128]{2,1,0:T(8,128)(2,1)}, s16[33,64,128]{2,1,0:T(8,128)(2,1)}) custom-call(bf16[64,128,128]{2,1,0:T(8,128)(2,1)} %pair_ref.3, bf16[64,128]{1,0:T(8,128)(2,1)} %bitcast.6, s32[64,128]{1,0:T(8,128)} %labels_ref.1, bf16[64,192]{1,0:T(8,128)(2,1)} %refs_0_.2, bf16[64,144]{1,0:T(8,128)(2,1)} %refs_1_.2, ...), custom_call_target="tpu_custom_call" | custom-call | flops 200000000 | bytes 6000000 | tf_op jit(solution)/shard_map/own_logits/pallas_call | solution.py:221
  5.9 3.8 %collective-permute-start = (s16[40,64,128]{2,1,0:T(8,128)(2,1)}, s16[40,64,128]{2,1,0:T(8,128)(2,1)S(1)}, u32[]{:S(2)}, u32[]{:S(2)}) collective-permute-start(s16[40,64,128]{2,1,0:T(8,128)(2,1)} %get-tuple-element.15), channel_id=1, source_target_pairs={{0,0},{8,10},{16,16},{24,9},{32,32},{40,8},{48,48},{56,11},{4,4},{... | collective-permute-start | bytes 1966088 | tf_op jit(solution)/shard_map/ppermute | solution.py:554
  9.7 3.8 %collective-permute-start.3 = (s16[33,64,128]{2,1,0:T(8,128)(2,1)}, s16[33,64,128]{2,1,0:T(8,128)(2,1)S(1)}, u32[]{:S(2)}, u32[]{:S(2)}) collective-permute-start(s16[33,64,128]{2,1,0:T(8,128)(2,1)} %get-tuple-element.23), channel_id=1, source_target_pairs={{0,0},{8,10},{16,16},{24,9},{32,32},{40,8},{48,48},{56,11},{4,4},{... | collective-permute-start | bytes 1622024 | tf_op jit(solution)/shard_map/ppermute | solution.py:555
  13.6 0.0 copy-start.3
  13.6 0.0 copy-start.12
  13.6 2.4 %pair_parts.1 = (f32[64,16,128]{2,1,0:T(8,128)S(1)}, f32[64,16,128]{2,1,0:T(8,128)S(1)}, bf16[64,16,128]{2,1,0:T(8,128)(2,1)S(1)}) custom-call(bf16[64,128,128]{2,1,0:T(8,128)(2,1)S(1)} %copy-done, bf16[64,1536]{1,0:T(8,128)(2,1)S(1)} %copy-done.2, bf16[12,128]{1,0:T(8,128)(2,1)S(1)} %bitcast.10), custom_call_target="tpu_custom_call" | custom-call | flops 300000000 | bytes 4000000 | tf_op jit(solution)/shard_map/pair_parts/pallas_call | solution.py:266
  16.0 4.6 %collective-permute-done = s16[40,64,128]{2,1,0:T(8,128)(2,1)S(1)} collective-permute-done((s16[40,64,128]{2,1,0:T(8,128)(2,1)}, s16[40,64,128]{2,1,0:T(8,128)(2,1)S(1)}, u32[]{:S(2)}, u32[]{:S(2)}) %collective-permute-start) | collective-permute-done | bytes 655392 | tf_op jit(solution)/shard_map/ppermute | solution.py:554
  20.6 3.4 %collective-permute-start.1 = (s16[40,64,128]{2,1,0:T(8,128)(2,1)S(1)}, s16[40,64,128]{2,1,0:T(8,128)(2,1)S(1)}, u32[]{:S(2)}, u32[]{:S(2)}) collective-permute-start(s16[40,64,128]{2,1,0:T(8,128)(2,1)S(1)} %collective-permute-done), channel_id=1, source_target_pairs={{0,0},{10,8},{16,1},{9,9},{32,2},{8,10},{48,3},{11,11},{4,64},{74,... | collective-permute-start | bytes 1966088 | tf_op jit(solution)/shard_map/ppermute | solution.py:558
  23.9 2.4 %collective-permute-done.3 = s16[33,64,128]{2,1,0:T(8,128)(2,1)S(1)} collective-permute-done((s16[33,64,128]{2,1,0:T(8,128)(2,1)}, s16[33,64,128]{2,1,0:T(8,128)(2,1)S(1)}, u32[]{:S(2)}, u32[]{:S(2)}) %collective-permute-start.3) | collective-permute-done | bytes 540704 | tf_op jit(solution)/shard_map/ppermute | solution.py:555
  26.4 2.2 %collective-permute-start.4 = (s16[33,64,128]{2,1,0:T(8,128)(2,1)S(1)}, s16[33,64,128]{2,1,0:T(8,128)(2,1)S(1)}, u32[]{:S(2)}, u32[]{:S(2)}) collective-permute-start(s16[33,64,128]{2,1,0:T(8,128)(2,1)S(1)} %collective-permute-done.3), channel_id=1, source_target_pairs={{0,8},{10,0},{16,9},{9,1},{32,10},{8,2},{48,11},{11,3},{4,72},{74,... | collective-permute-start | bytes 1622024 | tf_op jit(solution)/shard_map/ppermute | solution.py:559
  28.5 5.4 %collective-permute-done.1.near_ref = s16[40,64,128]{2,1,0:T(8,128)(2,1)S(1)} collective-permute-done((s16[40,64,128]{2,1,0:T(8,128)(2,1)S(1)}, s16[40,64,128]{2,1,0:T(8,128)(2,1)S(1)}, u32[]{:S(2)}, u32[]{:S(2)}) %collective-permute-start.1) | collective-permute-done | bytes 655392 | tf_op jit(solution)/shard_map/ppermute | solution.py:558
  34.0 0.1 collective-permute-start.2
  34.0 1.3 %collective-permute-done.2.far_ref = s16[7,64,128]{2,1,0:T(8,128)(2,1)S(1)} collective-permute-done((s16[7,64,128]{2,1,0:T(8,128)(2,1)S(1)}, s16[7,64,128]{2,1,0:T(8,128)(2,1)S(1)}, u32[]{:S(2)}, u32[]{:S(2)}) %collective-permute-start.2) | collective-permute-done | bytes 114720 | tf_op jit(solution)/shard_map/ppermute | solution.py:560
  35.4 2.8 %attention_parts.1 = (f32[64,16,128]{2,1,0:T(8,128)S(1)}, f32[64,16,128]{2,1,0:T(8,128)S(1)}, f32[24,128]{1,0:T(8,128)S(1)}) custom-call(f32[12]{0:T(128)S(1)} %copy-done.11, s16[40,64,128]{2,1,0:T(8,128)(2,1)S(1)} %collective-permute-done.1.near_ref, s16[7,64,128]{2,1,0:T(8,128)(2,1)S(1)} %collective-permute-done.2.far_ref, ...), custom_call_target="tpu_custom_call" | custom-call | flops 500000000 | bytes 2000000 | tf_op jit(solution)/shard_map/attention_parts/pallas_call | solution.py:358
  38.2 0.0 copy-done.3
  38.2 4.1 %bin_gradient.1 = (bf16[64,64,128]{2,1,0:T(8,128)(2,1)S(1)}, f32[88,128]{1,0:T(8,128)S(1)}) custom-call(s32[1024]{0:T(1024)S(1)} %copy-done.6, bf16[64,128,128]{2,1,0:T(8,128)(2,1)S(1)} %copy-done, f32[64,64,128]{2,1,0:T(8,128)S(1)} %copy-done.1, s32[64,128]{1,0:T(8,128)S(1)} %copy-done.3, s16[40,64,128]{2,1,0:T(8,128)(2,1)S(1)} %collective-permute-done.1.near_ref, ...), custom_call_target="tpu_custom_call" | custom-call | flops 200000000 | bytes 6000000 | tf_op jit(solution)/shard_map/bin_gradient/pallas_call | solution.py:425
  42.3 1.4 %collective-permute-start.5 = (f32[88,128]{1,0:T(8,128)S(1)}, f32[88,128]{1,0:T(8,128)S(1)}, u32[]{:S(2)}, u32[]{:S(2)}) collective-permute-start(f32[88,128]{1,0:T(8,128)S(1)} %get-tuple-element.25.own_ref), channel_id=1, source_target_pairs={{0,8},{8,0},{16,24},{24,16},{32,40},{40,32},{48,56},{56,48},{4,12}... | collective-permute-start | bytes 135176 | tf_op jit(solution)/shard_map/ppermute | solution.py:573
  43.8 0.9 %collective-permute-done.5.swapped_ref = f32[88,128]{1,0:T(8,128)S(1)} collective-permute-done((f32[88,128]{1,0:T(8,128)S(1)}, f32[88,128]{1,0:T(8,128)S(1)}, u32[]{:S(2)}, u32[]{:S(2)}) %collective-permute-start.5) | collective-permute-done | bytes 45088 | tf_op jit(solution)/shard_map/ppermute | solution.py:573
  44.6 3.1 %collective-permute-start.8 = (f32[112,128]{1,0:T(8,128)S(1)}, f32[112,128]{1,0:T(8,128)S(1)}, u32[]{:S(2)}, u32[]{:S(2)}) collective-permute-start(f32[112,128]{1,0:T(8,128)S(1)} %sum_cores.1.own_ref.refs_0_), channel_id=1, source_target_pairs={{0,76},{8,68},{16,92},{24,84},{32,108},{40,100},{48,124},{56,116},... | collective-permute-start | bytes 172040 | tf_op jit(solution)/shard_map/ppermute | solution.py:526
  47.7 1.2 %collective-permute-start.7 = (f32[112,128]{1,0:T(8,128)S(1)}, f32[112,128]{1,0:T(8,128)S(1)}, u32[]{:S(2)}, u32[]{:S(2)}) collective-permute-start(f32[112,128]{1,0:T(8,128)S(1)} %sum_cores.1.own_ref.refs_0_), channel_id=1, source_target_pairs={{0,72},{8,64},{16,88},{24,80},{32,104},{40,96},{48,120},{56,112},{... | collective-permute-start | bytes 172040 | tf_op jit(solution)/shard_map/ppermute | solution.py:526
  48.9 1.8 %collective-permute-done.8.three_ref = f32[112,128]{1,0:T(8,128)S(1)} collective-permute-done((f32[112,128]{1,0:T(8,128)S(1)}, f32[112,128]{1,0:T(8,128)S(1)}, u32[]{:S(2)}, u32[]{:S(2)}) %collective-permute-start.8) | collective-permute-done | bytes 57376 | tf_op jit(solution)/shard_map/ppermute | solution.py:526
  50.6 2.5 %collective-permute-done.7.two_ref = f32[112,128]{1,0:T(8,128)S(1)} collective-permute-done((f32[112,128]{1,0:T(8,128)S(1)}, f32[112,128]{1,0:T(8,128)S(1)}, u32[]{:S(2)}, u32[]{:S(2)}) %collective-permute-start.7) | collective-permute-done | bytes 57376 | tf_op jit(solution)/shard_map/ppermute | solution.py:526
  53.2 4.1 %collective-permute-start.11 = (f32[112,128]{1,0:T(8,128)S(1)}, f32[112,128]{1,0:T(8,128)S(1)}, u32[]{:S(2)}, u32[]{:S(2)}) collective-permute-start(f32[112,128]{1,0:T(8,128)S(1)} %sum_y.1.own_ref), channel_id=1, source_target_pairs={{0,11},{8,3},{16,27},{24,19},{32,43},{40,35},{48,59},{56,51},{4,15... | collective-permute-start | bytes 172040 | tf_op jit(solution)/shard_map/ppermute | solution.py:526
  57.3 0.1 collective-permute-start.10
  57.4 2.3 %collective-permute-start.9 = (f32[112,128]{1,0:T(8,128)S(1)}, f32[112,128]{1,0:T(8,128)S(1)}, u32[]{:S(2)}, u32[]{:S(2)}) collective-permute-start(f32[112,128]{1,0:T(8,128)S(1)} %sum_y.1.own_ref), channel_id=1, source_target_pairs={{0,9},{8,1},{16,25},{24,17},{32,41},{40,33},{48,57},{56,49},{4,13}... | collective-permute-start | bytes 172040 | tf_op jit(solution)/shard_map/ppermute | solution.py:526
  59.7 2.8 %collective-permute-done.10.refs_3_.two_ref = f32[112,128]{1,0:T(8,128)S(1)} collective-permute-done((f32[112,128]{1,0:T(8,128)S(1)}, f32[112,128]{1,0:T(8,128)S(1)}, u32[]{:S(2)}, u32[]{:S(2)}) %collective-permute-start.10) | collective-permute-done | bytes 57376 | tf_op jit(solution)/shard_map/ppermute | solution.py:526
  62.5 0.6 collective-permute-done.9.refs_2_.one_ref
  63.1 2.2 %collective-permute-start.14 = (f32[64,128]{1,0:T(8,128)S(1)}, f32[64,128]{1,0:T(8,128)S(1)}, u32[]{:S(2)}, u32[]{:S(2)}) collective-permute-start(f32[64,128]{1,0:T(8,128)S(1)} %sum_x.1), channel_id=1, source_target_pairs={{0,56},{8,48},{16,40},{24,32},{32,24},{40,16},{48,8},{56,0},{4,60}... | collective-permute-start | bytes 98312 | tf_op jit(solution)/shard_map/ppermute | solution.py:526
  65.3 2.2 %collective-permute-start.12 = (f32[64,128]{1,0:T(8,128)S(1)}, f32[64,128]{1,0:T(8,128)S(1)}, u32[]{:S(2)}, u32[]{:S(2)}) collective-permute-start(f32[64,128]{1,0:T(8,128)S(1)} %sum_x.1), channel_id=1, source_target_pairs={{0,40},{8,32},{16,56},{24,48},{32,8},{40,0},{48,24},{56,16},{4,44}... | collective-permute-start | bytes 98312 | tf_op jit(solution)/shard_map/ppermute | solution.py:526
  67.5 2.2 %pair_gradient.1 = bf16[64,128,128]{2,1,0:T(8,128)(2,1)} custom-call(f32[64,16,128]{2,1,0:T(8,128)S(1)} %get-tuple-element.20.exp_ref, f32[64,16,128]{2,1,0:T(8,128)S(1)} %get-tuple-element.21.grad_ref, f32[112,128]{1,0:T(8,128)S(1)} %sum_cores.1.own_ref.refs_0_, f32[112,128]{1,0:T(8,128)S(1)} %collective-permute-done.6.one_ref.refs_1_, ...), custom_call_target="tpu_custom_call" | custom-call | flops 300000000 | bytes 5000000 | tf_op jit(solution)/shard_map/pair_gradient/pallas_call | solution.py:481
  69.8 0.3 collective-permute-done.12
  70.1 0.6 add_bitcast_fusion
  (34 shorter events, 0.1 us)
Async XLA Ops:
  0.6 12.9 %copy-start = (bf16[64,128,128]{2,1,0:T(8,128)(2,1)S(1)}, bf16[64,128,128]{2,1,0:T(8,128)(2,1)}, u32[]{:S(2)}) copy-start(bf16[64,128,128]{2,1,0:T(8,128)(2,1)} %pair_ref.3) | copy-start | bytes 6291460
  0.6 12.9 %copy-start.2 = (bf16[64,1536]{1,0:T(8,128)(2,1)S(1)}, bf16[64,1536]{1,0:T(8,128)(2,1)}, u32[]{:S(2)}) copy-start(bf16[64,1536]{1,0:T(8,128)(2,1)} %cot_ref.1) | copy-start | bytes 589828
  0.7 12.9 %copy-start.10 = (bf16[128,12]{0,1:T(8,128)(2,1)S(1)}, bf16[128,12]{0,1:T(8,128)(2,1)}, u32[]{:S(2)}) copy-start(bf16[128,12]{0,1:T(8,128)(2,1)} %param.21) | copy-start | bytes 9220
  0.7 34.7 %copy-start.5 = (bf16[64,288]{1,0:T(8,128)(2,1)S(1)}, bf16[64,288]{1,0:T(8,128)(2,1)}, u32[]{:S(2)}) copy-start(bf16[64,288]{1,0:T(8,128)(2,1)} %refs_3_.3) | copy-start | bytes 110596
  0.7 34.7 %copy-start.6 = (s32[1024]{0:T(1024)S(1)}, s32[1024]{0:T(1024)}, u32[]{:S(2)}) copy-start(s32[1024]{0:T(1024)} %mask_smem.1) | copy-start | bytes 12292
  0.7 34.7 %copy-start.7 = (bf16[64,192]{1,0:T(8,128)(2,1)S(1)}, bf16[64,192]{1,0:T(8,128)(2,1)}, u32[]{:S(2)}) copy-start(bf16[64,192]{1,0:T(8,128)(2,1)} %refs_0_.3) | copy-start | bytes 73732
  0.7 34.7 %copy-start.8 = (bf16[64,144]{1,0:T(8,128)(2,1)S(1)}, bf16[64,144]{1,0:T(8,128)(2,1)}, u32[]{:S(2)}) copy-start(bf16[64,144]{1,0:T(8,128)(2,1)} %refs_1_.3) | copy-start | bytes 55300
  0.7 34.7 %copy-start.9 = (bf16[64,192]{1,0:T(8,128)(2,1)S(1)}, bf16[64,192]{1,0:T(8,128)(2,1)}, u32[]{:S(2)}) copy-start(bf16[64,192]{1,0:T(8,128)(2,1)} %refs_2_.3) | copy-start | bytes 73732
  0.7 34.7 %copy-start.11 = (f32[12]{0:T(128)S(1)}, f32[12]{0:T(128)}, u32[]{:S(2)}) copy-start(f32[12]{0:T(128)} %point_smem.1) | copy-start | bytes 148
  5.9 14.7 %collective-permute-start = (s16[40,64,128]{2,1,0:T(8,128)(2,1)}, s16[40,64,128]{2,1,0:T(8,128)(2,1)S(1)}, u32[]{:S(2)}, u32[]{:S(2)}) collective-permute-start(s16[40,64,128]{2,1,0:T(8,128)(2,1)} %get-tuple-element.15), channel_id=1, source_target_pairs={{0,0},{8,10},{16,16},{24,9},{32,32},{40,8},{48,48},{56,11},{4,4},{... | collective-permute-start | bytes 1966088 | tf_op jit(solution)/shard_map/ppermute | solution.py:554
  9.7 16.7 %collective-permute-start.3 = (s16[33,64,128]{2,1,0:T(8,128)(2,1)}, s16[33,64,128]{2,1,0:T(8,128)(2,1)S(1)}, u32[]{:S(2)}, u32[]{:S(2)}) collective-permute-start(s16[33,64,128]{2,1,0:T(8,128)(2,1)} %get-tuple-element.23), channel_id=1, source_target_pairs={{0,0},{8,10},{16,16},{24,9},{32,32},{40,8},{48,48},{56,11},{4,4},{... | collective-permute-start | bytes 1622024 | tf_op jit(solution)/shard_map/ppermute | solution.py:555
  13.6 24.6 %copy-start.1 = (f32[64,64,128]{2,1,0:T(8,128)S(1)}, f32[64,64,128]{2,1,0:T(8,128)}, u32[]{:S(2)}) copy-start(f32[64,64,128]{2,1,0:T(8,128)} %get-tuple-element.22.own_ref) | copy-start | bytes 6291460
  13.6 24.6 %copy-start.3 = (s32[64,128]{1,0:T(8,128)S(1)}, s32[64,128]{1,0:T(8,128)}, u32[]{:S(2)}) copy-start(s32[64,128]{1,0:T(8,128)} %labels_ref.1) | copy-start | bytes 98308
  13.6 24.6 %copy-start.12 = (f32[64]{0:T(128)S(1)}, f32[64]{0:T(128)}, u32[]{:S(2)}) copy-start(f32[64]{0:T(128)} %param.20) | copy-start | bytes 772
  20.6 13.4 %collective-permute-start.1 = (s16[40,64,128]{2,1,0:T(8,128)(2,1)S(1)}, s16[40,64,128]{2,1,0:T(8,128)(2,1)S(1)}, u32[]{:S(2)}, u32[]{:S(2)}) collective-permute-start(s16[40,64,128]{2,1,0:T(8,128)(2,1)S(1)} %collective-permute-done), channel_id=1, source_target_pairs={{0,0},{10,8},{16,1},{9,9},{32,2},{8,10},{48,3},{11,11},{4,64},{74,... | collective-permute-start | bytes 1966088 | tf_op jit(solution)/shard_map/ppermute | solution.py:558
  26.4 11.8 %collective-permute-start.4 = (s16[33,64,128]{2,1,0:T(8,128)(2,1)S(1)}, s16[33,64,128]{2,1,0:T(8,128)(2,1)S(1)}, u32[]{:S(2)}, u32[]{:S(2)}) collective-permute-start(s16[33,64,128]{2,1,0:T(8,128)(2,1)S(1)} %collective-permute-done.3), channel_id=1, source_target_pairs={{0,8},{10,0},{16,9},{9,1},{32,10},{8,2},{48,11},{11,3},{4,72},{74,... | collective-permute-start | bytes 1622024 | tf_op jit(solution)/shard_map/ppermute | solution.py:559
  34.0 1.4 %collective-permute-start.2 = (s16[7,64,128]{2,1,0:T(8,128)(2,1)S(1)}, s16[7,64,128]{2,1,0:T(8,128)(2,1)S(1)}, u32[]{:S(2)}, u32[]{:S(2)}) collective-permute-start(s16[7,64,128]{2,1,0:T(8,128)(2,1)S(1)} %slice.4), channel_id=1, source_target_pairs={{0,8},{8,0},{16,24},{24,16},{32,40},{40,32},{48,56},{56,48},{4,12}... | collective-permute-start | bytes 344072 | tf_op jit(solution)/shard_map/ppermute | solution.py:560
  38.2 29.3 %copy-start.4 = (bf16[128,64]{0,1:T(8,128)(2,1)S(1)}, bf16[128,64]{0,1:T(8,128)(2,1)}, u32[]{:S(2)}) copy-start(bf16[128,64]{0,1:T(8,128)(2,1)} %param.19) | copy-start | bytes 49156
  42.3 2.3 %collective-permute-start.5 = (f32[88,128]{1,0:T(8,128)S(1)}, f32[88,128]{1,0:T(8,128)S(1)}, u32[]{:S(2)}, u32[]{:S(2)}) collective-permute-start(f32[88,128]{1,0:T(8,128)S(1)} %get-tuple-element.25.own_ref), channel_id=1, source_target_pairs={{0,8},{8,0},{16,24},{24,16},{32,40},{40,32},{48,56},{56,48},{4,12}... | collective-permute-start | bytes 135176 | tf_op jit(solution)/shard_map/ppermute | solution.py:573
  44.6 6.0 %collective-permute-start.8 = (f32[112,128]{1,0:T(8,128)S(1)}, f32[112,128]{1,0:T(8,128)S(1)}, u32[]{:S(2)}, u32[]{:S(2)}) collective-permute-start(f32[112,128]{1,0:T(8,128)S(1)} %sum_cores.1.own_ref.refs_0_), channel_id=1, source_target_pairs={{0,76},{8,68},{16,92},{24,84},{32,108},{40,100},{48,124},{56,116},... | collective-permute-start | bytes 172040 | tf_op jit(solution)/shard_map/ppermute | solution.py:526
  47.7 5.5 %collective-permute-start.7 = (f32[112,128]{1,0:T(8,128)S(1)}, f32[112,128]{1,0:T(8,128)S(1)}, u32[]{:S(2)}, u32[]{:S(2)}) collective-permute-start(f32[112,128]{1,0:T(8,128)S(1)} %sum_cores.1.own_ref.refs_0_), channel_id=1, source_target_pairs={{0,72},{8,64},{16,88},{24,80},{32,104},{40,96},{48,120},{56,112},{... | collective-permute-start | bytes 172040 | tf_op jit(solution)/shard_map/ppermute | solution.py:526
  48.9 4.3 %collective-permute-start.6 = (f32[112,128]{1,0:T(8,128)S(1)}, f32[112,128]{1,0:T(8,128)S(1)}, u32[]{:S(2)}, u32[]{:S(2)}) collective-permute-start(f32[112,128]{1,0:T(8,128)S(1)} %sum_cores.1.own_ref.refs_0_), channel_id=1, source_target_pairs={{0,12},{8,4},{16,28},{24,20},{32,44},{40,36},{48,60},{56,52},{4,8}... | collective-permute-start | bytes 172040 | tf_op jit(solution)/shard_map/ppermute | solution.py:526
  53.2 6.5 %collective-permute-start.11 = (f32[112,128]{1,0:T(8,128)S(1)}, f32[112,128]{1,0:T(8,128)S(1)}, u32[]{:S(2)}, u32[]{:S(2)}) collective-permute-start(f32[112,128]{1,0:T(8,128)S(1)} %sum_y.1.own_ref), channel_id=1, source_target_pairs={{0,11},{8,3},{16,27},{24,19},{32,43},{40,35},{48,59},{56,51},{4,15... | collective-permute-start | bytes 172040 | tf_op jit(solution)/shard_map/ppermute | solution.py:526
  57.3 5.2 %collective-permute-start.10 = (f32[112,128]{1,0:T(8,128)S(1)}, f32[112,128]{1,0:T(8,128)S(1)}, u32[]{:S(2)}, u32[]{:S(2)}) collective-permute-start(f32[112,128]{1,0:T(8,128)S(1)} %sum_y.1.own_ref), channel_id=1, source_target_pairs={{0,10},{8,2},{16,26},{24,18},{32,42},{40,34},{48,58},{56,50},{4,14... | collective-permute-start | bytes 172040 | tf_op jit(solution)/shard_map/ppermute | solution.py:526
  57.4 5.6 %collective-permute-start.9 = (f32[112,128]{1,0:T(8,128)S(1)}, f32[112,128]{1,0:T(8,128)S(1)}, u32[]{:S(2)}, u32[]{:S(2)}) collective-permute-start(f32[112,128]{1,0:T(8,128)S(1)} %sum_y.1.own_ref), channel_id=1, source_target_pairs={{0,9},{8,1},{16,25},{24,17},{32,41},{40,33},{48,57},{56,49},{4,13}... | collective-permute-start | bytes 172040 | tf_op jit(solution)/shard_map/ppermute | solution.py:526
  63.1 6.7 %collective-permute-start.14 = (f32[64,128]{1,0:T(8,128)S(1)}, f32[64,128]{1,0:T(8,128)S(1)}, u32[]{:S(2)}, u32[]{:S(2)}) collective-permute-start(f32[64,128]{1,0:T(8,128)S(1)} %sum_x.1), channel_id=1, source_target_pairs={{0,56},{8,48},{16,40},{24,32},{32,24},{40,16},{48,8},{56,0},{4,60}... | collective-permute-start | bytes 98312 | tf_op jit(solution)/shard_map/ppermute | solution.py:526
  65.3 4.5 %collective-permute-start.13 = (f32[64,128]{1,0:T(8,128)S(1)}, f32[64,128]{1,0:T(8,128)S(1)}, u32[]{:S(2)}, u32[]{:S(2)}) collective-permute-start(f32[64,128]{1,0:T(8,128)S(1)} %sum_x.1), channel_id=1, source_target_pairs={{0,24},{8,16},{16,8},{24,0},{32,56},{40,48},{48,40},{56,32},{4,28}... | collective-permute-start | bytes 98312 | tf_op jit(solution)/shard_map/ppermute | solution.py:526
  65.3 4.9 %collective-permute-start.12 = (f32[64,128]{1,0:T(8,128)S(1)}, f32[64,128]{1,0:T(8,128)S(1)}, u32[]{:S(2)}, u32[]{:S(2)}) collective-permute-start(f32[64,128]{1,0:T(8,128)S(1)} %sum_x.1), channel_id=1, source_target_pairs={{0,40},{8,32},{16,56},{24,48},{32,8},{40,0},{48,24},{56,16},{4,44}... | collective-permute-start | bytes 98312 | tf_op jit(solution)/shard_map/ppermute | solution.py:526
